TPU v7x, 128 devices: a whole 4x4x4 slice. The times are simulated.
128 devices in a mesh: tile: 16 (over x, y), lev: 8 (over z, core).
Axes of the slice: x: 4, y: 4, z: 4, core: 2. Of those that a mesh axis runs over, the one named last changes fastest.
Arguments:
- anomalies: bfloat16 [64, 32768, 256], P('lev', 'tile'), may hold values from -12 to 12
- mean_state: float32 [64, 32768], P('lev', 'tile'), may hold values from -6 to 6
- obs_op: bfloat16 [65536, 4096], P(('tile', 'lev')), may hold values from -0.005859375 to 0.005859375
- innovations: float32 [4194304], P(('tile', 'lev')), may hold values from -24 to 24
- obs_rinv: float32 [4194304], P(('tile', 'lev')), may hold values from 0.25 to 4
- obs_cols: int32 [524288], P(('tile', 'lev')), may hold values from 0 to 2431, as said below
- send_cols: int32 [16, 384], P('tile'), may hold values from 0 to 2047
- obs_count: int32 [128], P(('tile', 'lev')), may hold values from 1 to 512, 32768 in all
Outputs:
- analysis: bfloat16 [64, 32768, 256], P('lev', 'tile')
Inputs may be any that keep to these rules, and one draw needn't show every extreme that they name: `obs_cols`: an entry below 2048 names the block's own tile's column of that number; an entry 2048 + p * 24 + s names the column in slot s of tile p's send list for this tile. `send_cols`: row p, entries t * 24 to t * 24 + 23 are the own columns tile p sends to tile t. `obs_count`: blocks of a device beyond its count are padding.
All inputs are finite; a program needn't handle non-finite values.
Results may differ from a plain program's by a relative error of at most 0.0083.
Values may be sent and summed in bfloat16 or wider, within the bound.
No kernel may reach another device: no remote copies, remote signals or barrier semaphores. Data moves between devices by JAX's collectives and lax.ppermute only.
A program may use at most 192 MiB of HBM per device.

v0:
```python
import jax
import jax.numpy as jnp
from jax import lax
from jax.sharding import PartitionSpec as P

HIGH = lax.Precision.HIGHEST


def square_root(spread, iterations):
    norm_scale = jnp.sqrt(jnp.sum(spread * spread))
    identity = jnp.eye(spread.shape[0], dtype=jnp.float32)

    def advance(turn_index, carried):
        approx, inverse = carried
        middle = 1.5 * identity - 0.5 * jnp.dot(inverse, approx, precision=HIGH)
        return (jnp.dot(approx, middle, precision=HIGH), jnp.dot(middle, inverse, precision=HIGH))

    approx, inverse = lax.fori_loop(0, iterations, advance, (spread / norm_scale, identity))
    return jnp.sqrt(norm_scale) * approx


def transform_weights(gram_sym, projection, numerator, obs_total, members):
    rho_value = numerator / obs_total
    identity = jnp.eye(members, dtype=jnp.float32)
    system = (members - 1.0) / rho_value * identity + gram_sym
    factor = jnp.linalg.cholesky(system)
    inverse = jax.scipy.linalg.cho_solve((factor, True), identity)
    mean_weights = jnp.dot(inverse, projection, precision=HIGH)
    spread = (members - 1.0) * inverse
    spread = 0.5 * (spread + spread.T)
    root = square_root(spread, 14)
    return (root + mean_weights[:, None]).astype(jnp.bfloat16)


def per_device(
    anomalies, mean_state, obs_op, innovations, obs_rinv, obs_cols, send_cols, obs_count
):
    lev_dev, col_dev, members = anomalies.shape
    block_total = obs_op.shape[0]
    per_block = innovations.shape[0] // block_total
    support = obs_cols.shape[0] // block_total
    group_size = min(block_total, 64)
    group_total = block_total // group_size
    outgoing = jnp.take(anomalies, send_cols[0], axis=1)
    incoming = lax.all_to_all(outgoing, "tile", split_axis=1, concat_axis=1, tiled=True)
    live_mask = jnp.arange(block_total)[:, None] < obs_count[0]
    rinv_blocks = obs_rinv.reshape(block_total, per_block)
    innov_blocks = innovations.reshape(block_total, per_block)
    obs_weight = jnp.where(live_mask, jnp.sqrt(rinv_blocks), 0.0)
    numerator = jnp.sum(jnp.where(live_mask, rinv_blocks * innov_blocks * innov_blocks, 0.0))
    obs_local = (obs_count[0] * per_block).astype(jnp.float32)
    numerator, obs_total = lax.psum((numerator, obs_local), ("tile", "lev"))
    operators = obs_op.reshape(group_total, group_size, per_block, support, lev_dev)
    weight_groups = obs_weight.reshape(group_total, group_size * per_block)
    innov_groups = (obs_weight * innov_blocks).reshape(group_total, group_size * per_block)
    column_groups = obs_cols.reshape(group_total, group_size * support)

    def project(group_index, picked):
        picked = picked.reshape(lev_dev, group_size, support, members)
        images = jnp.einsum(
            "boql,lbqk->bok", operators[group_index], picked, preferred_element_type=jnp.float32
        )
        return images.reshape(group_size * per_block, members)

    def add_terms(carried, group_index, images):
        gram_part, projection = carried
        scaled = (weight_groups[group_index][:, None] * images).astype(jnp.bfloat16)
        gram_part = gram_part + lax.dot_general(
            scaled, scaled, (((0,), (0,)), ((), ())), preferred_element_type=jnp.float32
        )
        projection = projection + jnp.dot(
            innov_groups[group_index], scaled, precision=HIGH, preferred_element_type=jnp.float32
        )
        return (gram_part, projection)

    zero_terms = (jnp.zeros((members, members), jnp.float32), jnp.zeros((members,), jnp.float32))
    extended = jnp.concatenate([anomalies, incoming], axis=1)

    def whole_terms(group_index, carried):
        picked = jnp.take(extended, column_groups[group_index], axis=1)
        return add_terms(carried, group_index, project(group_index, picked))

    gram_part, projection = lax.fori_loop(0, group_total, whole_terms, zero_terms)
    gram_whole, projection = lax.psum((gram_part, projection), ("tile", "lev"))
    gram_sym = 0.5 * (gram_whole + gram_whole.T)
    transform = transform_weights(gram_sym, projection, numerator, obs_total, members)
    updated = jnp.dot(
        anomalies.reshape(lev_dev * col_dev, members), transform, preferred_element_type=jnp.float32
    )
    analysis = mean_state[:, :, None] + updated.reshape(lev_dev, col_dev, members)
    return analysis.astype(jnp.bfloat16)


def solution(mesh):
    return jax.shard_map(
        per_device,
        mesh=mesh,
        in_specs=(
            P("lev", "tile", None),
            P("lev", "tile"),
            P(("tile", "lev"), None),
            P(("tile", "lev")),
            P(("tile", "lev")),
            P(("tile", "lev")),
            P("tile", None),
            P(("tile", "lev")),
        ),
        out_specs=P("lev", "tile", None),
        check_vma=False,
    )
```

profile of v0, /device:TPU:1, one launch (start us, length us, event | category | flops | bytes accessed | tf_op | source)
XLA Modules:
  0.0 440.1 jit_solution(10736331046295487436)
XLA Ops:
  6.5 0.7 fusion.37
  7.2 0.7 reduce.15
  8.0 10.4 %gather_fusion.1 = bf16[384,8,256]{2,0,1:T(8,128)(2,1)S(1)} fusion(bf16[8,2048,256]{2,1,0:T(8,128)(2,1)} %param.12, s32[1024]{0:T(1024)S(1)} %pad_clamp_fusion.1), kind=kCustom, calls=%fused_computation.1 | custom fusion | bytes 3147264 | tf_op jit(solution)/shard_map/jit(_take)/gather | solution.py:44
  18.6 2.1 copy.33
  20.7 7.6 %all-to-all-start = ((bf16[8,384,256]{2,0,1:T(8,128)(2,1)}), bf16[8,384,256]{2,0,1:T(8,128)(2,1)S(1)}, u32[]{:S(2)}, u32[]{:S(2)}) async-start(bf16[8,384,256]{2,0,1:T(8,128)(2,1)} %copy.33), calls=%async_computation | async-start | bytes 3145728 | tf_op jit(solution)/shard_map/all_to_all | solution.py:45
  28.8 10.2 %copy.34 = bf16[8,2048,256]{2,0,1:T(8,128)(2,1)} copy(bf16[8,2048,256]{2,1,0:T(8,128)(2,1)} %param.12) | data formatting | bytes 16777216 | tf_op args[0]
  40.4 0.6 fusion.24
  41.0 6.5 %copy.32 = bf16[512,4096]{0,1:T(8,128)(2,1)} copy(bf16[512,4096]{1,0:T(8,128)(2,1)} %param.14) | data formatting | bytes 8388608 | tf_op args[2]
  47.5 11.1 %reshape.174 = bf16[8,64,64,8,8]{1,0,4,3,2:T(8,128)(2,1)} reshape(bf16[512,4096]{0,1:T(8,128)(2,1)} %copy.32) | data formatting | bytes 8388608 | tf_op jit(solution)/shard_map/reshape | solution.py:53
  58.6 14.6 %copy.35 = bf16[8,64,64,8,8]{2,3,4,1,0:T(8,128)(2,1)} copy(bf16[8,64,64,8,8]{1,0,4,3,2:T(8,128)(2,1)} %reshape.174) | data formatting | bytes 8388608
  73.3 13.9 %pad_maximum_fusion = bf16[8,2432,256]{2,0,1:T(8,128)(2,1)} fusion(bf16[8,384,256]{2,0,1:T(8,128)(2,1)S(1)} %all-to-all-done, bf16[8,2048,256]{2,0,1:T(8,128)(2,1)} %copy.34), kind=kLoop, calls=%fused_computation.34 | loop fusion | flops 4980736 | bytes 19922944 | tf_op jit(solution)/shard_map/concatenate | solution.py:77
  87.2 74.6 %while.32 = (s32[]{:T(128)}, f32[256,256]{1,0:T(8,128)S(1)}, f32[256]{0:T(256)S(1)}, f32[8,4096]{1,0:T(8,128)S(1)}, bf16[8,64,64,8,8]{2,3,4,1,0:T(8,128)(2,1)}, ...) while((s32[]{:T(128)}, f32[256,256]{1,0:T(8,128)S(1)}, ...), condition=%wide.region_4.5_spmd.clone, body=%wide.region_3.4_spmd.clone.sunk | while | flops 686954496 | bytes 14281868 | solution.py:83
  87.5 4.8 %gather_fusion = bf16[512,8,256]{2,1,0:T(8,128)(2,1)S(1)} fusion(bf16[8,2432,256]{2,0,1:T(8,128)(2,1)} %get-tuple-element.408, s32[1024]{0:T(1024)S(1)} %pad_clamp_fusion.3), kind=kCustom, calls=%fused_computation.clone.clone.1 | custom fusion | bytes 4196352 | tf_op jit(solution)/shard_map/while/body/eval_jaxpr/jit(_take)/gather | solution.py:80
  92.3 2.4 fusion.93
  94.7 0.9 fusion.95
  95.7 0.8 fusion.94
  96.8 4.8 %gather_fusion = bf16[512,8,256]{2,1,0:T(8,128)(2,1)S(1)} fusion(bf16[8,2432,256]{2,0,1:T(8,128)(2,1)} %get-tuple-element.408, s32[1024]{0:T(1024)S(1)} %pad_clamp_fusion.3), kind=kCustom, calls=%fused_computation.clone.clone.1 | custom fusion | bytes 4196352 | tf_op jit(solution)/shard_map/while/body/eval_jaxpr/jit(_take)/gather | solution.py:80
  101.6 2.4 fusion.93
  104.0 0.9 fusion.95
  105.0 0.8 fusion.94
  106.1 4.8 %gather_fusion = bf16[512,8,256]{2,1,0:T(8,128)(2,1)S(1)} fusion(bf16[8,2432,256]{2,0,1:T(8,128)(2,1)} %get-tuple-element.408, s32[1024]{0:T(1024)S(1)} %pad_clamp_fusion.3), kind=kCustom, calls=%fused_computation.clone.clone.1 | custom fusion | bytes 4196352 | tf_op jit(solution)/shard_map/while/body/eval_jaxpr/jit(_take)/gather | solution.py:80
  110.9 2.4 fusion.93
  113.4 0.9 fusion.95
  114.3 0.8 fusion.94
  115.4 4.8 %gather_fusion = bf16[512,8,256]{2,1,0:T(8,128)(2,1)S(1)} fusion(bf16[8,2432,256]{2,0,1:T(8,128)(2,1)} %get-tuple-element.408, s32[1024]{0:T(1024)S(1)} %pad_clamp_fusion.3), kind=kCustom, calls=%fused_computation.clone.clone.1 | custom fusion | bytes 4196352 | tf_op jit(solution)/shard_map/while/body/eval_jaxpr/jit(_take)/gather | solution.py:80
  120.2 2.4 fusion.93
  122.7 0.9 fusion.95
  123.6 0.8 fusion.94
  124.7 4.8 %gather_fusion = bf16[512,8,256]{2,1,0:T(8,128)(2,1)S(1)} fusion(bf16[8,2432,256]{2,0,1:T(8,128)(2,1)} %get-tuple-element.408, s32[1024]{0:T(1024)S(1)} %pad_clamp_fusion.3), kind=kCustom, calls=%fused_computation.clone.clone.1 | custom fusion | bytes 4196352 | tf_op jit(solution)/shard_map/while/body/eval_jaxpr/jit(_take)/gather | solution.py:80
  129.6 2.4 fusion.93
  132.0 0.9 fusion.95
  132.9 0.8 fusion.94
  134.1 4.8 %gather_fusion = bf16[512,8,256]{2,1,0:T(8,128)(2,1)S(1)} fusion(bf16[8,2432,256]{2,0,1:T(8,128)(2,1)} %get-tuple-element.408, s32[1024]{0:T(1024)S(1)} %pad_clamp_fusion.3), kind=kCustom, calls=%fused_computation.clone.clone.1 | custom fusion | bytes 4196352 | tf_op jit(solution)/shard_map/while/body/eval_jaxpr/jit(_take)/gather | solution.py:80
  138.9 2.4 fusion.93
  141.3 0.9 fusion.95
  142.3 0.8 fusion.94
  143.4 4.8 %gather_fusion = bf16[512,8,256]{2,1,0:T(8,128)(2,1)S(1)} fusion(bf16[8,2432,256]{2,0,1:T(8,128)(2,1)} %get-tuple-element.408, s32[1024]{0:T(1024)S(1)} %pad_clamp_fusion.3), kind=kCustom, calls=%fused_computation.clone.clone.1 | custom fusion | bytes 4196352 | tf_op jit(solution)/shard_map/while/body/eval_jaxpr/jit(_take)/gather | solution.py:80
  148.2 2.4 fusion.93
  150.6 0.9 fusion.95
  151.6 0.8 fusion.94
  152.7 4.8 %gather_fusion = bf16[512,8,256]{2,1,0:T(8,128)(2,1)S(1)} fusion(bf16[8,2432,256]{2,0,1:T(8,128)(2,1)} %get-tuple-element.408, s32[1024]{0:T(1024)S(1)} %pad_clamp_fusion.3), kind=kCustom, calls=%fused_computation.clone.clone.1 | custom fusion | bytes 4196352 | tf_op jit(solution)/shard_map/while/body/eval_jaxpr/jit(_take)/gather | solution.py:80
  157.5 2.4 fusion.93
  160.0 0.9 fusion.95
  160.9 0.8 fusion.94
  161.7 0.8 copy.36
  162.6 68.2 %all-reduce.1 = (f32[]{:T(128)}, f32[]{:T(128)}, f32[256]{0:T(256)S(1)}) all-reduce(f32[]{:T(128)S(6)} %convert_element_type.33, f32[]{:T(128)} %get-tuple-element.275, f32[256]{0:T(256)S(1)} %get-tuple-element.169), channel_id=1, replica_groups=mesh['tile'=16,'lev'=8] {'tile','lev'}, use_global_device_ids=true, to_apply=%region_0.1 | all-reduce | flops 258 | bytes 2064 | tf_op jit(solution)/shard_map/psum | solution.py:52
  232.1 75.3 %all-reduce.4.cloned.1.call-done = f32[256,256]{0,1:T(8,128)} async-done(((f32[256,256]{0,1:T(8,128)}), f32[256,256]{0,1:T(8,128)}) %all-reduce.4.cloned.1.call-update) | async-done | bytes 262160 | tf_op jit(solution)/shard_map/psum | solution.py:84
  307.4 1.1 copy.37
  308.5 1.0 fusion.19
  309.7 11.7 %cholesky.49 = f32[128,128]{1,0:T(8,128)S(1)} custom-call(f32[128,128]{1,0:T(8,128)S(1)} %cholesky.115), custom_call_target="Cholesky" | custom-call | tf_op jit(solution)/shard_map/jit(cholesky)/cholesky | solution.py:26
  321.4 9.8 %custom-call.18 = f32[1,128,128]{1,2,0:T(8,128)S(1)} custom-call(f32[1,128,128]{2,1,0:T(8,128)S(1)} %get-tuple-element.280), custom_call_target="InvertDiagBlocksLowerTriangular" | custom-call | tf_op jit(solution)/shard_map/jit(cholesky)/cholesky | solution.py:26
  331.8 11.7 %cholesky.103 = f32[128,128]{1,0:T(8,128)S(1)} custom-call(f32[128,128]{1,0:T(8,128)S(1)} %convolution_subtract_fusion.2), custom_call_target="Cholesky" | custom-call | tf_op jit(solution)/shard_map/jit(cholesky)/cholesky | solution.py:26
  343.5 0.7 compare_reduce_fusion
  345.7 4.1 while.30
  346.3 1.4 bitcast_dynamic-update-slice_fusion.2
  348.4 1.4 bitcast_dynamic-update-slice_fusion.2
  349.8 19.9 %custom-call.19 = f32[2,128,128]{1,2,0:T(8,128)S(1)} custom-call(f32[2,128,128]{2,1,0:T(8,128)S(1)} %get-tuple-element.177), custom_call_target="InvertDiagBlocksLowerTriangular" | custom-call | tf_op jit(solution)/shard_map/jit(_cho_solve)/triangular_solve | solution.py:27
  371.8 0.7 multiply_reduce_fusion
  373.6 20.7 %while.31 = (s32[]{:T(128)}, f32[256,256]{0,1:T(8,128)S(1)}, f32[256,256]{1,0:T(8,128)S(1)}, s32[]{:T(128)}) while((s32[]{:T(128)}, f32[256,256]{0,1:T(8,128)S(1)}, f32[256,256]{1,0:T(8,128)S(1)}, s32[]{:T(128)}) %tuple.79), condition=%wide.region_12.13_spmd.clone, body=%wide.region_11.12_spmd.clone.sunk | while | flops 604241920 | bytes 3407925 | solution.py:18
  377.5 0.6 convolution_bitcast_fusion.4
  381.9 0.6 convolution_bitcast_fusion.4
  394.4 11.5 %convolution_bitcast_fusion.2 = f32[16384,256]{0,1:T(8,128)} fusion(bf16[16384,256]{1,0:T(8,128)(2,1)} %bitcast.141, f32[256,256]{0,1:T(8,128)S(1)} %get-tuple-element.168, f32[256]{0:T(256)S(1)} %bitcast.147, f32[]{:T(128)S(6)} %sqrt.17), kind=kOutput, calls=%fused_computation.32 | convolution fusion | flops 2147680256 | bytes 25428996 | tf_op jit(solution)/shard_map/dot_general | solution.py:87
  405.8 17.5 %copy.46 = f32[16384,256]{1,0:T(8,128)} copy(f32[16384,256]{0,1:T(8,128)} %convolution_bitcast_fusion.2) | data formatting | bytes 33554432 | tf_op jit(solution)/shard_map/reshape | solution.py:90
  423.3 9.6 %add_convert_fusion = bf16[8,2048,256]{2,1,0:T(8,128)(2,1)} fusion(f32[8,2048,256]{2,1,0:T(8,128)} %bitcast.142, f32[8,2048]{1,0:T(8,128)S(1)} %copy-done.2), kind=kLoop, calls=%fused_computation.33 | loop fusion | flops 8388608 | bytes 25231360 | tf_op jit(solution)/shard_map/convert_element_type | solution.py:91
  (188 shorter events, 26.9 us)
Async XLA Ops:
  20.7 52.6 %all-to-all-start = ((bf16[8,384,256]{2,0,1:T(8,128)(2,1)}), bf16[8,384,256]{2,0,1:T(8,128)(2,1)S(1)}, u32[]{:S(2)}, u32[]{:S(2)}) async-start(bf16[8,384,256]{2,0,1:T(8,128)(2,1)} %copy.33), calls=%async_computation | async-start | bytes 3145728 | tf_op jit(solution)/shard_map/all_to_all | solution.py:45
  28.2 279.2 %all-reduce.4.cloned.1.call-start = ((), (), s32[]{:S(2)}) async-start(), calls=%async_computation.1 | async-start | bytes 524288 | tf_op jit(solution)/shard_map/psum | solution.py:84
  28.8 10.9 %copy-start.3 = (s32[4096]{0:T(1024)S(1)}, s32[4096]{0:T(1024)}, u32[]{:S(2)}) copy-start(s32[4096]{0:T(1024)} %param.17) | copy-start | bytes 49156
  28.8 11.5 %copy-start = (f32[32768]{0:T(1024)S(1)}, f32[32768]{0:T(1024)}, u32[]{:S(2)}) copy-start(f32[32768]{0:T(1024)} %param.15) | copy-start | bytes 393220
  28.8 11.6 %copy-start.1 = (f32[32768]{0:T(1024)S(1)}, f32[32768]{0:T(1024)}, u32[]{:S(2)}) copy-start(f32[32768]{0:T(1024)} %param.16) | copy-start | bytes 393220
  405.8 17.5 %copy-start.2 = (f32[8,2048]{1,0:T(8,128)S(1)}, f32[8,2048]{1,0:T(8,128)}, u32[]{:S(2)}) copy-start(f32[8,2048]{1,0:T(8,128)} %param.13) | copy-start | bytes 196612
Sparse Core Ops, SparseCore 0:
  162.7 144.6 all-reduce.3
where the time goes:
time: 446 us; the launch traced here: 440 us
  local copies, waits for them, and re-layouts  120 us (27%)
  other arithmetic  81.9 us (18%)
  waiting for transfers between devices  75.4 us (17%)
  blocking collectives  68.2 us (15%)
  matrix products  66.7 us (15%)
  between operations  18 us (4%)
  starting transfers between devices  8.08 us (2%)
    psum x1, waiting for transfers between devices, per_device(): gram_whole, projection = lax.psum((gram_part, projection), ('tile', 'lev'))  75.3 us
    psum x1, blocking collectives, per_device(): numerator, obs_total = lax.psum((numerator, obs_local), ('tile', 'lev'))  68.2 us
    gather x8, local copies, waits for them, and re-layouts, whole_terms(): picked = jnp.take(extended, column_groups[group_index], axis=1)  38.4 us
    another operation x6, other arithmetic, transform_weights(): factor = jnp.linalg.cholesky(system)  34 us
    unnamed x12, local copies, waits for them, and re-layouts  31.5 us
    another operation x3, other arithmetic, transform_weights(): inverse = jax.scipy.linalg.cho_solve((factor, True), identity)  19.9 us
    dot_general x8, matrix products, project(): jnp.einsum('boql,lbqk->bok', operators[group_index], picked, preferred_el...  19.5 us
    reshape x1, local copies, waits for them, and re-layouts, per_device(): updated.reshape(lev_dev, col_dev, members)  17.5 us
  transfers between devices with their start and end apart: 2, of which 1 were waited for; matrix products, arithmetic and copies ran while one was open for 10% of the time, Pallas kernels for 0%

commit v1 on v0

v1 whole, which is shorter than its diff:
```python
import functools

import jax
import jax.numpy as jnp
from jax import lax
from jax.experimental import pallas as pl
from jax.experimental.pallas import tpu as pltpu
from jax.sharding import PartitionSpec as P

F32 = jnp.float32
BF16 = jnp.bfloat16
AXES = ("tile", "lev")
VMEM_BYTES = 60 << 20
GROUP = 16
CHUNK = 64
PACK = 104


def split3(value):
    high = value.astype(BF16)
    rest = value - high.astype(F32)
    middle = rest.astype(BF16)
    low = (rest - middle.astype(F32)).astype(BF16)
    return high, middle, low


def send_kernel(send_ref, anom_ref, out_ref, level_ref, wide_ref, sems):
    lev_dev, col_dev, members = anom_ref.shape
    slots = send_ref.shape[1]
    copies = [
        pltpu.make_async_copy(anom_ref.at[v], level_ref.at[v], sems.at[v]) for v in range(lev_dev)
    ]
    for copy in copies:
        copy.start()
    listed = jnp.broadcast_to(send_ref[...].astype(F32), (8, slots)).T[:, 0:1]
    lanes = lax.broadcasted_iota(jnp.int32, (slots, col_dev), 1).astype(F32)
    chosen = jnp.where(lanes == listed, 1.0, 0.0).astype(BF16)
    for v in range(lev_dev):
        copies[v].wait()
        rows = jnp.dot(chosen, level_ref[v], preferred_element_type=F32)
        for h in range(members // 128):
            wide_ref.at[h][pl.ds(v, slots, stride=lev_dev), :] = rows[:, h * 128 : (h + 1) * 128]
    for h in range(members // 128):
        half = wide_ref[h].reshape(slots, lev_dev, 128)
        out_ref[:, :, h * 128 : (h + 1) * 128] = half.astype(BF16)


def gather_sent(send_cols, anomalies):
    lev_dev, col_dev, members = anomalies.shape
    slots = send_cols.shape[1]
    return pl.pallas_call(
        send_kernel,
        in_specs=[pl.BlockSpec(memory_space=pltpu.VMEM), pl.BlockSpec(memory_space=pl.ANY)],
        out_specs=pl.BlockSpec(memory_space=pltpu.VMEM),
        out_shape=jax.ShapeDtypeStruct((slots, lev_dev, members), BF16),
        scratch_shapes=[
            pltpu.VMEM((lev_dev, col_dev, members), BF16),
            pltpu.VMEM((members // 128, slots * lev_dev, 128), F32),
            pltpu.SemaphoreType.DMA((lev_dev,)),
        ],
        compiler_params=pltpu.CompilerParams(vmem_limit_bytes=VMEM_BYTES),
        name="gather_sent",
    )(send_cols, anomalies)


def prepare_kernel(count_ref, op_ref, rinv_ref, innov_ref, pair_ref, sums_ref, wide_ref):
    blocks, width = op_ref.shape
    per_block = rinv_ref.shape[1]
    points = width // per_block
    tiles = width // 128
    count = count_ref[0]
    spread_row = lax.broadcasted_iota(jnp.int32, (per_block, width), 0)
    spread_lane = lax.broadcasted_iota(jnp.int32, (per_block, width), 1)
    expand = jnp.where(spread_lane // points == spread_row, 1.0, 0.0).astype(BF16)
    live = lax.broadcasted_iota(jnp.int32, (blocks, per_block), 0) < count
    innov = innov_ref[...]
    squares = jnp.where(live, rinv_ref[...] * innov * innov, 0.0)
    numerator = jnp.sum(squares, axis=(0, 1), keepdims=True)
    total = jnp.full((1, 1), count * per_block, jnp.int32).astype(F32)
    lane = lax.broadcasted_iota(jnp.int32, (8, 256), 1)
    sums_ref[...] = jnp.where(lane == 0, numerator, jnp.where(lane == 1, total, 0.0))
    low_half = lax.broadcasted_iota(jnp.int32, (1, 1, 128), 2) < points

    def chunk(step, carried):
        start = pl.multiple_of(step * CHUNK, CHUNK)
        alive = start + lax.broadcasted_iota(jnp.int32, (CHUNK, per_block), 0) < count
        weight = jnp.where(alive, jnp.sqrt(rinv_ref[pl.ds(start, CHUNK), :]), 0.0)
        parts = split3(weight)
        wide = jnp.dot(parts[0], expand, preferred_element_type=F32)
        wide = wide + jnp.dot(parts[1], expand, preferred_element_type=F32)
        wide = wide + jnp.dot(parts[2], expand, preferred_element_type=F32)
        weighted = op_ref[pl.ds(start, CHUNK), :].astype(F32) * wide
        for r in range(tiles):
            wide_ref[pl.ds(r, CHUNK, stride=tiles), :] = weighted[:, r * 128 : (r + 1) * 128]
        rows = wide_ref[...].reshape(CHUNK // 2, 2, tiles, 128)
        first, second = rows[:, 0], rows[:, 1]
        first_turned = pltpu.roll(first.reshape(-1, 128), 64, 1).reshape(first.shape)
        second_turned = pltpu.roll(second.reshape(-1, 128), 64, 1).reshape(second.shape)
        pieces = [
            jnp.where(low_half, first, 0.0),
            jnp.where(low_half, first_turned, 0.0),
            jnp.where(low_half, 0.0, second_turned),
            jnp.where(low_half, 0.0, second),
        ]
        out = pl.multiple_of(step * (CHUNK // 2), CHUNK // 2)
        pair_ref[pl.ds(out, CHUNK // 2)] = jnp.concatenate(pieces, axis=1).astype(BF16)
        return carried

    lax.fori_loop(0, blocks // CHUNK, chunk, 0)


def prepare(obs_count, obs_op, rinv_blocks, innov_blocks):
    blocks = obs_op.shape[0]
    vmem = pl.BlockSpec(memory_space=pltpu.VMEM)
    return pl.pallas_call(
        prepare_kernel,
        in_specs=[pl.BlockSpec(memory_space=pltpu.SMEM), vmem, vmem, vmem],
        out_specs=[vmem, vmem],
        out_shape=[
            jax.ShapeDtypeStruct((blocks // 2, 128, 128), BF16),
            jax.ShapeDtypeStruct((8, 256), F32),
        ],
        scratch_shapes=[pltpu.VMEM((CHUNK * 32, 128), F32)],
        compiler_params=pltpu.CompilerParams(vmem_limit_bytes=VMEM_BYTES),
        name="prepare_operators",
    )(obs_count, obs_op, rinv_blocks, innov_blocks)


def gram_kernel(
    cols_ref, count_ref, core_ref, own_ref, remote_ref, pair_ref, innov_ref, sums_ref,
    keep_ref, give_ref, table, pairs, support, scaled, total, sems,
):
    own_cols = own_ref.shape[0]
    n_pairs = pair_ref.shape[0]
    chunk_pairs = CHUNK // 2
    chunks = n_pairs // chunk_pairs
    own = pltpu.make_async_copy(own_ref, table.at[pl.ds(0, own_cols)], sems.at[chunks])
    remote = pltpu.make_async_copy(
        remote_ref, table.at[pl.ds(own_cols, remote_ref.shape[0])], sems.at[chunks + 1]
    )
    own.start()
    remote.start()
    fetches = []
    for k in range(chunks):
        part = pl.ds(k * chunk_pairs, chunk_pairs)
        fetches.append(pltpu.make_async_copy(pair_ref.at[part], pairs.at[part], sems.at[k]))
        fetches[k].start()
    total[...] = jnp.zeros_like(total)
    groups = (count_ref[0] + GROUP - 1) // GROUP
    own.wait()
    remote.wait()

    def step(g, carried):
        for i in range(GROUP * 8):
            support[i] = table[cols_ref[g * (GROUP * 8) + i]]
        for j in range(GROUP // 2):
            points = support[j * 16 : (j + 1) * 16].reshape(128, 256)
            images = jnp.dot(pairs[g * (GROUP // 2) + j], points, preferred_element_type=F32)
            scaled[j * 128 : (j + 1) * 128, :] = images.astype(BF16)
        rows = scaled[...]
        parts = split3(innov_ref[pl.ds(g, 1), :])
        row_index = lax.broadcasted_iota(jnp.int32, (16, GROUP * 64), 0)
        extra = jnp.where(row_index == 0, parts[0].astype(F32), 0.0)
        extra = jnp.where(row_index == 1, parts[1].astype(F32), extra)
        extra = jnp.where(row_index == 2, parts[2].astype(F32), extra).astype(BF16)
        left = jnp.concatenate([rows.T, extra], axis=0)
        total[...] += jnp.dot(left, rows, preferred_element_type=F32)
        return carried

    per_chunk = CHUNK // GROUP
    for k in range(chunks):
        fetches[k].wait()
        last = jnp.minimum(groups, (k + 1) * per_chunk)
        lax.fori_loop(k * per_chunk, jnp.maximum(last, k * per_chunk), step, 0)

    projection = total[256:257, :] + total[257:258, :] + total[258:259, :]
    row = lax.broadcasted_iota(jnp.int32, (8, 256), 0)
    ending = jnp.where(row == 0, projection, jnp.where(row == 1, sums_ref[...], 0.0))
    zeros = jnp.zeros((8, 256), F32)
    first = total[0:PACK, :]
    corner = jnp.concatenate([total[128:192, 128:256], total[192:256, 128:256]], axis=1)
    second = jnp.concatenate([total[PACK:128, :], corner, ending, zeros], axis=0)
    core = core_ref[0]

    @pl.when(core == 0)
    def _():
        keep_ref[...] = first
        give_ref[...] = second

    @pl.when(core != 0)
    def _():
        keep_ref[...] = second
        give_ref[...] = first


def gram_sums(obs_cols, obs_count, core, own, remote, pairs, innov_rows, sums):
    vmem = pl.BlockSpec(memory_space=pltpu.VMEM)
    smem = pl.BlockSpec(memory_space=pltpu.SMEM)
    anywhere = pl.BlockSpec(memory_space=pl.ANY)
    half = jax.ShapeDtypeStruct((PACK, 256), F32)
    chunks = pairs.shape[0] // (CHUNK // 2)
    return pl.pallas_call(
        gram_kernel,
        in_specs=[smem, smem, smem, anywhere, anywhere, anywhere, vmem, vmem],
        out_specs=[vmem, vmem],
        out_shape=[half, half],
        scratch_shapes=[
            pltpu.VMEM((own.shape[0] + remote.shape[0],) + own.shape[1:], BF16),
            pltpu.VMEM(pairs.shape, BF16),
            pltpu.VMEM((GROUP * 8, 8, 256), BF16),
            pltpu.VMEM((GROUP * 64, 256), BF16),
            pltpu.VMEM((272, 256), F32),
            pltpu.SemaphoreType.DMA((chunks + 2,)),
        ],
        compiler_params=pltpu.CompilerParams(vmem_limit_bytes=VMEM_BYTES),
        name="gram_sums",
    )(obs_cols, obs_count, core, own, remote, pairs, innov_rows, sums)


def dot3(left, right):
    left_high = left.astype(BF16)
    left_low = (left - left_high.astype(F32)).astype(BF16)
    right_high = right.astype(BF16)
    right_low = (right - right_high.astype(F32)).astype(BF16)
    return jnp.dot(
        jnp.concatenate([left_high, left_high, left_low], axis=1),
        jnp.concatenate([right_high, right_low, right_high], axis=0),
        preferred_element_type=F32,
    )


def apply_kernel(
    core_ref, mine_ref, other_ref, mean_ref, anom_ref, out_ref,
    levels, results, approx_ref, inverse_ref, in_sems, out_sems,
):
    lev_dev = anom_ref.shape[0]
    members = anom_ref.shape[2]
    loads = [
        pltpu.make_async_copy(anom_ref.at[v], levels.at[v], in_sems.at[v]) for v in range(lev_dev)
    ]
    for load in loads:
        load.start()
    core = core_ref[0]
    mine, other = mine_ref[...], other_ref[...]
    first = jnp.where(core == 0, mine, other)
    second = jnp.where(core == 0, other, mine)
    upper = jnp.concatenate([first, second[: 128 - PACK]], axis=0)
    packed = second[128 - PACK : 192 - PACK]
    corner = jnp.concatenate([packed[:, :128], packed[:, 128:]], axis=0)
    projection = second[192 - PACK : 193 - PACK]
    sums = second[193 - PACK : 194 - PACK]
    side = upper[:, 128:]
    gram = jnp.concatenate([upper, jnp.concatenate([side.T, corner], axis=1)], axis=0)
    gram = 0.5 * (gram + gram.T)

    numerator, obs_total = sums[:, 0:1], sums[:, 1:2]
    shift = (members - 1.0) * obs_total / numerator
    rows = lax.broadcasted_iota(jnp.int32, (members, members), 0)
    lanes = lax.broadcasted_iota(jnp.int32, (members, members), 1)
    identity = jnp.where(rows == lanes, 1.0, 0.0)
    system = gram + shift * identity
    norm = jnp.sqrt(jnp.sum(system * system, axis=(0, 1), keepdims=True))
    approx_ref[...] = system / norm
    inverse_ref[...] = identity
    lowest = jnp.minimum(jnp.sqrt(shift / norm), 1.0)[0, 0]

    def advance(scale):
        approx, inverse = approx_ref[...], inverse_ref[...]
        middle = (1.5 * scale) * identity - (0.5 * scale * scale * scale) * dot3(inverse, approx)
        approx_ref[...] = dot3(approx, middle)
        inverse_ref[...] = dot3(middle, inverse)

    def more(carried):
        turn, low = carried
        return jnp.logical_and(turn < 60, low < 0.999)

    def turn_once(carried):
        turn, low = carried
        x = jnp.maximum(low, 0.02)
        scale = 1.7323 + x * (-0.88804 + x * (-0.071549 + x * (0.385863 - 0.15965 * x)))
        scale = jnp.maximum(scale, 1.0)
        advance(scale)
        at_low = 0.5 * scale * low * (3.0 - scale * scale * low * low)
        at_one = 0.5 * scale * (3.0 - scale * scale)
        return turn + 1, jnp.minimum(at_low, at_one)

    lax.while_loop(more, turn_once, (jnp.int32(0), lowest))
    advance(1.0)
    inverse = inverse_ref[...]
    line = jnp.broadcast_to(projection, (128, members)).T
    weights = dot3(inverse, dot3(inverse, line)) / norm
    root = (jnp.sqrt((members - 1.0) / norm)) * inverse
    transform = (root + jnp.concatenate([weights, weights], axis=1)).astype(BF16)

    means = mean_ref[...].T
    stores = []
    for v in range(lev_dev):
        loads[v].wait()
        updated = jnp.dot(levels[v], transform, preferred_element_type=F32)
        results[v] = (means[:, v : v + 1] + updated).astype(BF16)
        stores.append(pltpu.make_async_copy(results.at[v], out_ref.at[v], out_sems.at[v]))
        stores[v].start()
    for store in stores:
        store.wait()


def solve_and_apply(core, mine, other, mean_state, anomalies):
    vmem = pl.BlockSpec(memory_space=pltpu.VMEM)
    anywhere = pl.BlockSpec(memory_space=pl.ANY)
    lev_dev, _, members = anomalies.shape
    return pl.pallas_call(
        apply_kernel,
        in_specs=[pl.BlockSpec(memory_space=pltpu.SMEM), vmem, vmem, vmem, anywhere],
        out_specs=anywhere,
        out_shape=jax.ShapeDtypeStruct(anomalies.shape, BF16),
        scratch_shapes=[
            pltpu.VMEM(anomalies.shape, BF16),
            pltpu.VMEM(anomalies.shape, BF16),
            pltpu.VMEM((members, members), F32),
            pltpu.VMEM((members, members), F32),
            pltpu.SemaphoreType.DMA((lev_dev,)),
            pltpu.SemaphoreType.DMA((lev_dev,)),
        ],
        compiler_params=pltpu.CompilerParams(vmem_limit_bytes=VMEM_BYTES),
        name="solve_and_apply",
    )(core, mine, other, mean_state, anomalies)


def turns(devices, stride, distance):
    pairs = []
    for device in range(devices):
        place = (device // stride) % 4
        pairs.append((device, device + ((place + distance) % 4 - place) * stride))
    return pairs


def sum_over(value, devices, stride):
    arrived = [lax.ppermute(value, AXES, turns(devices, stride, d)) for d in (2, 1, 3)]
    return (value + arrived[0]) + (arrived[1] + arrived[2])


def per_device(
    devices, anomalies, mean_state, obs_op, innovations, obs_rinv, obs_cols, send_cols, obs_count
):
    blocks = obs_op.shape[0]
    per_block = innovations.shape[0] // blocks
    core = (lax.axis_index("lev") % 2).astype(jnp.int32).reshape(1)
    outgoing = gather_sent(send_cols, anomalies)
    remote = lax.all_to_all(outgoing, "tile", split_axis=0, concat_axis=0, tiled=True)

    own = jnp.transpose(anomalies, (1, 0, 2))
    rinv_blocks = obs_rinv.reshape(blocks, per_block)
    innov_blocks = innovations.reshape(blocks, per_block)
    pairs, sums = prepare(obs_count, obs_op, rinv_blocks, innov_blocks)
    weighted = jnp.sqrt(rinv_blocks) * innov_blocks
    weighted = jnp.where(jnp.arange(blocks)[:, None] < obs_count[0], weighted, 0.0)
    weighted = weighted.reshape(blocks, per_block // 2, 2).swapaxes(1, 2)
    innov_rows = weighted.reshape(blocks // GROUP, GROUP * per_block)

    keep, give = gram_sums(obs_cols, obs_count, core, own, remote, pairs, innov_rows, sums)
    value = keep + lax.ppermute(give, AXES, [(d, d ^ 1) for d in range(devices)])
    for stride in (2, 8, 32):
        value = sum_over(value, devices, stride)
    other = lax.ppermute(value, AXES, [(d, d ^ 1) for d in range(devices)])
    return solve_and_apply(core, value, other, mean_state, anomalies)


def solution(mesh):
    return jax.shard_map(
        functools.partial(per_device, mesh.size),
        mesh=mesh,
        in_specs=(
            P("lev", "tile", None),
            P("lev", "tile"),
            P(("tile", "lev"), None),
            P(("tile", "lev")),
            P(("tile", "lev")),
            P(("tile", "lev")),
            P("tile", None),
            P(("tile", "lev")),
        ),
        out_specs=P("lev", "tile", None),
        check_vma=False,
    )
```

time: 446 us -> 149 us (0.33); the launches traced: 440 us -> 148 us
  local copies, waits for them, and re-layouts: 120 us -> 30.6 us
  other arithmetic: 81.9 us -> 7.31 us
  blocking collectives: 68.2 us -> 0 us
  matrix products: 66.7 us -> 0 us
  waiting for transfers between devices: 75.4 us -> 13.8 us
  Pallas kernels: 0 us -> 55.3 us
  starting transfers between devices: 8.08 us -> 39.9 us
  between operations: 18 us -> 0.94 us
    psum x1 -> x0, waiting for transfers between devices: 75.3 us -> none  [per_device(): gram_whole, projection = lax.psum((gram_part, projection), ('tile', 'lev'))]
    psum x1 -> x0, blocking collectives: 68.2 us -> none  [per_device(): numerator, obs_total = lax.psum((numerator, obs_local), ('tile', 'lev'))]
    dot_general x68 -> x0, matrix products: 64.4 us -> none  [the longest x8 19.5 us: project(): jnp.einsum('boql,lbqk->bok', operators[group_index], picked, preferred_el...]
    pallas_call x0 -> x4, Pallas kernels: none -> 55.3 us  [the longest x1 16.7 us: prepare(): pl.pallas_call(prepare_kernel, in_specs=[pl.BlockSpec(memory_space=pltpu....]
    another operation x9 -> x0, other arithmetic: 54 us -> none  [the longest x6 34 us: transform_weights(): factor = jnp.linalg.cholesky(system)]
    gather x9 -> x0, local copies, waits for them, and re-layouts: 48.8 us -> none  [the longest x8 38.4 us: whole_terms(): picked = jnp.take(extended, column_groups[group_index], axis=1)]
    ppermute x0 -> x11, starting transfers between devices: none -> 32.3 us  [the longest x9 15.8 us: sum_over(): lax.ppermute(value, AXES, turns(devices, stride, d))]
    reshape x4 -> x3, local copies, waits for them, and re-layouts: 28.7 us -> 2.93 us  [the longest x1 1.31 us: per_device(): innov_rows = weighted.reshape(blocks // GROUP, GROUP * per_block)]
  transfers between devices with their start and end apart: 2 -> 12, of which waited for: 1 -> 9; matrix products, arithmetic and copies ran while one was open for 10% -> 24% of each run, Pallas kernels for 0% -> 11%
where the time goes in v1:
time: 149 us; the launch traced here: 148 us
  Pallas kernels  55.3 us (37%)
  starting transfers between devices  39.9 us (27%)
  local copies, waits for them, and re-layouts  30.6 us (21%)
  waiting for transfers between devices  13.8 us (9%)
  other arithmetic  7.31 us (5%)
    pallas_call x1, Pallas kernels, prepare(): pl.pallas_call(prepare_kernel, in_specs=[pl.BlockSpec(memory_space=pltpu....  16.7 us
    ppermute x9, starting transfers between devices, sum_over(): lax.ppermute(value, AXES, turns(devices, stride, d))  15.8 us
    pallas_call x1, Pallas kernels, gram_sums(): pl.pallas_call(gram_kernel, in_specs=[smem, smem, smem, anywhere, anywher...  13.8 us
    pallas_call x1, Pallas kernels, solve_and_apply(): pl.pallas_call(apply_kernel, in_specs=[pl.BlockSpec(memory_space=pltpu.SM...  13.7 us
    ppermute x1, starting transfers between devices, per_device(): lax.ppermute(give, AXES, [(d, d ^ 1) for d in range(devices)])  12.5 us
    unnamed x11, local copies, waits for them, and re-layouts  12 us
    ppermute x9, waiting for transfers between devices, sum_over(): lax.ppermute(value, AXES, turns(devices, stride, d))  11.6 us
    pallas_call x1, Pallas kernels, gather_sent(): pl.pallas_call(send_kernel, in_specs=[pl.BlockSpec(memory_space=pltpu.VME...  11 us
  transfers between devices with their start and end apart: 12, of which 9 were waited for; matrix products, arithmetic and copies ran while one was open for 24% of the time, Pallas kernels for 11%

profile of v1, /device:TPU:1, one launch (start us, length us, event | category | flops | bytes accessed | tf_op | source)
XLA Modules:
  0.0 147.8 jit_solution(523648482616739364)
XLA Ops:
  0.0 11.0 %gather_sent.1 = bf16[384,8,256]{2,1,0:T(8,128)(2,1)} custom-call(s32[1,384]{1,0:T(1,128)} %send_ref.1, bf16[8,2048,256]{2,1,0:T(8,128)(2,1)} %anom_ref.3), custom_call_target="tpu_custom_call" | custom-call | tf_op jit(solution)/shard_map/gather_sent/pallas_call | solution.py:51
  11.1 7.6 %all-to-all-start = ((bf16[384,8,256]{2,1,0:T(8,128)(2,1)}), bf16[384,8,256]{2,1,0:T(8,128)(2,1)S(1)}, u32[]{:S(2)}, u32[]{:S(2)}) async-start(bf16[384,8,256]{2,1,0:T(8,128)(2,1)} %gather_sent.1), calls=%async_computation | async-start | bytes 3145728 | tf_op jit(solution)/shard_map/all_to_all | solution.py:349
  18.7 0.0 copy-start.2
  18.7 0.0 copy-start.1
  18.7 10.1 %copy.13 = bf16[8,2048,256]{2,0,1:T(8,128)(2,1)} copy(bf16[8,2048,256]{2,1,0:T(8,128)(2,1)} %anom_ref.3) | data formatting | bytes 16777216 | tf_op args[0]
  29.5 0.0 copy-done.2
  29.5 0.8 reshape.29.innov_ref
  30.3 0.0 copy-done.1
  30.3 0.8 reshape.28.rinv_ref
  31.1 9.8 %mul.8 = f32[512,32,2]{2,1,0:T(8,128)} reshape(f32[32768]{0:T(1024)S(1)} %sqrt_multiply_fusion) | data formatting | bytes 262144 | tf_op jit(solution)/shard_map/mul | solution.py:355
  40.9 6.3 %select_bitcast_fusion = f32[512,2,32]{1,2,0:T(8,128)} fusion(f32[512,32,2]{2,1,0:T(8,128)} %mul.8, pred[512]{0:T(512)(128)(4,1)S(1)} %iota_compare_fusion), kind=kLoop, calls=%fused_computation.1 | loop fusion | flops 32768 | bytes 262656 | tf_op jit(solution)/shard_map/transpose | solution.py:357
  47.2 5.9 %copy.11 = f32[512,2,32]{2,1,0:T(2,128)S(1)} copy(f32[512,2,32]{1,2,0:T(8,128)} %select_bitcast_fusion) | data formatting | bytes 262144 | tf_op jit(solution)/shard_map/transpose | solution.py:357
  53.1 1.3 reshape.30.innov_ref
  54.4 16.7 %prepare_operators.1 = (bf16[256,128,128]{2,1,0:T(8,128)(2,1)}, f32[8,256]{1,0:T(8,128)}) custom-call(s32[1]{0:T(128)} %copy.14.count_ref, bf16[512,4096]{1,0:T(8,128)(2,1)} %op_ref.1, f32[512,64]{1,0:T(8,128)} %reshape.28.rinv_ref, f32[512,64]{1,0:T(8,128)} %reshape.29.innov_ref), custom_call_target="tpu_custom_call" | custom-call | tf_op jit(solution)/shard_map/prepare_operators/pallas_call | solution.py:115
  71.1 0.0 all-to-all-done.remote_ref
  71.1 0.0 copy-start
  71.1 1.2 copy-done
  72.3 13.8 %gram_sums.1 = (f32[104,256]{1,0:T(8,128)}, f32[104,256]{1,0:T(8,128)}) custom-call(s32[4096]{0:T(1024)} %cols_ref.1, s32[1]{0:T(128)} %copy.14.count_ref, s32[1]{0:T(128)} %bitcast.core_ref, bf16[2048,8,256]{2,1,0:T(8,128)(2,1)} %bitcast.8, bf16[384,8,256]{2,1,0:T(8,128)(2,1)} %copy-done, bf16[256,128,128]{2,1,0:T(8,128)(2,1)} %get-tuple-element.9.pair_ref, ...), custom_call_target="tpu_custom_call" | custom-call | tf_op jit(solution)/shard_map/gram_sums/pallas_call | solution.py:202
  86.2 12.5 %collective-permute-start = (f32[104,256]{1,0:T(8,128)}, f32[104,256]{1,0:T(8,128)S(1)}, u32[]{:S(2)}, u32[]{:S(2)}) collective-permute-start(f32[104,256]{1,0:T(8,128)} %get-tuple-element.12), channel_id=1, source_target_pairs={{0,1},{1,0},{2,3},{3,2},{4,5},{5,4},{6,7},{7,6},{8,9},{9,8},{10,11... | collective-permute-start | bytes 319496 | tf_op jit(solution)/shard_map/ppermute | solution.py:361
  98.6 1.2 collective-permute-done
  99.8 0.9 add.35
  100.7 0.1 collective-permute-start.3
  100.8 1.7 %collective-permute-start.2 = (f32[104,256]{1,0:T(8,128)S(1)}, f32[104,256]{1,0:T(8,128)S(1)}, u32[]{:S(2)}, u32[]{:S(2)}) collective-permute-start(f32[104,256]{1,0:T(8,128)S(1)} %add.35), channel_id=1, source_target_pairs={{0,2},{1,3},{2,4},{3,5},{4,6},{5,7},{6,0},{7,1},{8,10},{9,11},{10,... | collective-permute-start | bytes 319496 | tf_op jit(solution)/shard_map/ppermute | solution.py:338
  102.5 3.3 %collective-permute-start.1 = (f32[104,256]{1,0:T(8,128)S(1)}, f32[104,256]{1,0:T(8,128)S(1)}, u32[]{:S(2)}, u32[]{:S(2)}) collective-permute-start(f32[104,256]{1,0:T(8,128)S(1)} %add.35), channel_id=1, source_target_pairs={{0,4},{1,5},{2,6},{3,7},{4,0},{5,1},{6,2},{7,3},{8,12},{9,13},{10,... | collective-permute-start | bytes 319496 | tf_op jit(solution)/shard_map/ppermute | solution.py:338
  105.8 0.0 collective-permute-done.3
  105.8 1.5 %collective-permute-done.2 = f32[104,256]{1,0:T(8,128)S(1)} collective-permute-done((f32[104,256]{1,0:T(8,128)S(1)}, f32[104,256]{1,0:T(8,128)S(1)}, u32[]{:S(2)}, u32[]{:S(2)}) %collective-permute-start.2) | collective-permute-done | bytes 106528 | tf_op jit(solution)/shard_map/ppermute | solution.py:338
  107.4 3.1 %collective-permute-done.1 = f32[104,256]{1,0:T(8,128)S(1)} collective-permute-done((f32[104,256]{1,0:T(8,128)S(1)}, f32[104,256]{1,0:T(8,128)S(1)}, u32[]{:S(2)}, u32[]{:S(2)}) %collective-permute-start.1) | collective-permute-done | bytes 106528 | tf_op jit(solution)/shard_map/ppermute | solution.py:338
  110.6 1.1 collective-permute-start.6
  111.6 0.5 collective-permute-start.5
  112.1 4.9 %collective-permute-start.4 = (f32[104,256]{1,0:T(8,128)S(1)}, f32[104,256]{1,0:T(8,128)S(1)}, u32[]{:S(2)}, u32[]{:S(2)}) collective-permute-start(f32[104,256]{1,0:T(8,128)S(1)} %add_add_fusion.2), channel_id=1, source_target_pairs={{0,16},{1,17},{2,18},{3,19},{4,20},{5,21},{6,22},{7,23},{8,24},{9,... | collective-permute-start | bytes 319496 | tf_op jit(solution)/shard_map/ppermute | solution.py:338
  117.0 0.0 collective-permute-done.6
  117.0 0.9 collective-permute-done.5
  117.9 2.7 %collective-permute-done.4 = f32[104,256]{1,0:T(8,128)S(1)} collective-permute-done((f32[104,256]{1,0:T(8,128)S(1)}, f32[104,256]{1,0:T(8,128)S(1)}, u32[]{:S(2)}, u32[]{:S(2)}) %collective-permute-start.4) | collective-permute-done | bytes 106528 | tf_op jit(solution)/shard_map/ppermute | solution.py:338
  120.7 1.2 collective-permute-start.9
  121.9 1.2 collective-permute-start.8
  123.2 1.7 %collective-permute-start.7 = (f32[104,256]{1,0:T(8,128)S(1)}, f32[104,256]{1,0:T(8,128)S(1)}, u32[]{:S(2)}, u32[]{:S(2)}) collective-permute-start(f32[104,256]{1,0:T(8,128)S(1)} %add_add_fusion.1), channel_id=1, source_target_pairs={{0,64},{1,65},{2,66},{3,67},{4,68},{5,69},{6,70},{7,71},{8,72},{9,... | collective-permute-start | bytes 319496 | tf_op jit(solution)/shard_map/ppermute | solution.py:338
  124.9 0.3 collective-permute-done.9
  125.2 1.5 %collective-permute-done.8 = f32[104,256]{1,0:T(8,128)S(1)} collective-permute-done((f32[104,256]{1,0:T(8,128)S(1)}, f32[104,256]{1,0:T(8,128)S(1)}, u32[]{:S(2)}, u32[]{:S(2)}) %collective-permute-start.8) | collective-permute-done | bytes 106528 | tf_op jit(solution)/shard_map/ppermute | solution.py:338
  126.7 1.5 %collective-permute-done.7 = f32[104,256]{1,0:T(8,128)S(1)} collective-permute-done((f32[104,256]{1,0:T(8,128)S(1)}, f32[104,256]{1,0:T(8,128)S(1)}, u32[]{:S(2)}, u32[]{:S(2)}) %collective-permute-start.7) | collective-permute-done | bytes 106528 | tf_op jit(solution)/shard_map/ppermute | solution.py:338
  128.3 0.0 copy-start.3
  128.3 4.1 %collective-permute-start.10 = (f32[104,256]{1,0:T(8,128)S(1)}, f32[104,256]{1,0:T(8,128)S(1)}, u32[]{:S(2)}, u32[]{:S(2)}) collective-permute-start(f32[104,256]{1,0:T(8,128)S(1)} %add_add_fusion.mine_ref), channel_id=1, source_target_pairs={{0,1},{1,0},{2,3},{3,2},{4,5},{5,4},{6,7},{7,6},{8,9},{9,8},{10,11... | collective-permute-start | bytes 319496 | tf_op jit(solution)/shard_map/ppermute | solution.py:364
  132.4 1.0 collective-permute-done.10.other_ref
  133.3 0.0 copy-done.3
  133.3 0.0 copy-start.4
  133.3 0.6 copy-done.4
  133.9 13.7 %solve_and_apply.1 = bf16[8,2048,256]{2,1,0:T(8,128)(2,1)} custom-call(s32[1]{0:T(128)} %bitcast.core_ref, f32[104,256]{1,0:T(8,128)} %copy-done.3, f32[104,256]{1,0:T(8,128)} %copy-done.4, f32[8,2048]{1,0:T(8,128)} %mean_ref.1, bf16[8,2048,256]{2,1,0:T(8,128)(2,1)} %anom_ref.3), custom_call_target="tpu_custom_call" | custom-call | tf_op jit(solution)/shard_map/solve_and_apply/pallas_call | solution.py:311
  (5 shorter events, 0.1 us)
Async XLA Ops:
  11.1 60.0 %all-to-all-start = ((bf16[384,8,256]{2,1,0:T(8,128)(2,1)}), bf16[384,8,256]{2,1,0:T(8,128)(2,1)S(1)}, u32[]{:S(2)}, u32[]{:S(2)}) async-start(bf16[384,8,256]{2,1,0:T(8,128)(2,1)} %gather_sent.1), calls=%async_computation | async-start | bytes 3145728 | tf_op jit(solution)/shard_map/all_to_all | solution.py:349
  18.7 10.8 %copy-start.2 = (f32[32768]{0:T(1024)S(1)}, f32[32768]{0:T(1024)}, u32[]{:S(2)}) copy-start(f32[32768]{0:T(1024)} %param.11) | copy-start | bytes 393220
  18.7 11.6 %copy-start.1 = (f32[32768]{0:T(1024)S(1)}, f32[32768]{0:T(1024)}, u32[]{:S(2)}) copy-start(f32[32768]{0:T(1024)} %param.12) | copy-start | bytes 393220
  71.1 1.2 copy-start
  86.2 13.6 %collective-permute-start = (f32[104,256]{1,0:T(8,128)}, f32[104,256]{1,0:T(8,128)S(1)}, u32[]{:S(2)}, u32[]{:S(2)}) collective-permute-start(f32[104,256]{1,0:T(8,128)} %get-tuple-element.12), channel_id=1, source_target_pairs={{0,1},{1,0},{2,3},{3,2},{4,5},{5,4},{6,7},{7,6},{8,9},{9,8},{10,11... | collective-permute-start | bytes 319496 | tf_op jit(solution)/shard_map/ppermute | solution.py:361
  100.7 5.1 %collective-permute-start.3 = (f32[104,256]{1,0:T(8,128)S(1)}, f32[104,256]{1,0:T(8,128)S(1)}, u32[]{:S(2)}, u32[]{:S(2)}) collective-permute-start(f32[104,256]{1,0:T(8,128)S(1)} %add.35), channel_id=1, source_target_pairs={{0,6},{1,7},{2,0},{3,1},{4,2},{5,3},{6,4},{7,5},{8,14},{9,15},{10,... | collective-permute-start | bytes 319496 | tf_op jit(solution)/shard_map/ppermute | solution.py:338
  100.8 6.6 %collective-permute-start.2 = (f32[104,256]{1,0:T(8,128)S(1)}, f32[104,256]{1,0:T(8,128)S(1)}, u32[]{:S(2)}, u32[]{:S(2)}) collective-permute-start(f32[104,256]{1,0:T(8,128)S(1)} %add.35), channel_id=1, source_target_pairs={{0,2},{1,3},{2,4},{3,5},{4,6},{5,7},{6,0},{7,1},{8,10},{9,11},{10,... | collective-permute-start | bytes 319496 | tf_op jit(solution)/shard_map/ppermute | solution.py:338
  102.5 8.0 %collective-permute-start.1 = (f32[104,256]{1,0:T(8,128)S(1)}, f32[104,256]{1,0:T(8,128)S(1)}, u32[]{:S(2)}, u32[]{:S(2)}) collective-permute-start(f32[104,256]{1,0:T(8,128)S(1)} %add.35), channel_id=1, source_target_pairs={{0,4},{1,5},{2,6},{3,7},{4,0},{5,1},{6,2},{7,3},{8,12},{9,13},{10,... | collective-permute-start | bytes 319496 | tf_op jit(solution)/shard_map/ppermute | solution.py:338
  110.6 6.5 %collective-permute-start.6 = (f32[104,256]{1,0:T(8,128)S(1)}, f32[104,256]{1,0:T(8,128)S(1)}, u32[]{:S(2)}, u32[]{:S(2)}) collective-permute-start(f32[104,256]{1,0:T(8,128)S(1)} %add_add_fusion.2), channel_id=1, source_target_pairs={{0,24},{1,25},{2,26},{3,27},{4,28},{5,29},{6,30},{7,31},{8,0},{9,1... | collective-permute-start | bytes 319496 | tf_op jit(solution)/shard_map/ppermute | solution.py:338
  111.6 6.3 %collective-permute-start.5 = (f32[104,256]{1,0:T(8,128)S(1)}, f32[104,256]{1,0:T(8,128)S(1)}, u32[]{:S(2)}, u32[]{:S(2)}) collective-permute-start(f32[104,256]{1,0:T(8,128)S(1)} %add_add_fusion.2), channel_id=1, source_target_pairs={{0,8},{1,9},{2,10},{3,11},{4,12},{5,13},{6,14},{7,15},{8,16},{9,17... | collective-permute-start | bytes 319496 | tf_op jit(solution)/shard_map/ppermute | solution.py:338
  112.1 8.6 %collective-permute-start.4 = (f32[104,256]{1,0:T(8,128)S(1)}, f32[104,256]{1,0:T(8,128)S(1)}, u32[]{:S(2)}, u32[]{:S(2)}) collective-permute-start(f32[104,256]{1,0:T(8,128)S(1)} %add_add_fusion.2), channel_id=1, source_target_pairs={{0,16},{1,17},{2,18},{3,19},{4,20},{5,21},{6,22},{7,23},{8,24},{9,... | collective-permute-start | bytes 319496 | tf_op jit(solution)/shard_map/ppermute | solution.py:338
  120.7 4.5 %collective-permute-start.9 = (f32[104,256]{1,0:T(8,128)S(1)}, f32[104,256]{1,0:T(8,128)S(1)}, u32[]{:S(2)}, u32[]{:S(2)}) collective-permute-start(f32[104,256]{1,0:T(8,128)S(1)} %add_add_fusion.1), channel_id=1, source_target_pairs={{0,96},{1,97},{2,98},{3,99},{4,100},{5,101},{6,102},{7,103},{8,104... | collective-permute-start | bytes 319496 | tf_op jit(solution)/shard_map/ppermute | solution.py:338
  121.9 4.8 %collective-permute-start.8 = (f32[104,256]{1,0:T(8,128)S(1)}, f32[104,256]{1,0:T(8,128)S(1)}, u32[]{:S(2)}, u32[]{:S(2)}) collective-permute-start(f32[104,256]{1,0:T(8,128)S(1)} %add_add_fusion.1), channel_id=1, source_target_pairs={{0,32},{1,33},{2,34},{3,35},{4,36},{5,37},{6,38},{7,39},{8,40},{9,... | collective-permute-start | bytes 319496 | tf_op jit(solution)/shard_map/ppermute | solution.py:338
  123.2 5.1 %collective-permute-start.7 = (f32[104,256]{1,0:T(8,128)S(1)}, f32[104,256]{1,0:T(8,128)S(1)}, u32[]{:S(2)}, u32[]{:S(2)}) collective-permute-start(f32[104,256]{1,0:T(8,128)S(1)} %add_add_fusion.1), channel_id=1, source_target_pairs={{0,64},{1,65},{2,66},{3,67},{4,68},{5,69},{6,70},{7,71},{8,72},{9,... | collective-permute-start | bytes 319496 | tf_op jit(solution)/shard_map/ppermute | solution.py:338
  128.3 5.1 %copy-start.3 = (f32[104,256]{1,0:T(8,128)}, f32[104,256]{1,0:T(8,128)S(1)}, u32[]{:S(2)}) copy-start(f32[104,256]{1,0:T(8,128)S(1)} %add_add_fusion.mine_ref) | copy-start | bytes 319492
  128.3 5.0 %collective-permute-start.10 = (f32[104,256]{1,0:T(8,128)S(1)}, f32[104,256]{1,0:T(8,128)S(1)}, u32[]{:S(2)}, u32[]{:S(2)}) collective-permute-start(f32[104,256]{1,0:T(8,128)S(1)} %add_add_fusion.mine_ref), channel_id=1, source_target_pairs={{0,1},{1,0},{2,3},{3,2},{4,5},{5,4},{6,7},{7,6},{8,9},{9,8},{10,11... | collective-permute-start | bytes 319496 | tf_op jit(solution)/shard_map/ppermute | solution.py:364
  133.3 0.6 copy-start.4

commit v2 on v1

--- a/solution.py
+++ b/solution.py
@@ -10,8 +10,7 @@
 F32 = jnp.float32
 BF16 = jnp.bfloat16
 AXES = ("tile", "lev")
-VMEM_BYTES = 60 << 20
-GROUP = 16
+GROUP = 64
 CHUNK = 64
 PACK = 104
 
@@ -24,25 +23,38 @@
     return high, middle, low
 
 
-def send_kernel(send_ref, anom_ref, out_ref, level_ref, wide_ref, sems):
+def send_kernel(send_ref, anom_ref, out_ref, levels, wide, sems):
     lev_dev, col_dev, members = anom_ref.shape
-    slots = send_ref.shape[1]
+    slots = out_ref.shape[0]
     copies = [
-        pltpu.make_async_copy(anom_ref.at[v], level_ref.at[v], sems.at[v]) for v in range(lev_dev)
+        pltpu.make_async_copy(anom_ref.at[v], levels.at[v], sems.at[v]) for v in range(lev_dev)
     ]
     for copy in copies:
         copy.start()
-    listed = jnp.broadcast_to(send_ref[...].astype(F32), (8, slots)).T[:, 0:1]
-    lanes = lax.broadcasted_iota(jnp.int32, (slots, col_dev), 1).astype(F32)
-    chosen = jnp.where(lanes == listed, 1.0, 0.0).astype(BF16)
+    rows = 512
+
     for v in range(lev_dev):
         copies[v].wait()
-        rows = jnp.dot(chosen, level_ref[v], preferred_element_type=F32)
-        for h in range(members // 128):
-            wide_ref.at[h][pl.ds(v, slots, stride=lev_dev), :] = rows[:, h * 128 : (h + 1) * 128]
-    for h in range(members // 128):
-        half = wide_ref[h].reshape(slots, lev_dev, 128)
-        out_ref[:, :, h * 128 : (h + 1) * 128] = half.astype(BF16)
+
+        def spread(step, carried, v=v):
+            start = pl.multiple_of(step * rows, rows)
+            part = levels[v, pl.ds(start, rows), :].astype(F32)
+            for h in range(members // 128):
+                place = pl.ds(start * lev_dev + v, rows, stride=lev_dev)
+                wide.at[h][place, :] = part[:, h * 128 : (h + 1) * 128]
+            return carried
+
+        lax.fori_loop(0, col_dev // rows, spread, 0)
+
+    def pick(step, carried):
+        for i in range(32):
+            slot = step * 32 + i
+            place = pl.ds(pl.multiple_of(send_ref[0, slot] * lev_dev, lev_dev), lev_dev)
+            for h in range(members // 128):
+                out_ref[slot, :, h * 128 : (h + 1) * 128] = wide[h, place, :].astype(BF16)
+        return carried
+
+    lax.fori_loop(0, slots // 32, pick, 0)
 
 
 def gather_sent(send_cols, anomalies):
@@ -50,28 +62,37 @@
     slots = send_cols.shape[1]
     return pl.pallas_call(
         send_kernel,
-        in_specs=[pl.BlockSpec(memory_space=pltpu.VMEM), pl.BlockSpec(memory_space=pl.ANY)],
+        in_specs=[pl.BlockSpec(memory_space=pltpu.SMEM), pl.BlockSpec(memory_space=pl.ANY)],
         out_specs=pl.BlockSpec(memory_space=pltpu.VMEM),
         out_shape=jax.ShapeDtypeStruct((slots, lev_dev, members), BF16),
         scratch_shapes=[
             pltpu.VMEM((lev_dev, col_dev, members), BF16),
-            pltpu.VMEM((members // 128, slots * lev_dev, 128), F32),
+            pltpu.VMEM((members // 128, col_dev * lev_dev, 128), F32),
             pltpu.SemaphoreType.DMA((lev_dev,)),
         ],
-        compiler_params=pltpu.CompilerParams(vmem_limit_bytes=VMEM_BYTES),
+        compiler_params=pltpu.CompilerParams(vmem_limit_bytes=60 << 20),
         name="gather_sent",
     )(send_cols, anomalies)
 
 
-def prepare_kernel(count_ref, op_ref, rinv_ref, innov_ref, pair_ref, sums_ref, wide_ref):
+def prepare_kernel(
+    count_ref, op_ref, rinv_ref, innov_ref, pair_ref, sums_ref,
+    ops, expand, wide, folded, built, in_sems, out_sems,
+):
     blocks, width = op_ref.shape
     per_block = rinv_ref.shape[1]
     points = width // per_block
     tiles = width // 128
     count = count_ref[0]
-    spread_row = lax.broadcasted_iota(jnp.int32, (per_block, width), 0)
-    spread_lane = lax.broadcasted_iota(jnp.int32, (per_block, width), 1)
-    expand = jnp.where(spread_lane // points == spread_row, 1.0, 0.0).astype(BF16)
+    steps = blocks // CHUNK
+    loads = []
+    for k in range(steps):
+        part = pl.ds(k * CHUNK, CHUNK)
+        loads.append(pltpu.make_async_copy(op_ref.at[part], ops.at[part], in_sems.at[k]))
+        loads[k].start()
+    spread_row = lax.broadcasted_iota(jnp.int32, (2 * per_block, width), 0) % per_block
+    spread_lane = lax.broadcasted_iota(jnp.int32, (2 * per_block, width), 1) // points
+    expand[...] = jnp.where(spread_lane == spread_row, 1.0, 0.0).astype(BF16)
     live = lax.broadcasted_iota(jnp.int32, (blocks, per_block), 0) < count
     innov = innov_ref[...]
     squares = jnp.where(live, rinv_ref[...] * innov * innov, 0.0)
@@ -79,101 +100,143 @@
     total = jnp.full((1, 1), count * per_block, jnp.int32).astype(F32)
     lane = lax.broadcasted_iota(jnp.int32, (8, 256), 1)
     sums_ref[...] = jnp.where(lane == 0, numerator, jnp.where(lane == 1, total, 0.0))
-    low_half = lax.broadcasted_iota(jnp.int32, (1, 1, 128), 2) < points
-
-    def chunk(step, carried):
-        start = pl.multiple_of(step * CHUNK, CHUNK)
+    low_half = lax.broadcasted_iota(jnp.int32, (1, 128), 1) < points
+    extra_row = lax.broadcasted_iota(jnp.int32, (CHUNK // 2, 16, 128), 1)
+
+    def store(k):
+        part = pl.ds(k * (CHUNK // 2), CHUNK // 2)
+        return pltpu.make_async_copy(built.at[k % 2], pair_ref.at[part], out_sems.at[k % 2])
+
+    for k in range(steps):
+        start = k * CHUNK
         alive = start + lax.broadcasted_iota(jnp.int32, (CHUNK, per_block), 0) < count
-        weight = jnp.where(alive, jnp.sqrt(rinv_ref[pl.ds(start, CHUNK), :]), 0.0)
-        parts = split3(weight)
-        wide = jnp.dot(parts[0], expand, preferred_element_type=F32)
-        wide = wide + jnp.dot(parts[1], expand, preferred_element_type=F32)
-        wide = wide + jnp.dot(parts[2], expand, preferred_element_type=F32)
-        weighted = op_ref[pl.ds(start, CHUNK), :].astype(F32) * wide
-        for r in range(tiles):
-            wide_ref[pl.ds(r, CHUNK, stride=tiles), :] = weighted[:, r * 128 : (r + 1) * 128]
-        rows = wide_ref[...].reshape(CHUNK // 2, 2, tiles, 128)
-        first, second = rows[:, 0], rows[:, 1]
-        first_turned = pltpu.roll(first.reshape(-1, 128), 64, 1).reshape(first.shape)
-        second_turned = pltpu.roll(second.reshape(-1, 128), 64, 1).reshape(second.shape)
-        pieces = [
-            jnp.where(low_half, first, 0.0),
-            jnp.where(low_half, first_turned, 0.0),
-            jnp.where(low_half, 0.0, second_turned),
-            jnp.where(low_half, 0.0, second),
-        ]
-        out = pl.multiple_of(step * (CHUNK // 2), CHUNK // 2)
-        pair_ref[pl.ds(out, CHUNK // 2)] = jnp.concatenate(pieces, axis=1).astype(BF16)
-        return carried
-
-    lax.fori_loop(0, blocks // CHUNK, chunk, 0)
+        rinv = jnp.where(alive, rinv_ref[start : start + CHUNK, :], 0.0)
+        factors = jnp.concatenate([jnp.sqrt(rinv), rinv * innov_ref[start : start + CHUNK, :]], 0)
+        high, middle, _ = split3(factors)
+        both = jnp.concatenate([high, middle], axis=1)
+        loads[k].wait()
+        column = jnp.zeros((CHUNK, 128), F32)
+        for t in range(tiles // 2):
+            lanes = slice(t * 256, (t + 1) * 256)
+            spread = jnp.dot(both, expand[:, lanes], preferred_element_type=F32)
+            part = ops[start : start + CHUNK, lanes].astype(F32)
+            weighted = part * spread[:CHUNK]
+            pulled = part * spread[CHUNK:]
+            column = column + (pulled[:, :128] + pulled[:, 128:])
+            wide[pl.ds(2 * t, CHUNK, stride=tiles), :] = weighted[:, :128]
+            wide[pl.ds(2 * t + 1, CHUNK, stride=tiles), :] = weighted[:, 128:]
+        folded[...] = column + pltpu.roll(column, points, 1)
+        if k >= 2:
+            store(k - 2).wait()
+        slot = built.at[k % 2]
+        column = jnp.where(
+            low_half,
+            folded[pl.ds(0, CHUNK // 2, stride=2), :],
+            folded[pl.ds(1, CHUNK // 2, stride=2), :],
+        )
+        high, middle, low = [piece.astype(F32)[:, None, :] for piece in split3(column)]
+        extra = jnp.where(extra_row == 2, low, 0.0)
+        extra = jnp.where(extra_row == 1, middle, extra)
+        slot[:, 128:144, :] = jnp.where(extra_row == 0, high, extra).astype(BF16)
+
+        def pair_up(step, carried, slot=slot):
+            for i in range(8):
+                pair = step * 8 + i
+                place = pl.multiple_of(pair * 2 * tiles, 2 * tiles)
+                first = wide[pl.ds(place, tiles), :]
+                second = wide[pl.ds(place + tiles, tiles), :]
+                pieces = [
+                    jnp.where(low_half, first, 0.0),
+                    jnp.where(low_half, pltpu.roll(first, points, 1), 0.0),
+                    jnp.where(low_half, 0.0, pltpu.roll(second, points, 1)),
+                    jnp.where(low_half, 0.0, second),
+                ]
+                for q in range(4):
+                    slot[pair, q * tiles : (q + 1) * tiles, :] = pieces[q].astype(BF16)
+            return carried
+
+        lax.fori_loop(0, CHUNK // 16, pair_up, 0)
+        store(k).start()
+    store(steps - 2).wait()
+    store(steps - 1).wait()
 
 
 def prepare(obs_count, obs_op, rinv_blocks, innov_blocks):
-    blocks = obs_op.shape[0]
+    blocks, width = obs_op.shape
     vmem = pl.BlockSpec(memory_space=pltpu.VMEM)
+    anywhere = pl.BlockSpec(memory_space=pl.ANY)
     return pl.pallas_call(
         prepare_kernel,
-        in_specs=[pl.BlockSpec(memory_space=pltpu.SMEM), vmem, vmem, vmem],
-        out_specs=[vmem, vmem],
+        in_specs=[pl.BlockSpec(memory_space=pltpu.SMEM), anywhere, vmem, vmem],
+        out_specs=[anywhere, vmem],
         out_shape=[
-            jax.ShapeDtypeStruct((blocks // 2, 128, 128), BF16),
+            jax.ShapeDtypeStruct((blocks // 2, 144, 128), BF16),
             jax.ShapeDtypeStruct((8, 256), F32),
         ],
-        scratch_shapes=[pltpu.VMEM((CHUNK * 32, 128), F32)],
-        compiler_params=pltpu.CompilerParams(vmem_limit_bytes=VMEM_BYTES),
+        scratch_shapes=[
+            pltpu.VMEM((blocks, width), BF16),
+            pltpu.VMEM((128, width), BF16),
+            pltpu.VMEM((CHUNK * width // 128, 128), F32),
+            pltpu.VMEM((CHUNK, 128), F32),
+            pltpu.VMEM((2, CHUNK // 2, 144, 128), BF16),
+            pltpu.SemaphoreType.DMA((blocks // CHUNK,)),
+            pltpu.SemaphoreType.DMA((2,)),
+        ],
+        compiler_params=pltpu.CompilerParams(vmem_limit_bytes=60 << 20),
         name="prepare_operators",
     )(obs_count, obs_op, rinv_blocks, innov_blocks)
 
 
 def gram_kernel(
-    cols_ref, count_ref, core_ref, own_ref, remote_ref, pair_ref, innov_ref, sums_ref,
-    keep_ref, give_ref, table, pairs, support, scaled, total, sems,
+    cols_ref, count_ref, core_ref, own_ref, remote_ref, pair_ref, sums_ref,
+    keep_ref, give_ref, table, pairs, support, scaled, total, pulled, sems,
 ):
     own_cols = own_ref.shape[0]
     n_pairs = pair_ref.shape[0]
-    chunk_pairs = CHUNK // 2
-    chunks = n_pairs // chunk_pairs
-    own = pltpu.make_async_copy(own_ref, table.at[pl.ds(0, own_cols)], sems.at[chunks])
+    group_pairs = GROUP // 2
+    most = n_pairs // group_pairs
+    own = pltpu.make_async_copy(own_ref, table.at[pl.ds(0, own_cols)], sems.at[most])
     remote = pltpu.make_async_copy(
-        remote_ref, table.at[pl.ds(own_cols, remote_ref.shape[0])], sems.at[chunks + 1]
+        remote_ref, table.at[pl.ds(own_cols, remote_ref.shape[0])], sems.at[most + 1]
     )
     own.start()
     remote.start()
-    fetches = []
-    for k in range(chunks):
-        part = pl.ds(k * chunk_pairs, chunk_pairs)
-        fetches.append(pltpu.make_async_copy(pair_ref.at[part], pairs.at[part], sems.at[k]))
-        fetches[k].start()
+    groups = (count_ref[0] + GROUP - 1) // GROUP
+
+    def fetch(g):
+        part = pl.ds(g * group_pairs, group_pairs)
+        return pltpu.make_async_copy(pair_ref.at[part], pairs.at[part], sems.at[g])
+
+    def begin(g, carried):
+        fetch(g).start()
+        return carried
+
+    lax.fori_loop(0, groups, begin, 0)
     total[...] = jnp.zeros_like(total)
-    groups = (count_ref[0] + GROUP - 1) // GROUP
+    pulled[...] = jnp.zeros_like(pulled)
     own.wait()
     remote.wait()
 
     def step(g, carried):
+        fetch(g).wait()
         for i in range(GROUP * 8):
             support[i] = table[cols_ref[g * (GROUP * 8) + i]]
-        for j in range(GROUP // 2):
+        extra = jnp.zeros((16, 256), F32)
+        for j in range(group_pairs):
             points = support[j * 16 : (j + 1) * 16].reshape(128, 256)
-            images = jnp.dot(pairs[g * (GROUP // 2) + j], points, preferred_element_type=F32)
-            scaled[j * 128 : (j + 1) * 128, :] = images.astype(BF16)
+            images = jnp.dot(pairs[g * group_pairs + j], points, preferred_element_type=F32)
+            scaled[j * 128 : (j + 1) * 128, :] = images[:128].astype(BF16)
+            extra = extra + images[128:]
+        pulled[...] += extra
         rows = scaled[...]
-        parts = split3(innov_ref[pl.ds(g, 1), :])
-        row_index = lax.broadcasted_iota(jnp.int32, (16, GROUP * 64), 0)
-        extra = jnp.where(row_index == 0, parts[0].astype(F32), 0.0)
-        extra = jnp.where(row_index == 1, parts[1].astype(F32), extra)
-        extra = jnp.where(row_index == 2, parts[2].astype(F32), extra).astype(BF16)
-        left = jnp.concatenate([rows.T, extra], axis=0)
-        total[...] += jnp.dot(left, rows, preferred_element_type=F32)
+        total[...] += lax.dot_general(
+            rows, rows, (((0,), (0,)), ((), ())), preferred_element_type=F32
+        )
         return carried
 
-    per_chunk = CHUNK // GROUP
-    for k in range(chunks):
-        fetches[k].wait()
-        last = jnp.minimum(groups, (k + 1) * per_chunk)
-        lax.fori_loop(k * per_chunk, jnp.maximum(last, k * per_chunk), step, 0)
-
-    projection = total[256:257, :] + total[257:258, :] + total[258:259, :]
+    lax.fori_loop(0, groups, step, 0)
+
+    projection = pulled[0:1, :] + pulled[1:2, :] + pulled[2:3, :]
     row = lax.broadcasted_iota(jnp.int32, (8, 256), 0)
     ending = jnp.where(row == 0, projection, jnp.where(row == 1, sums_ref[...], 0.0))
     zeros = jnp.zeros((8, 256), F32)
@@ -193,15 +256,15 @@
         give_ref[...] = first
 
 
-def gram_sums(obs_cols, obs_count, core, own, remote, pairs, innov_rows, sums):
+def gram_sums(obs_cols, obs_count, core, own, remote, pairs, sums):
     vmem = pl.BlockSpec(memory_space=pltpu.VMEM)
     smem = pl.BlockSpec(memory_space=pltpu.SMEM)
     anywhere = pl.BlockSpec(memory_space=pl.ANY)
     half = jax.ShapeDtypeStruct((PACK, 256), F32)
-    chunks = pairs.shape[0] // (CHUNK // 2)
+    most = pairs.shape[0] // (GROUP // 2)
     return pl.pallas_call(
         gram_kernel,
-        in_specs=[smem, smem, smem, anywhere, anywhere, anywhere, vmem, vmem],
+        in_specs=[smem, smem, smem, anywhere, anywhere, anywhere, vmem],
         out_specs=[vmem, vmem],
         out_shape=[half, half],
         scratch_shapes=[
@@ -209,12 +272,13 @@
             pltpu.VMEM(pairs.shape, BF16),
             pltpu.VMEM((GROUP * 8, 8, 256), BF16),
             pltpu.VMEM((GROUP * 64, 256), BF16),
-            pltpu.VMEM((272, 256), F32),
-            pltpu.SemaphoreType.DMA((chunks + 2,)),
+            pltpu.VMEM((256, 256), F32),
+            pltpu.VMEM((16, 256), F32),
+            pltpu.SemaphoreType.DMA((most + 2,)),
         ],
-        compiler_params=pltpu.CompilerParams(vmem_limit_bytes=VMEM_BYTES),
+        compiler_params=pltpu.CompilerParams(vmem_limit_bytes=56 << 20),
         name="gram_sums",
-    )(obs_cols, obs_count, core, own, remote, pairs, innov_rows, sums)
+    )(obs_cols, obs_count, core, own, remote, pairs, sums)
 
 
 def dot3(left, right):
@@ -321,7 +385,7 @@
             pltpu.SemaphoreType.DMA((lev_dev,)),
             pltpu.SemaphoreType.DMA((lev_dev,)),
         ],
-        compiler_params=pltpu.CompilerParams(vmem_limit_bytes=VMEM_BYTES),
+        compiler_params=pltpu.CompilerParams(vmem_limit_bytes=58 << 20),
         name="solve_and_apply",
     )(core, mine, other, mean_state, anomalies)
 
@@ -352,12 +416,7 @@
     rinv_blocks = obs_rinv.reshape(blocks, per_block)
     innov_blocks = innovations.reshape(blocks, per_block)
     pairs, sums = prepare(obs_count, obs_op, rinv_blocks, innov_blocks)
-    weighted = jnp.sqrt(rinv_blocks) * innov_blocks
-    weighted = jnp.where(jnp.arange(blocks)[:, None] < obs_count[0], weighted, 0.0)
-    weighted = weighted.reshape(blocks, per_block // 2, 2).swapaxes(1, 2)
-    innov_rows = weighted.reshape(blocks // GROUP, GROUP * per_block)
-
-    keep, give = gram_sums(obs_cols, obs_count, core, own, remote, pairs, innov_rows, sums)
+    keep, give = gram_sums(obs_cols, obs_count, core, own, remote, pairs, sums)
     value = keep + lax.ppermute(give, AXES, [(d, d ^ 1) for d in range(devices)])
     for stride in (2, 8, 32):
         value = sum_over(value, devices, stride)

time: 149 us -> 117 us (0.79)
  local copies, waits for them, and re-layouts: 30.6 us -> 13.5 us
  other arithmetic: 7.31 us -> 0.99 us
  starting transfers between devices: 39.9 us -> 34 us
  Pallas kernels: 55.3 us -> 50.6 us
  waiting for transfers between devices: 13.8 us -> 16.3 us
    mul x1 -> x0, local copies, waits for them, and re-layouts: 9.76 us -> none  [per_device(): weighted = jnp.sqrt(rinv_blocks) * innov_blocks]
    ppermute x1, starting transfers between devices: 12.5 us -> 4.16 us  [per_device(): lax.ppermute(give, AXES, [(d, d ^ 1) for d in range(devices)])]
    transpose x1 -> x0, other arithmetic: 6.28 us -> none  [per_device(): weighted = weighted.reshape(blocks, per_block // 2, 2).swapaxes(1, 2)]
    transpose x1 -> x0, local copies, waits for them, and re-layouts: 5.88 us -> none  [per_device(): weighted = weighted.reshape(blocks, per_block // 2, 2).swapaxes(1, 2)]
    pallas_call x1, Pallas kernels: 11 us -> 8.26 us  [gather_sent(): pl.pallas_call(send_kernel, in_specs=[pl.BlockSpec(memory_space=pltpu.SME...]
    ppermute x9, waiting for transfers between devices: 11.6 us -> 14.2 us  [sum_over(): lax.ppermute(value, AXES, turns(devices, stride, d))]
    ppermute x9, starting transfers between devices: 15.8 us -> 18.3 us  [sum_over(): lax.ppermute(value, AXES, turns(devices, stride, d))]
    pallas_call x1, Pallas kernels: 13.8 us -> 12.1 us  [gram_sums(): pl.pallas_call(gram_kernel, in_specs=[smem, smem, smem, anywhere, anywher...]
  transfers between devices with their start and end apart: 12 -> 12, of which waited for: 9 -> 9; matrix products, arithmetic and copies ran while one was open for 24% -> 10% of each run, Pallas kernels for 11% -> 14%
where the time goes in v2:
time: 117 us; the launch traced here: 116 us
  Pallas kernels  50.6 us (43%)
  starting transfers between devices  34 us (29%)
  waiting for transfers between devices  16.3 us (14%)
  local copies, waits for them, and re-layouts  13.5 us (12%)
    ppermute x9, starting transfers between devices, sum_over(): lax.ppermute(value, AXES, turns(devices, stride, d))  18.3 us
    pallas_call x1, Pallas kernels, prepare(): pl.pallas_call(prepare_kernel, in_specs=[pl.BlockSpec(memory_space=pltpu....  16.8 us
    ppermute x9, waiting for transfers between devices, sum_over(): lax.ppermute(value, AXES, turns(devices, stride, d))  14.2 us
    pallas_call x1, Pallas kernels, solve_and_apply(): pl.pallas_call(apply_kernel, in_specs=[pl.BlockSpec(memory_space=pltpu.SM...  13.5 us
    pallas_call x1, Pallas kernels, gram_sums(): pl.pallas_call(gram_kernel, in_specs=[smem, smem, smem, anywhere, anywher...  12.1 us
    unnamed x11, local copies, waits for them, and re-layouts  11.9 us
    pallas_call x1, Pallas kernels, gather_sent(): pl.pallas_call(send_kernel, in_specs=[pl.BlockSpec(memory_space=pltpu.SME...  8.26 us
    all_to_all x1, starting transfers between devices, per_device(): lax.all_to_all(outgoing, 'tile', split_axis=0, concat_axis=0, tiled=True)  7.6 us
  transfers between devices with their start and end apart: 12, of which 9 were waited for; matrix products, arithmetic and copies ran while one was open for 10% of the time, Pallas kernels for 14%

profile of v2, /device:TPU:1, one launch (start us, length us, event | category | flops | bytes accessed | tf_op | source)
XLA Modules:
  0.0 116.4 jit_solution(74986537121688646)
XLA Ops:
  0.0 8.3 %gather_sent.1 = bf16[384,8,256]{2,1,0:T(8,128)(2,1)} custom-call(s32[1,384]{1,0:T(1,128)} %send_ref.1, bf16[8,2048,256]{2,1,0:T(8,128)(2,1)} %anom_ref.3), custom_call_target="tpu_custom_call" | custom-call | tf_op jit(solution)/shard_map/gather_sent/pallas_call | solution.py:63
  8.3 7.6 %all-to-all-start = ((bf16[384,8,256]{2,1,0:T(8,128)(2,1)}), bf16[384,8,256]{2,1,0:T(8,128)(2,1)S(1)}, u32[]{:S(2)}, u32[]{:S(2)}) async-start(bf16[384,8,256]{2,1,0:T(8,128)(2,1)} %gather_sent.1), calls=%async_computation | async-start | bytes 3145728 | tf_op jit(solution)/shard_map/all_to_all | solution.py:413
  15.9 0.0 copy-start.2
  15.9 0.0 copy-start.3
  15.9 10.1 %copy.12 = bf16[8,2048,256]{2,0,1:T(8,128)(2,1)} copy(bf16[8,2048,256]{2,1,0:T(8,128)(2,1)} %anom_ref.3) | data formatting | bytes 16777216 | tf_op args[0]
  26.7 0.0 copy-done.2
  26.7 0.8 reshape.11.innov_ref
  27.5 0.0 copy-done.3
  27.5 0.8 reshape.10.rinv_ref
  28.3 16.8 %prepare_operators.1 = (bf16[256,144,128]{2,1,0:T(8,128)(2,1)}, f32[8,256]{1,0:T(8,128)}) custom-call(s32[1]{0:T(128)S(6)} %copy.13.count_ref, bf16[512,4096]{1,0:T(8,128)(2,1)} %op_ref.1, f32[512,64]{1,0:T(8,128)} %reshape.10.rinv_ref, f32[512,64]{1,0:T(8,128)} %reshape.11.innov_ref), custom_call_target="tpu_custom_call" | custom-call | tf_op jit(solution)/shard_map/prepare_operators/pallas_call | solution.py:168
  45.1 0.0 all-to-all-done.remote_ref
  45.1 0.0 copy-start
  45.1 1.1 copy-done
  46.2 12.1 %gram_sums.1 = (f32[104,256]{1,0:T(8,128)}, f32[104,256]{1,0:T(8,128)}) custom-call(s32[4096]{0:T(1024)} %cols_ref.1, s32[1]{0:T(128)S(6)} %copy.13.count_ref, s32[1]{0:T(128)} %bitcast.core_ref, bf16[2048,8,256]{2,1,0:T(8,128)(2,1)} %bitcast.4, bf16[384,8,256]{2,1,0:T(8,128)(2,1)} %copy-done, bf16[256,144,128]{2,1,0:T(8,128)(2,1)} %get-tuple-element.9.pair_ref, ...), custom_call_target="tpu_custom_call" | custom-call | tf_op jit(solution)/shard_map/gram_sums/pallas_call | solution.py:265
  58.3 4.2 %collective-permute-start = (f32[104,256]{1,0:T(8,128)}, f32[104,256]{1,0:T(8,128)S(1)}, u32[]{:S(2)}, u32[]{:S(2)}) collective-permute-start(f32[104,256]{1,0:T(8,128)} %get-tuple-element.12), channel_id=1, source_target_pairs={{0,1},{1,0},{2,3},{3,2},{4,5},{5,4},{6,7},{7,6},{8,9},{9,8},{10,11... | collective-permute-start | bytes 319496 | tf_op jit(solution)/shard_map/ppermute | solution.py:420
  62.5 1.2 %collective-permute-done = f32[104,256]{1,0:T(8,128)S(1)} collective-permute-done((f32[104,256]{1,0:T(8,128)}, f32[104,256]{1,0:T(8,128)S(1)}, u32[]{:S(2)}, u32[]{:S(2)}) %collective-permute-start) | collective-permute-done | bytes 106528 | tf_op jit(solution)/shard_map/ppermute | solution.py:420
  63.7 0.9 add.35
  64.6 0.7 collective-permute-start.3
  65.3 0.8 collective-permute-start.2
  66.1 6.1 %collective-permute-start.1 = (f32[104,256]{1,0:T(8,128)S(1)}, f32[104,256]{1,0:T(8,128)S(1)}, u32[]{:S(2)}, u32[]{:S(2)}) collective-permute-start(f32[104,256]{1,0:T(8,128)S(1)} %add.35), channel_id=1, source_target_pairs={{0,4},{1,5},{2,6},{3,7},{4,0},{5,1},{6,2},{7,3},{8,12},{9,13},{10,... | collective-permute-start | bytes 319496 | tf_op jit(solution)/shard_map/ppermute | solution.py:402
  72.3 0.0 collective-permute-done.3
  72.3 1.8 %collective-permute-done.2 = f32[104,256]{1,0:T(8,128)S(1)} collective-permute-done((f32[104,256]{1,0:T(8,128)S(1)}, f32[104,256]{1,0:T(8,128)S(1)}, u32[]{:S(2)}, u32[]{:S(2)}) %collective-permute-start.2) | collective-permute-done | bytes 106528 | tf_op jit(solution)/shard_map/ppermute | solution.py:402
  74.0 3.1 %collective-permute-done.1 = f32[104,256]{1,0:T(8,128)S(1)} collective-permute-done((f32[104,256]{1,0:T(8,128)S(1)}, f32[104,256]{1,0:T(8,128)S(1)}, u32[]{:S(2)}, u32[]{:S(2)}) %collective-permute-start.1) | collective-permute-done | bytes 106528 | tf_op jit(solution)/shard_map/ppermute | solution.py:402
  77.2 3.3 %collective-permute-start.6 = (f32[104,256]{1,0:T(8,128)S(1)}, f32[104,256]{1,0:T(8,128)S(1)}, u32[]{:S(2)}, u32[]{:S(2)}) collective-permute-start(f32[104,256]{1,0:T(8,128)S(1)} %add_add_fusion.2), channel_id=1, source_target_pairs={{0,24},{1,25},{2,26},{3,27},{4,28},{5,29},{6,30},{7,31},{8,0},{9,1... | collective-permute-start | bytes 319496 | tf_op jit(solution)/shard_map/ppermute | solution.py:402
  80.5 0.0 collective-permute-start.5
  80.5 1.3 %collective-permute-start.4 = (f32[104,256]{1,0:T(8,128)S(1)}, f32[104,256]{1,0:T(8,128)S(1)}, u32[]{:S(2)}, u32[]{:S(2)}) collective-permute-start(f32[104,256]{1,0:T(8,128)S(1)} %add_add_fusion.2), channel_id=1, source_target_pairs={{0,16},{1,17},{2,18},{3,19},{4,20},{5,21},{6,22},{7,23},{8,24},{9,... | collective-permute-start | bytes 319496 | tf_op jit(solution)/shard_map/ppermute | solution.py:402
  81.8 0.5 collective-permute-done.6
  82.2 4.1 %collective-permute-done.5 = f32[104,256]{1,0:T(8,128)S(1)} collective-permute-done((f32[104,256]{1,0:T(8,128)S(1)}, f32[104,256]{1,0:T(8,128)S(1)}, u32[]{:S(2)}, u32[]{:S(2)}) %collective-permute-start.5) | collective-permute-done | bytes 106528 | tf_op jit(solution)/shard_map/ppermute | solution.py:402
  86.4 0.1 collective-permute-done.4
  86.5 4.8 %collective-permute-start.9 = (f32[104,256]{1,0:T(8,128)S(1)}, f32[104,256]{1,0:T(8,128)S(1)}, u32[]{:S(2)}, u32[]{:S(2)}) collective-permute-start(f32[104,256]{1,0:T(8,128)S(1)} %add_add_fusion.1), channel_id=1, source_target_pairs={{0,96},{1,97},{2,98},{3,99},{4,100},{5,101},{6,102},{7,103},{8,104... | collective-permute-start | bytes 319496 | tf_op jit(solution)/shard_map/ppermute | solution.py:402
  91.3 0.0 collective-permute-start.8
  91.3 1.3 %collective-permute-start.7 = (f32[104,256]{1,0:T(8,128)S(1)}, f32[104,256]{1,0:T(8,128)S(1)}, u32[]{:S(2)}, u32[]{:S(2)}) collective-permute-start(f32[104,256]{1,0:T(8,128)S(1)} %add_add_fusion.1), channel_id=1, source_target_pairs={{0,64},{1,65},{2,66},{3,67},{4,68},{5,69},{6,70},{7,71},{8,72},{9,... | collective-permute-start | bytes 319496 | tf_op jit(solution)/shard_map/ppermute | solution.py:402
  92.5 0.5 collective-permute-done.9
  93.0 4.2 %collective-permute-done.8 = f32[104,256]{1,0:T(8,128)S(1)} collective-permute-done((f32[104,256]{1,0:T(8,128)S(1)}, f32[104,256]{1,0:T(8,128)S(1)}, u32[]{:S(2)}, u32[]{:S(2)}) %collective-permute-start.8) | collective-permute-done | bytes 106528 | tf_op jit(solution)/shard_map/ppermute | solution.py:402
  97.2 0.0 collective-permute-done.7
  97.2 0.0 copy-start.1
  97.2 3.9 %collective-permute-start.10 = (f32[104,256]{1,0:T(8,128)S(1)}, f32[104,256]{1,0:T(8,128)S(1)}, u32[]{:S(2)}, u32[]{:S(2)}) collective-permute-start(f32[104,256]{1,0:T(8,128)S(1)} %add_add_fusion.mine_ref), channel_id=1, source_target_pairs={{0,1},{1,0},{2,3},{3,2},{4,5},{5,4},{6,7},{7,6},{8,9},{9,8},{10,11... | collective-permute-start | bytes 319496 | tf_op jit(solution)/shard_map/ppermute | solution.py:423
  101.1 1.0 collective-permute-done.10.other_ref
  102.1 0.0 copy-done.1
  102.1 0.0 copy-start.4
  102.1 0.6 copy-done.4
  102.7 13.5 %solve_and_apply.1 = bf16[8,2048,256]{2,1,0:T(8,128)(2,1)} custom-call(s32[1]{0:T(128)} %bitcast.core_ref, f32[104,256]{1,0:T(8,128)} %copy-done.1, f32[104,256]{1,0:T(8,128)} %copy-done.4, f32[8,2048]{1,0:T(8,128)} %mean_ref.1, bf16[8,2048,256]{2,1,0:T(8,128)(2,1)} %anom_ref.3), custom_call_target="tpu_custom_call" | custom-call | tf_op jit(solution)/shard_map/solve_and_apply/pallas_call | solution.py:375
  (3 shorter events, 0.1 us)
Async XLA Ops:
  8.3 36.8 %all-to-all-start = ((bf16[384,8,256]{2,1,0:T(8,128)(2,1)}), bf16[384,8,256]{2,1,0:T(8,128)(2,1)S(1)}, u32[]{:S(2)}, u32[]{:S(2)}) async-start(bf16[384,8,256]{2,1,0:T(8,128)(2,1)} %gather_sent.1), calls=%async_computation | async-start | bytes 3145728 | tf_op jit(solution)/shard_map/all_to_all | solution.py:413
  15.9 10.8 %copy-start.2 = (f32[32768]{0:T(1024)S(1)}, f32[32768]{0:T(1024)}, u32[]{:S(2)}) copy-start(f32[32768]{0:T(1024)} %param.11) | copy-start | bytes 393220
  15.9 11.6 %copy-start.3 = (f32[32768]{0:T(1024)S(1)}, f32[32768]{0:T(1024)}, u32[]{:S(2)}) copy-start(f32[32768]{0:T(1024)} %param.12) | copy-start | bytes 393220
  45.1 1.1 copy-start
  58.3 5.3 %collective-permute-start = (f32[104,256]{1,0:T(8,128)}, f32[104,256]{1,0:T(8,128)S(1)}, u32[]{:S(2)}, u32[]{:S(2)}) collective-permute-start(f32[104,256]{1,0:T(8,128)} %get-tuple-element.12), channel_id=1, source_target_pairs={{0,1},{1,0},{2,3},{3,2},{4,5},{5,4},{6,7},{7,6},{8,9},{9,8},{10,11... | collective-permute-start | bytes 319496 | tf_op jit(solution)/shard_map/ppermute | solution.py:420
  64.6 7.7 %collective-permute-start.3 = (f32[104,256]{1,0:T(8,128)S(1)}, f32[104,256]{1,0:T(8,128)S(1)}, u32[]{:S(2)}, u32[]{:S(2)}) collective-permute-start(f32[104,256]{1,0:T(8,128)S(1)} %add.35), channel_id=1, source_target_pairs={{0,6},{1,7},{2,0},{3,1},{4,2},{5,3},{6,4},{7,5},{8,14},{9,15},{10,... | collective-permute-start | bytes 319496 | tf_op jit(solution)/shard_map/ppermute | solution.py:402
  65.3 8.8 %collective-permute-start.2 = (f32[104,256]{1,0:T(8,128)S(1)}, f32[104,256]{1,0:T(8,128)S(1)}, u32[]{:S(2)}, u32[]{:S(2)}) collective-permute-start(f32[104,256]{1,0:T(8,128)S(1)} %add.35), channel_id=1, source_target_pairs={{0,2},{1,3},{2,4},{3,5},{4,6},{5,7},{6,0},{7,1},{8,10},{9,11},{10,... | collective-permute-start | bytes 319496 | tf_op jit(solution)/shard_map/ppermute | solution.py:402
  66.1 11.1 %collective-permute-start.1 = (f32[104,256]{1,0:T(8,128)S(1)}, f32[104,256]{1,0:T(8,128)S(1)}, u32[]{:S(2)}, u32[]{:S(2)}) collective-permute-start(f32[104,256]{1,0:T(8,128)S(1)} %add.35), channel_id=1, source_target_pairs={{0,4},{1,5},{2,6},{3,7},{4,0},{5,1},{6,2},{7,3},{8,12},{9,13},{10,... | collective-permute-start | bytes 319496 | tf_op jit(solution)/shard_map/ppermute | solution.py:402
  77.2 5.0 %collective-permute-start.6 = (f32[104,256]{1,0:T(8,128)S(1)}, f32[104,256]{1,0:T(8,128)S(1)}, u32[]{:S(2)}, u32[]{:S(2)}) collective-permute-start(f32[104,256]{1,0:T(8,128)S(1)} %add_add_fusion.2), channel_id=1, source_target_pairs={{0,24},{1,25},{2,26},{3,27},{4,28},{5,29},{6,30},{7,31},{8,0},{9,1... | collective-permute-start | bytes 319496 | tf_op jit(solution)/shard_map/ppermute | solution.py:402
  80.5 5.9 %collective-permute-start.5 = (f32[104,256]{1,0:T(8,128)S(1)}, f32[104,256]{1,0:T(8,128)S(1)}, u32[]{:S(2)}, u32[]{:S(2)}) collective-permute-start(f32[104,256]{1,0:T(8,128)S(1)} %add_add_fusion.2), channel_id=1, source_target_pairs={{0,8},{1,9},{2,10},{3,11},{4,12},{5,13},{6,14},{7,15},{8,16},{9,17... | collective-permute-start | bytes 319496 | tf_op jit(solution)/shard_map/ppermute | solution.py:402
  80.5 5.9 %collective-permute-start.4 = (f32[104,256]{1,0:T(8,128)S(1)}, f32[104,256]{1,0:T(8,128)S(1)}, u32[]{:S(2)}, u32[]{:S(2)}) collective-permute-start(f32[104,256]{1,0:T(8,128)S(1)} %add_add_fusion.2), channel_id=1, source_target_pairs={{0,16},{1,17},{2,18},{3,19},{4,20},{5,21},{6,22},{7,23},{8,24},{9,... | collective-permute-start | bytes 319496 | tf_op jit(solution)/shard_map/ppermute | solution.py:402
  86.5 6.5 %collective-permute-start.9 = (f32[104,256]{1,0:T(8,128)S(1)}, f32[104,256]{1,0:T(8,128)S(1)}, u32[]{:S(2)}, u32[]{:S(2)}) collective-permute-start(f32[104,256]{1,0:T(8,128)S(1)} %add_add_fusion.1), channel_id=1, source_target_pairs={{0,96},{1,97},{2,98},{3,99},{4,100},{5,101},{6,102},{7,103},{8,104... | collective-permute-start | bytes 319496 | tf_op jit(solution)/shard_map/ppermute | solution.py:402
  91.3 5.9 %collective-permute-start.8 = (f32[104,256]{1,0:T(8,128)S(1)}, f32[104,256]{1,0:T(8,128)S(1)}, u32[]{:S(2)}, u32[]{:S(2)}) collective-permute-start(f32[104,256]{1,0:T(8,128)S(1)} %add_add_fusion.1), channel_id=1, source_target_pairs={{0,32},{1,33},{2,34},{3,35},{4,36},{5,37},{6,38},{7,39},{8,40},{9,... | collective-permute-start | bytes 319496 | tf_op jit(solution)/shard_map/ppermute | solution.py:402
  91.3 5.9 %collective-permute-start.7 = (f32[104,256]{1,0:T(8,128)S(1)}, f32[104,256]{1,0:T(8,128)S(1)}, u32[]{:S(2)}, u32[]{:S(2)}) collective-permute-start(f32[104,256]{1,0:T(8,128)S(1)} %add_add_fusion.1), channel_id=1, source_target_pairs={{0,64},{1,65},{2,66},{3,67},{4,68},{5,69},{6,70},{7,71},{8,72},{9,... | collective-permute-start | bytes 319496 | tf_op jit(solution)/shard_map/ppermute | solution.py:402
  97.2 4.9 %copy-start.1 = (f32[104,256]{1,0:T(8,128)}, f32[104,256]{1,0:T(8,128)S(1)}, u32[]{:S(2)}) copy-start(f32[104,256]{1,0:T(8,128)S(1)} %add_add_fusion.mine_ref) | copy-start | bytes 319492
  97.2 4.9 %collective-permute-start.10 = (f32[104,256]{1,0:T(8,128)S(1)}, f32[104,256]{1,0:T(8,128)S(1)}, u32[]{:S(2)}, u32[]{:S(2)}) collective-permute-start(f32[104,256]{1,0:T(8,128)S(1)} %add_add_fusion.mine_ref), channel_id=1, source_target_pairs={{0,1},{1,0},{2,3},{3,2},{4,5},{5,4},{6,7},{7,6},{8,9},{9,8},{10,11... | collective-permute-start | bytes 319496 | tf_op jit(solution)/shard_map/ppermute | solution.py:423
  102.1 0.6 copy-start.4

commit v3 on v2

--- a/solution.py
+++ b/solution.py
@@ -10,7 +10,7 @@
 F32 = jnp.float32
 BF16 = jnp.bfloat16
 AXES = ("tile", "lev")
-GROUP = 64
+GROUP = 128
 CHUNK = 64
 PACK = 104
 
@@ -76,8 +76,8 @@
 
 
 def prepare_kernel(
-    count_ref, op_ref, rinv_ref, innov_ref, pair_ref, sums_ref,
-    ops, expand, wide, folded, built, in_sems, out_sems,
+    count_ref, op_ref, rinv_ref, innov_ref, anom_ref, pair_ref, sums_ref, own_ref,
+    ops, levels, expand, wide, folded, built, turned, in_sems, anom_sems, out_sems, own_sems,
 ):
     blocks, width = op_ref.shape
     per_block = rinv_ref.shape[1]
@@ -90,9 +90,21 @@
         part = pl.ds(k * CHUNK, CHUNK)
         loads.append(pltpu.make_async_copy(op_ref.at[part], ops.at[part], in_sems.at[k]))
         loads[k].start()
-    spread_row = lax.broadcasted_iota(jnp.int32, (2 * per_block, width), 0) % per_block
-    spread_lane = lax.broadcasted_iota(jnp.int32, (2 * per_block, width), 1) // points
-    expand[...] = jnp.where(spread_lane == spread_row, 1.0, 0.0).astype(BF16)
+    col_dev = anom_ref.shape[1]
+    some = col_dev // steps
+    reads = []
+    for k in range(steps):
+        part = pl.ds(k * some, some)
+        reads.append(
+            pltpu.make_async_copy(anom_ref.at[:, part], levels.at[:, part], anom_sems.at[k])
+        )
+        reads[k].start()
+    spread_row = lax.broadcasted_iota(jnp.int32, (2 * per_block, 256), 0)
+    spread_row = jnp.where(spread_row < per_block, spread_row, spread_row - per_block) * points
+    ahead = lax.broadcasted_iota(jnp.int32, (2 * per_block, 256), 1) - spread_row
+    for t in range(tiles // 2):
+        inside = jnp.logical_and(ahead >= -t * 256, ahead < points - t * 256)
+        expand[:, t * 256 : (t + 1) * 256] = jnp.where(inside, 1.0, 0.0).astype(BF16)
     live = lax.broadcasted_iota(jnp.int32, (blocks, per_block), 0) < count
     innov = innov_ref[...]
     squares = jnp.where(live, rinv_ref[...] * innov * innov, 0.0)
@@ -106,6 +118,10 @@
     def store(k):
         part = pl.ds(k * (CHUNK // 2), CHUNK // 2)
         return pltpu.make_async_copy(built.at[k % 2], pair_ref.at[part], out_sems.at[k % 2])
+
+    def store_own(k):
+        part = pl.ds(k * some, some)
+        return pltpu.make_async_copy(turned.at[k % 2], own_ref.at[part], own_sems.at[k % 2])
 
     for k in range(steps):
         start = k * CHUNK
@@ -140,8 +156,8 @@
         slot[:, 128:144, :] = jnp.where(extra_row == 0, high, extra).astype(BF16)
 
         def pair_up(step, carried, slot=slot):
-            for i in range(8):
-                pair = step * 8 + i
+            for i in range(CHUNK // 2):
+                pair = step * (CHUNK // 2) + i
                 place = pl.multiple_of(pair * 2 * tiles, 2 * tiles)
                 first = wide[pl.ds(place, tiles), :]
                 second = wide[pl.ds(place + tiles, tiles), :]
@@ -155,49 +171,61 @@
                     slot[pair, q * tiles : (q + 1) * tiles, :] = pieces[q].astype(BF16)
             return carried
 
-        lax.fori_loop(0, CHUNK // 16, pair_up, 0)
+        lax.fori_loop(0, 1, pair_up, 0)
         store(k).start()
+        reads[k].wait()
+        if k >= 2:
+            store_own(k - 2).wait()
+        turned[k % 2] = jnp.swapaxes(levels[:, k * some : (k + 1) * some, :], 0, 1)
+        store_own(k).start()
+    store_own(steps - 2).wait()
+    store_own(steps - 1).wait()
     store(steps - 2).wait()
     store(steps - 1).wait()
 
 
-def prepare(obs_count, obs_op, rinv_blocks, innov_blocks):
+def prepare(obs_count, obs_op, rinv_blocks, innov_blocks, anomalies):
     blocks, width = obs_op.shape
+    lev_dev, col_dev, members = anomalies.shape
+    steps = blocks // CHUNK
     vmem = pl.BlockSpec(memory_space=pltpu.VMEM)
     anywhere = pl.BlockSpec(memory_space=pl.ANY)
     return pl.pallas_call(
         prepare_kernel,
-        in_specs=[pl.BlockSpec(memory_space=pltpu.SMEM), anywhere, vmem, vmem],
-        out_specs=[anywhere, vmem],
+        in_specs=[pl.BlockSpec(memory_space=pltpu.SMEM), anywhere, vmem, vmem, anywhere],
+        out_specs=[anywhere, vmem, anywhere],
         out_shape=[
             jax.ShapeDtypeStruct((blocks // 2, 144, 128), BF16),
             jax.ShapeDtypeStruct((8, 256), F32),
+            jax.ShapeDtypeStruct((col_dev, lev_dev, members), BF16),
         ],
         scratch_shapes=[
             pltpu.VMEM((blocks, width), BF16),
+            pltpu.VMEM(anomalies.shape, BF16),
             pltpu.VMEM((128, width), BF16),
             pltpu.VMEM((CHUNK * width // 128, 128), F32),
             pltpu.VMEM((CHUNK, 128), F32),
             pltpu.VMEM((2, CHUNK // 2, 144, 128), BF16),
-            pltpu.SemaphoreType.DMA((blocks // CHUNK,)),
+            pltpu.VMEM((2, col_dev // steps, lev_dev, members), BF16),
+            pltpu.SemaphoreType.DMA((steps,)),
+            pltpu.SemaphoreType.DMA((steps,)),
+            pltpu.SemaphoreType.DMA((2,)),
             pltpu.SemaphoreType.DMA((2,)),
         ],
         compiler_params=pltpu.CompilerParams(vmem_limit_bytes=60 << 20),
         name="prepare_operators",
-    )(obs_count, obs_op, rinv_blocks, innov_blocks)
+    )(obs_count, obs_op, rinv_blocks, innov_blocks, anomalies)
 
 
 def gram_kernel(
     cols_ref, count_ref, core_ref, own_ref, remote_ref, pair_ref, sums_ref,
-    keep_ref, give_ref, table, pairs, support, scaled, total, pulled, sems,
+    keep_ref, give_ref, table, pairs, support_a, support_b, scaled_a, scaled_b, total, pulled, sems,
 ):
     own_cols = own_ref.shape[0]
-    n_pairs = pair_ref.shape[0]
     group_pairs = GROUP // 2
-    most = n_pairs // group_pairs
-    own = pltpu.make_async_copy(own_ref, table.at[pl.ds(0, own_cols)], sems.at[most])
+    own = pltpu.make_async_copy(own_ref, table.at[pl.ds(0, own_cols)], sems.at[2])
     remote = pltpu.make_async_copy(
-        remote_ref, table.at[pl.ds(own_cols, remote_ref.shape[0])], sems.at[most + 1]
+        remote_ref, table.at[pl.ds(own_cols, remote_ref.shape[0])], sems.at[3]
     )
     own.start()
     remote.start()
@@ -205,26 +233,27 @@
 
     def fetch(g):
         part = pl.ds(g * group_pairs, group_pairs)
-        return pltpu.make_async_copy(pair_ref.at[part], pairs.at[part], sems.at[g])
-
-    def begin(g, carried):
-        fetch(g).start()
-        return carried
-
-    lax.fori_loop(0, groups, begin, 0)
+        return pltpu.make_async_copy(pair_ref.at[part], pairs.at[g % 2], sems.at[g % 2])
+
+    fetch(0).start()
     total[...] = jnp.zeros_like(total)
     pulled[...] = jnp.zeros_like(pulled)
+    remote.wait()
     own.wait()
-    remote.wait()
-
-    def step(g, carried):
-        fetch(g).wait()
-        for i in range(GROUP * 8):
-            support[i] = table[cols_ref[g * (GROUP * 8) + i]]
+
+    half = GROUP // 2
+    most_halves = cols_ref.shape[0] // (half * 8)
+
+    def collect(h, support):
+        place = jnp.minimum(h, most_halves - 1) * (half * 8)
+        for i in range(half * 8):
+            support[i] = table[cols_ref[place + i]]
+
+    def add(operators, first, support, scaled):
         extra = jnp.zeros((16, 256), F32)
-        for j in range(group_pairs):
+        for j in range(half // 2):
             points = support[j * 16 : (j + 1) * 16].reshape(128, 256)
-            images = jnp.dot(pairs[g * group_pairs + j], points, preferred_element_type=F32)
+            images = jnp.dot(operators[first + j], points, preferred_element_type=F32)
             scaled[j * 128 : (j + 1) * 128, :] = images[:128].astype(BF16)
             extra = extra + images[128:]
         pulled[...] += extra
@@ -232,8 +261,22 @@
         total[...] += lax.dot_general(
             rows, rows, (((0,), (0,)), ((), ())), preferred_element_type=F32
         )
+
+    def step(g, carried):
+        fetch(g).wait()
+
+        @pl.when(g + 1 < groups)
+        def _():
+            fetch(g + 1).start()
+
+        operators = pairs.at[g % 2]
+        collect(2 * g + 1, support_b)
+        add(operators, 0, support_a, scaled_a)
+        collect(2 * g + 2, support_a)
+        add(operators, half // 2, support_b, scaled_b)
         return carried
 
+    collect(0, support_a)
     lax.fori_loop(0, groups, step, 0)
 
     projection = pulled[0:1, :] + pulled[1:2, :] + pulled[2:3, :]
@@ -261,7 +304,6 @@
     smem = pl.BlockSpec(memory_space=pltpu.SMEM)
     anywhere = pl.BlockSpec(memory_space=pl.ANY)
     half = jax.ShapeDtypeStruct((PACK, 256), F32)
-    most = pairs.shape[0] // (GROUP // 2)
     return pl.pallas_call(
         gram_kernel,
         in_specs=[smem, smem, smem, anywhere, anywhere, anywhere, vmem],
@@ -269,14 +311,16 @@
         out_shape=[half, half],
         scratch_shapes=[
             pltpu.VMEM((own.shape[0] + remote.shape[0],) + own.shape[1:], BF16),
-            pltpu.VMEM(pairs.shape, BF16),
-            pltpu.VMEM((GROUP * 8, 8, 256), BF16),
-            pltpu.VMEM((GROUP * 64, 256), BF16),
+            pltpu.VMEM((2, GROUP // 2) + pairs.shape[1:], BF16),
+            pltpu.VMEM((GROUP * 4, 8, 256), BF16),
+            pltpu.VMEM((GROUP * 4, 8, 256), BF16),
+            pltpu.VMEM((GROUP * 32, 256), BF16),
+            pltpu.VMEM((GROUP * 32, 256), BF16),
             pltpu.VMEM((256, 256), F32),
             pltpu.VMEM((16, 256), F32),
-            pltpu.SemaphoreType.DMA((most + 2,)),
+            pltpu.SemaphoreType.DMA((4,)),
         ],
-        compiler_params=pltpu.CompilerParams(vmem_limit_bytes=56 << 20),
+        compiler_params=pltpu.CompilerParams(vmem_limit_bytes=50 << 20),
         name="gram_sums",
     )(obs_cols, obs_count, core, own, remote, pairs, sums)
 
@@ -385,21 +429,17 @@
             pltpu.SemaphoreType.DMA((lev_dev,)),
             pltpu.SemaphoreType.DMA((lev_dev,)),
         ],
-        compiler_params=pltpu.CompilerParams(vmem_limit_bytes=58 << 20),
+        compiler_params=pltpu.CompilerParams(vmem_limit_bytes=53 << 20),
         name="solve_and_apply",
     )(core, mine, other, mean_state, anomalies)
 
 
-def turns(devices, stride, distance):
-    pairs = []
-    for device in range(devices):
-        place = (device // stride) % 4
-        pairs.append((device, device + ((place + distance) % 4 - place) * stride))
-    return pairs
-
-
-def sum_over(value, devices, stride):
-    arrived = [lax.ppermute(value, AXES, turns(devices, stride, d)) for d in (2, 1, 3)]
+def swap(value, devices, mask):
+    return lax.ppermute(value, AXES, [(d, d ^ mask) for d in range(devices)])
+
+
+def sum_over(value, devices, one, two):
+    arrived = [swap(value, devices, mask) for mask in (one, two, one | two)]
     return (value + arrived[0]) + (arrived[1] + arrived[2])
 
 
@@ -412,15 +452,14 @@
     outgoing = gather_sent(send_cols, anomalies)
     remote = lax.all_to_all(outgoing, "tile", split_axis=0, concat_axis=0, tiled=True)
 
-    own = jnp.transpose(anomalies, (1, 0, 2))
     rinv_blocks = obs_rinv.reshape(blocks, per_block)
     innov_blocks = innovations.reshape(blocks, per_block)
-    pairs, sums = prepare(obs_count, obs_op, rinv_blocks, innov_blocks)
+    pairs, sums, own = prepare(obs_count, obs_op, rinv_blocks, innov_blocks, anomalies)
     keep, give = gram_sums(obs_cols, obs_count, core, own, remote, pairs, sums)
-    value = keep + lax.ppermute(give, AXES, [(d, d ^ 1) for d in range(devices)])
-    for stride in (2, 8, 32):
-        value = sum_over(value, devices, stride)
-    other = lax.ppermute(value, AXES, [(d, d ^ 1) for d in range(devices)])
+    value = keep + swap(give, devices, 1)
+    for one, two in ((2, 8), (32, 6), (24, 96)):
+        value = sum_over(value, devices, one, two)
+    other = swap(value, devices, 1)
     return solve_and_apply(core, value, other, mean_state, anomalies)
 
 

time: 117 us -> 99.9 us (0.85)
  local copies, waits for them, and re-layouts: 13.5 us -> 2.31 us
  Pallas kernels: 50.6 us -> 45.3 us
    unnamed x11 -> x10, local copies, waits for them, and re-layouts: 11.9 us -> 0.71 us
    pallas_call x1, Pallas kernels: 12.1 us -> 7.71 us  [gram_sums(): pl.pallas_call(gram_kernel, in_specs=[smem, smem, smem, anywhere, anywher...]
    all_to_all x1, waiting for transfers between devices: 0.01 us -> 1.88 us  [per_device(): lax.all_to_all(outgoing, 'tile', split_axis=0, concat_axis=0, tiled=True)]
    ppermute x11, waiting for transfers between devices: 16.3 us -> 14.5 us  [swap(): return lax.ppermute(value, AXES, [(d, d ^ mask) for d in range(devices)])]
  transfers between devices with their start and end apart: 12 -> 12, of which waited for: 9 -> 11; matrix products, arithmetic and copies ran while one was open for 10% -> 2% of each run, Pallas kernels for 14% -> 17%
where the time goes in v3:
time: 99.9 us; the launch traced here: 99.8 us
  Pallas kernels  45.3 us (45%)
  starting transfers between devices  34.8 us (35%)
  waiting for transfers between devices  16.4 us (16%)
  local copies, waits for them, and re-layouts  2.31 us (2%)
    ppermute x11, starting transfers between devices, swap(): return lax.ppermute(value, AXES, [(d, d ^ mask) for d in range(devices)])  27.2 us
    pallas_call x1, Pallas kernels, prepare(): pl.pallas_call(prepare_kernel, in_specs=[pl.BlockSpec(memory_space=pltpu....  16.5 us
    ppermute x11, waiting for transfers between devices, swap(): return lax.ppermute(value, AXES, [(d, d ^ mask) for d in range(devices)])  14.5 us
    pallas_call x1, Pallas kernels, solve_and_apply(): pl.pallas_call(apply_kernel, in_specs=[pl.BlockSpec(memory_space=pltpu.SM...  12.8 us
    pallas_call x1, Pallas kernels, gather_sent(): pl.pallas_call(send_kernel, in_specs=[pl.BlockSpec(memory_space=pltpu.SME...  8.4 us
    pallas_call x1, Pallas kernels, gram_sums(): pl.pallas_call(gram_kernel, in_specs=[smem, smem, smem, anywhere, anywher...  7.71 us
    all_to_all x1, starting transfers between devices, per_device(): lax.all_to_all(outgoing, 'tile', split_axis=0, concat_axis=0, tiled=True)  7.6 us
  transfers between devices with their start and end apart: 12, of which 11 were waited for; matrix products, arithmetic and copies ran while one was open for 2% of the time, Pallas kernels for 17%

profile of v3, /device:TPU:1, one launch (start us, length us, event | category | flops | bytes accessed | tf_op | source)
XLA Modules:
  0.0 99.8 jit_solution(5515785739420409691)
XLA Ops:
  0.0 0.0 copy-start.3
  0.0 0.0 copy-start.4
  0.0 8.4 %gather_sent.1 = bf16[384,8,256]{2,1,0:T(8,128)(2,1)} custom-call(s32[1,384]{1,0:T(1,128)} %send_ref.1, bf16[8,2048,256]{2,1,0:T(8,128)(2,1)} %anom_ref.5), custom_call_target="tpu_custom_call" | custom-call | tf_op jit(solution)/shard_map/gather_sent/pallas_call | solution.py:63
  8.4 0.0 copy-start.1
  8.4 7.6 %all-to-all-start = ((bf16[384,8,256]{2,1,0:T(8,128)(2,1)}), bf16[384,8,256]{2,1,0:T(8,128)(2,1)S(1)}, u32[]{:S(2)}, u32[]{:S(2)}) async-start(bf16[384,8,256]{2,1,0:T(8,128)(2,1)} %gather_sent.1), calls=%async_computation | async-start | bytes 3145728 | tf_op jit(solution)/shard_map/all_to_all | solution.py:453
  16.7 0.0 copy-done.3
  16.7 0.8 reshape.11.innov_ref
  17.5 0.0 copy-done.4
  17.5 0.8 reshape.10.rinv_ref
  18.3 16.5 %prepare_operators.1 = (bf16[256,144,128]{2,1,0:T(8,128)(2,1)}, f32[8,256]{1,0:T(8,128)}, bf16[2048,8,256]{2,1,0:T(8,128)(2,1)}) custom-call(s32[1]{0:T(128)S(6)} %copy.9.count_ref, bf16[512,4096]{1,0:T(8,128)(2,1)} %op_ref.1, f32[512,64]{1,0:T(8,128)} %reshape.10.rinv_ref, f32[512,64]{1,0:T(8,128)} %reshape.11.innov_ref, bf16[8,2048,256]{2,1,0:T(8,128)(2,1)} %anom_ref.5), custom_call_target="tpu_custom_call" | custom-call | tf_op jit(solution)/shard_map/prepare_operators/pallas_call | solution.py:193
  34.8 1.9 %all-to-all-done.remote_ref = bf16[384,8,256]{2,1,0:T(8,128)(2,1)S(1)} async-done(((bf16[384,8,256]{2,1,0:T(8,128)(2,1)}), bf16[384,8,256]{2,1,0:T(8,128)(2,1)S(1)}, u32[]{:S(2)}, u32[]{:S(2)}) %all-to-all-start) | async-done | bytes 1572896 | tf_op jit(solution)/shard_map/all_to_all | solution.py:453
  36.7 0.0 copy-done.1
  36.7 0.0 copy-start.2
  36.7 0.7 copy-done.2
  37.4 0.0 copy-start
  37.4 7.7 %gram_sums.1 = (f32[104,256]{1,0:T(8,128)S(1)}, f32[104,256]{1,0:T(8,128)S(1)}) custom-call(s32[4096]{0:T(1024)S(1)} %copy-done.1, s32[1]{0:T(128)S(6)} %copy.9.count_ref, s32[1]{0:T(128)} %bitcast.core_ref, bf16[2048,8,256]{2,1,0:T(8,128)(2,1)} %get-tuple-element.10.own_ref, bf16[384,8,256]{2,1,0:T(8,128)(2,1)S(1)} %all-to-all-done.remote_ref, ...), custom_call_target="tpu_custom_call" | custom-call | tf_op jit(solution)/shard_map/gram_sums/pallas_call | solution.py:307
  45.1 12.4 %collective-permute-start = (f32[104,256]{1,0:T(8,128)S(1)}, f32[104,256]{1,0:T(8,128)S(1)}, u32[]{:S(2)}, u32[]{:S(2)}) collective-permute-start(f32[104,256]{1,0:T(8,128)S(1)} %get-tuple-element.14), channel_id=1, source_target_pairs={{0,1},{1,0},{2,3},{3,2},{4,5},{5,4},{6,7},{7,6},{8,9},{9,8},{10,11... | collective-permute-start | bytes 319496 | tf_op jit(solution)/shard_map/ppermute | solution.py:438
  57.5 1.0 collective-permute-done
  58.5 0.1 collective-permute-start.3
  58.5 0.3 collective-permute-start.2
  58.9 2.3 %collective-permute-start.1 = (f32[104,256]{1,0:T(8,128)S(1)}, f32[104,256]{1,0:T(8,128)S(1)}, u32[]{:S(2)}, u32[]{:S(2)}) collective-permute-start(f32[104,256]{1,0:T(8,128)S(1)} %add.35), channel_id=1, source_target_pairs={{0,2},{1,3},{2,0},{3,1},{4,6},{5,7},{6,4},{7,5},{8,10},{9,11},{10,... | collective-permute-start | bytes 319496 | tf_op jit(solution)/shard_map/ppermute | solution.py:438
  61.2 2.4 %collective-permute-done.3 = f32[104,256]{1,0:T(8,128)S(1)} collective-permute-done((f32[104,256]{1,0:T(8,128)S(1)}, f32[104,256]{1,0:T(8,128)S(1)}, u32[]{:S(2)}, u32[]{:S(2)}) %collective-permute-start.3) | collective-permute-done | bytes 106528 | tf_op jit(solution)/shard_map/ppermute | solution.py:438
  63.6 0.5 collective-permute-done.2
  64.1 2.5 %collective-permute-done.1 = f32[104,256]{1,0:T(8,128)S(1)} collective-permute-done((f32[104,256]{1,0:T(8,128)S(1)}, f32[104,256]{1,0:T(8,128)S(1)}, u32[]{:S(2)}, u32[]{:S(2)}) %collective-permute-start.1) | collective-permute-done | bytes 106528 | tf_op jit(solution)/shard_map/ppermute | solution.py:438
  66.6 0.1 collective-permute-start.6
  66.7 2.1 %collective-permute-start.5 = (f32[104,256]{1,0:T(8,128)S(1)}, f32[104,256]{1,0:T(8,128)S(1)}, u32[]{:S(2)}, u32[]{:S(2)}) collective-permute-start(f32[104,256]{1,0:T(8,128)S(1)} %add_add_fusion.2), channel_id=1, source_target_pairs={{0,6},{1,7},{2,4},{3,5},{4,2},{5,3},{6,0},{7,1},{8,14},{9,15},{10,... | collective-permute-start | bytes 319496 | tf_op jit(solution)/shard_map/ppermute | solution.py:438
  68.8 1.8 %collective-permute-start.4 = (f32[104,256]{1,0:T(8,128)S(1)}, f32[104,256]{1,0:T(8,128)S(1)}, u32[]{:S(2)}, u32[]{:S(2)}) collective-permute-start(f32[104,256]{1,0:T(8,128)S(1)} %add_add_fusion.2), channel_id=1, source_target_pairs={{0,32},{1,33},{2,34},{3,35},{4,36},{5,37},{6,38},{7,39},{8,40},{9,... | collective-permute-start | bytes 319496 | tf_op jit(solution)/shard_map/ppermute | solution.py:438
  70.6 2.3 %collective-permute-done.6 = f32[104,256]{1,0:T(8,128)S(1)} collective-permute-done((f32[104,256]{1,0:T(8,128)S(1)}, f32[104,256]{1,0:T(8,128)S(1)}, u32[]{:S(2)}, u32[]{:S(2)}) %collective-permute-start.6) | collective-permute-done | bytes 106528 | tf_op jit(solution)/shard_map/ppermute | solution.py:438
  72.9 1.5 %collective-permute-done.5 = f32[104,256]{1,0:T(8,128)S(1)} collective-permute-done((f32[104,256]{1,0:T(8,128)S(1)}, f32[104,256]{1,0:T(8,128)S(1)}, u32[]{:S(2)}, u32[]{:S(2)}) %collective-permute-start.5) | collective-permute-done | bytes 106528 | tf_op jit(solution)/shard_map/ppermute | solution.py:438
  74.4 0.0 collective-permute-done.4
  74.4 2.5 %collective-permute-start.9 = (f32[104,256]{1,0:T(8,128)S(1)}, f32[104,256]{1,0:T(8,128)S(1)}, u32[]{:S(2)}, u32[]{:S(2)}) collective-permute-start(f32[104,256]{1,0:T(8,128)S(1)} %add_add_fusion.1), channel_id=1, source_target_pairs={{0,120},{1,121},{2,122},{3,123},{4,124},{5,125},{6,126},{7,127},{8... | collective-permute-start | bytes 319496 | tf_op jit(solution)/shard_map/ppermute | solution.py:438
  76.9 0.5 collective-permute-start.8
  77.4 2.2 %collective-permute-start.7 = (f32[104,256]{1,0:T(8,128)S(1)}, f32[104,256]{1,0:T(8,128)S(1)}, u32[]{:S(2)}, u32[]{:S(2)}) collective-permute-start(f32[104,256]{1,0:T(8,128)S(1)} %add_add_fusion.1), channel_id=1, source_target_pairs={{0,24},{1,25},{2,26},{3,27},{4,28},{5,29},{6,30},{7,31},{8,16},{9,... | collective-permute-start | bytes 319496 | tf_op jit(solution)/shard_map/ppermute | solution.py:438
  79.6 1.8 %collective-permute-done.9 = f32[104,256]{1,0:T(8,128)S(1)} collective-permute-done((f32[104,256]{1,0:T(8,128)S(1)}, f32[104,256]{1,0:T(8,128)S(1)}, u32[]{:S(2)}, u32[]{:S(2)}) %collective-permute-start.9) | collective-permute-done | bytes 106528 | tf_op jit(solution)/shard_map/ppermute | solution.py:438
  81.4 0.8 collective-permute-done.8
  82.2 0.7 collective-permute-done.7
  82.9 3.0 %collective-permute-start.10 = (f32[104,256]{1,0:T(8,128)S(1)}, f32[104,256]{1,0:T(8,128)S(1)}, u32[]{:S(2)}, u32[]{:S(2)}) collective-permute-start(f32[104,256]{1,0:T(8,128)S(1)} %add_add_fusion.mine_ref), channel_id=1, source_target_pairs={{0,1},{1,0},{2,3},{3,2},{4,5},{5,4},{6,7},{7,6},{8,9},{9,8},{10,11... | collective-permute-start | bytes 319496 | tf_op jit(solution)/shard_map/ppermute | solution.py:438
  85.9 1.0 collective-permute-done.10.other_ref
  86.9 0.0 copy-done
  86.9 12.8 %solve_and_apply.1 = bf16[8,2048,256]{2,1,0:T(8,128)(2,1)} custom-call(s32[1]{0:T(128)} %bitcast.core_ref, f32[104,256]{1,0:T(8,128)S(1)} %add_add_fusion.mine_ref, f32[104,256]{1,0:T(8,128)S(1)} %collective-permute-done.10.other_ref, f32[8,2048]{1,0:T(8,128)S(1)} %copy-done, bf16[8,2048,256]{2,1,0:T(8,128)(2,1)} %anom_ref.5), custom_call_target="tpu_custom_call" | custom-call | tf_op jit(solution)/shard_map/solve_and_apply/pallas_call | solution.py:419
  (4 shorter events, 0.1 us)
Async XLA Ops:
  0.0 16.7 %copy-start.3 = (f32[32768]{0:T(1024)S(1)}, f32[32768]{0:T(1024)}, u32[]{:S(2)}) copy-start(f32[32768]{0:T(1024)} %param.11) | copy-start | bytes 393220
  0.0 17.5 %copy-start.4 = (f32[32768]{0:T(1024)S(1)}, f32[32768]{0:T(1024)}, u32[]{:S(2)}) copy-start(f32[32768]{0:T(1024)} %param.12) | copy-start | bytes 393220
  8.4 28.2 %copy-start.1 = (s32[4096]{0:T(1024)S(1)}, s32[4096]{0:T(1024)}, u32[]{:S(2)}) copy-start(s32[4096]{0:T(1024)} %cols_ref.1) | copy-start | bytes 49156
  8.4 28.2 %all-to-all-start = ((bf16[384,8,256]{2,1,0:T(8,128)(2,1)}), bf16[384,8,256]{2,1,0:T(8,128)(2,1)S(1)}, u32[]{:S(2)}, u32[]{:S(2)}) async-start(bf16[384,8,256]{2,1,0:T(8,128)(2,1)} %gather_sent.1), calls=%async_computation | async-start | bytes 3145728 | tf_op jit(solution)/shard_map/all_to_all | solution.py:453
  36.7 0.7 copy-start.2
  37.4 49.5 %copy-start = (f32[8,2048]{1,0:T(8,128)S(1)}, f32[8,2048]{1,0:T(8,128)}, u32[]{:S(2)}) copy-start(f32[8,2048]{1,0:T(8,128)} %mean_ref.1) | copy-start | bytes 196612
  45.1 13.4 %collective-permute-start = (f32[104,256]{1,0:T(8,128)S(1)}, f32[104,256]{1,0:T(8,128)S(1)}, u32[]{:S(2)}, u32[]{:S(2)}) collective-permute-start(f32[104,256]{1,0:T(8,128)S(1)} %get-tuple-element.14), channel_id=1, source_target_pairs={{0,1},{1,0},{2,3},{3,2},{4,5},{5,4},{6,7},{7,6},{8,9},{9,8},{10,11... | collective-permute-start | bytes 319496 | tf_op jit(solution)/shard_map/ppermute | solution.py:438
  58.5 5.2 %collective-permute-start.3 = (f32[104,256]{1,0:T(8,128)S(1)}, f32[104,256]{1,0:T(8,128)S(1)}, u32[]{:S(2)}, u32[]{:S(2)}) collective-permute-start(f32[104,256]{1,0:T(8,128)S(1)} %add.35), channel_id=1, source_target_pairs={{0,10},{1,11},{2,8},{3,9},{4,14},{5,15},{6,12},{7,13},{8,2},{9,3},... | collective-permute-start | bytes 319496 | tf_op jit(solution)/shard_map/ppermute | solution.py:438
  58.5 5.6 %collective-permute-start.2 = (f32[104,256]{1,0:T(8,128)S(1)}, f32[104,256]{1,0:T(8,128)S(1)}, u32[]{:S(2)}, u32[]{:S(2)}) collective-permute-start(f32[104,256]{1,0:T(8,128)S(1)} %add.35), channel_id=1, source_target_pairs={{0,8},{1,9},{2,10},{3,11},{4,12},{5,13},{6,14},{7,15},{8,0},{9,1},... | collective-permute-start | bytes 319496 | tf_op jit(solution)/shard_map/ppermute | solution.py:438
  58.9 7.7 %collective-permute-start.1 = (f32[104,256]{1,0:T(8,128)S(1)}, f32[104,256]{1,0:T(8,128)S(1)}, u32[]{:S(2)}, u32[]{:S(2)}) collective-permute-start(f32[104,256]{1,0:T(8,128)S(1)} %add.35), channel_id=1, source_target_pairs={{0,2},{1,3},{2,0},{3,1},{4,6},{5,7},{6,4},{7,5},{8,10},{9,11},{10,... | collective-permute-start | bytes 319496 | tf_op jit(solution)/shard_map/ppermute | solution.py:438
  66.6 6.3 %collective-permute-start.6 = (f32[104,256]{1,0:T(8,128)S(1)}, f32[104,256]{1,0:T(8,128)S(1)}, u32[]{:S(2)}, u32[]{:S(2)}) collective-permute-start(f32[104,256]{1,0:T(8,128)S(1)} %add_add_fusion.2), channel_id=1, source_target_pairs={{0,38},{1,39},{2,36},{3,37},{4,34},{5,35},{6,32},{7,33},{8,46},{9,... | collective-permute-start | bytes 319496 | tf_op jit(solution)/shard_map/ppermute | solution.py:438
  66.7 7.7 %collective-permute-start.5 = (f32[104,256]{1,0:T(8,128)S(1)}, f32[104,256]{1,0:T(8,128)S(1)}, u32[]{:S(2)}, u32[]{:S(2)}) collective-permute-start(f32[104,256]{1,0:T(8,128)S(1)} %add_add_fusion.2), channel_id=1, source_target_pairs={{0,6},{1,7},{2,4},{3,5},{4,2},{5,3},{6,0},{7,1},{8,14},{9,15},{10,... | collective-permute-start | bytes 319496 | tf_op jit(solution)/shard_map/ppermute | solution.py:438
  68.8 5.6 %collective-permute-start.4 = (f32[104,256]{1,0:T(8,128)S(1)}, f32[104,256]{1,0:T(8,128)S(1)}, u32[]{:S(2)}, u32[]{:S(2)}) collective-permute-start(f32[104,256]{1,0:T(8,128)S(1)} %add_add_fusion.2), channel_id=1, source_target_pairs={{0,32},{1,33},{2,34},{3,35},{4,36},{5,37},{6,38},{7,39},{8,40},{9,... | collective-permute-start | bytes 319496 | tf_op jit(solution)/shard_map/ppermute | solution.py:438
  74.4 7.0 %collective-permute-start.9 = (f32[104,256]{1,0:T(8,128)S(1)}, f32[104,256]{1,0:T(8,128)S(1)}, u32[]{:S(2)}, u32[]{:S(2)}) collective-permute-start(f32[104,256]{1,0:T(8,128)S(1)} %add_add_fusion.1), channel_id=1, source_target_pairs={{0,120},{1,121},{2,122},{3,123},{4,124},{5,125},{6,126},{7,127},{8... | collective-permute-start | bytes 319496 | tf_op jit(solution)/shard_map/ppermute | solution.py:438
  76.9 5.3 %collective-permute-start.8 = (f32[104,256]{1,0:T(8,128)S(1)}, f32[104,256]{1,0:T(8,128)S(1)}, u32[]{:S(2)}, u32[]{:S(2)}) collective-permute-start(f32[104,256]{1,0:T(8,128)S(1)} %add_add_fusion.1), channel_id=1, source_target_pairs={{0,96},{1,97},{2,98},{3,99},{4,100},{5,101},{6,102},{7,103},{8,104... | collective-permute-start | bytes 319496 | tf_op jit(solution)/shard_map/ppermute | solution.py:438
  77.4 5.5 %collective-permute-start.7 = (f32[104,256]{1,0:T(8,128)S(1)}, f32[104,256]{1,0:T(8,128)S(1)}, u32[]{:S(2)}, u32[]{:S(2)}) collective-permute-start(f32[104,256]{1,0:T(8,128)S(1)} %add_add_fusion.1), channel_id=1, source_target_pairs={{0,24},{1,25},{2,26},{3,27},{4,28},{5,29},{6,30},{7,31},{8,16},{9,... | collective-permute-start | bytes 319496 | tf_op jit(solution)/shard_map/ppermute | solution.py:438
  82.9 3.9 %collective-permute-start.10 = (f32[104,256]{1,0:T(8,128)S(1)}, f32[104,256]{1,0:T(8,128)S(1)}, u32[]{:S(2)}, u32[]{:S(2)}) collective-permute-start(f32[104,256]{1,0:T(8,128)S(1)} %add_add_fusion.mine_ref), channel_id=1, source_target_pairs={{0,1},{1,0},{2,3},{3,2},{4,5},{5,4},{6,7},{7,6},{8,9},{9,8},{10,11... | collective-permute-start | bytes 319496 | tf_op jit(solution)/shard_map/ppermute | solution.py:438

commit v4 on v3

--- a/solution.py
+++ b/solution.py
@@ -12,7 +12,7 @@
 AXES = ("tile", "lev")
 GROUP = 128
 CHUNK = 64
-PACK = 104
+PACK = 88
 
 
 def split3(value):
@@ -23,38 +23,28 @@
     return high, middle, low
 
 
-def send_kernel(send_ref, anom_ref, out_ref, levels, wide, sems):
-    lev_dev, col_dev, members = anom_ref.shape
+def send_kernel(send_ref, anom_ref, out_ref, levels, table, sems):
+    col_dev = anom_ref.shape[1]
     slots = out_ref.shape[0]
-    copies = [
-        pltpu.make_async_copy(anom_ref.at[v], levels.at[v], sems.at[v]) for v in range(lev_dev)
-    ]
-    for copy in copies:
-        copy.start()
-    rows = 512
-
-    for v in range(lev_dev):
-        copies[v].wait()
-
-        def spread(step, carried, v=v):
-            start = pl.multiple_of(step * rows, rows)
-            part = levels[v, pl.ds(start, rows), :].astype(F32)
-            for h in range(members // 128):
-                place = pl.ds(start * lev_dev + v, rows, stride=lev_dev)
-                wide.at[h][place, :] = part[:, h * 128 : (h + 1) * 128]
-            return carried
-
-        lax.fori_loop(0, col_dev // rows, spread, 0)
+    steps = sems.shape[0]
+    some = col_dev // steps
+    copies = []
+    for k in range(steps):
+        part = pl.ds(k * some, some)
+        copies.append(pltpu.make_async_copy(anom_ref.at[:, part], levels.at[:, part], sems.at[k]))
+        copies[k].start()
+    for k in range(steps):
+        copies[k].wait()
+        part = slice(k * some, (k + 1) * some)
+        table[part] = jnp.swapaxes(levels[:, part, :], 0, 1)
 
     def pick(step, carried):
-        for i in range(32):
-            slot = step * 32 + i
-            place = pl.ds(pl.multiple_of(send_ref[0, slot] * lev_dev, lev_dev), lev_dev)
-            for h in range(members // 128):
-                out_ref[slot, :, h * 128 : (h + 1) * 128] = wide[h, place, :].astype(BF16)
+        for i in range(64):
+            slot = step * 64 + i
+            out_ref[slot] = table[send_ref[0, slot]]
         return carried
 
-    lax.fori_loop(0, slots // 32, pick, 0)
+    lax.fori_loop(0, slots // 64, pick, 0)
 
 
 def gather_sent(send_cols, anomalies):
@@ -67,8 +57,8 @@
         out_shape=jax.ShapeDtypeStruct((slots, lev_dev, members), BF16),
         scratch_shapes=[
             pltpu.VMEM((lev_dev, col_dev, members), BF16),
-            pltpu.VMEM((members // 128, col_dev * lev_dev, 128), F32),
-            pltpu.SemaphoreType.DMA((lev_dev,)),
+            pltpu.VMEM((col_dev, lev_dev, members), BF16),
+            pltpu.SemaphoreType.DMA((8,)),
         ],
         compiler_params=pltpu.CompilerParams(vmem_limit_bytes=60 << 20),
         name="gather_sent",
@@ -212,7 +202,7 @@
             pltpu.SemaphoreType.DMA((2,)),
             pltpu.SemaphoreType.DMA((2,)),
         ],
-        compiler_params=pltpu.CompilerParams(vmem_limit_bytes=60 << 20),
+        compiler_params=pltpu.CompilerParams(vmem_limit_bytes=52 << 20),
         name="prepare_operators",
     )(obs_count, obs_op, rinv_blocks, innov_blocks, anomalies)
 
@@ -283,9 +273,13 @@
     row = lax.broadcasted_iota(jnp.int32, (8, 256), 0)
     ending = jnp.where(row == 0, projection, jnp.where(row == 1, sums_ref[...], 0.0))
     zeros = jnp.zeros((8, 256), F32)
-    first = total[0:PACK, :]
-    corner = jnp.concatenate([total[128:192, 128:256], total[192:256, 128:256]], axis=1)
-    second = jnp.concatenate([total[PACK:128, :], corner, ending, zeros], axis=0)
+    last = pltpu.roll(total[192:256, 128:256], 64, 1)
+    low_half = lax.broadcasted_iota(jnp.int32, (64, 128), 1) < 64
+    side = jnp.where(low_half, last, total[64:128, 0:128])
+    side = jnp.concatenate([side, total[64:128, 128:256]], axis=1)
+    corner = jnp.concatenate([total[128:160, 128:256], total[160:192, 128:256]], axis=1)
+    first = jnp.concatenate([total[0:64, :], side[: PACK - 64]], axis=0)
+    second = jnp.concatenate([side[PACK - 64 :], corner, ending, zeros], axis=0)
     core = core_ref[0]
 
     @pl.when(core == 0)
@@ -339,7 +333,7 @@
 
 def apply_kernel(
     core_ref, mine_ref, other_ref, mean_ref, anom_ref, out_ref,
-    levels, results, approx_ref, inverse_ref, in_sems, out_sems,
+    levels, results, means, approx_ref, inverse_ref, in_sems, out_sems,
 ):
     lev_dev = anom_ref.shape[0]
     members = anom_ref.shape[2]
@@ -350,21 +344,30 @@
         load.start()
     core = core_ref[0]
     mine, other = mine_ref[...], other_ref[...]
-    first = jnp.where(core == 0, mine, other)
-    second = jnp.where(core == 0, other, mine)
-    upper = jnp.concatenate([first, second[: 128 - PACK]], axis=0)
-    packed = second[128 - PACK : 192 - PACK]
-    corner = jnp.concatenate([packed[:, :128], packed[:, 128:]], axis=0)
-    projection = second[192 - PACK : 193 - PACK]
-    sums = second[193 - PACK : 194 - PACK]
-    side = upper[:, 128:]
-    gram = jnp.concatenate([upper, jnp.concatenate([side.T, corner], axis=1)], axis=0)
-    gram = 0.5 * (gram + gram.T)
+    packed = jnp.concatenate(
+        [jnp.where(core == 0, mine, other), jnp.where(core == 0, other, mine)], axis=0
+    )
+    side = packed[64:128]
+    corner = jnp.concatenate([packed[128:160, :128], packed[128:160, 128:]], axis=0)
+    corner = jnp.concatenate([corner, pltpu.roll(side[:, :128], 64, 1)], axis=0)
+    corner = jnp.concatenate([jnp.zeros((128, 128), F32), corner], axis=1)
+    upper = jnp.concatenate([packed[0:128], corner], axis=0)
+    lower = upper.T
+    rows = lax.broadcasted_iota(jnp.int32, (members, members), 0)
+    lanes = lax.broadcasted_iota(jnp.int32, (members, members), 1)
+    row_block = lax.shift_right_logical(rows, 6)
+    lane_block = lax.shift_right_logical(lanes, 6)
+    gram = jnp.where(
+        lane_block > row_block,
+        upper,
+        jnp.where(lane_block < row_block, lower, 0.5 * (upper + lower)),
+    )
+    projection = packed[160:161]
+    sums = packed[161:162]
+    means[...] = mean_ref[...].T
 
     numerator, obs_total = sums[:, 0:1], sums[:, 1:2]
     shift = (members - 1.0) * obs_total / numerator
-    rows = lax.broadcasted_iota(jnp.int32, (members, members), 0)
-    lanes = lax.broadcasted_iota(jnp.int32, (members, members), 1)
     identity = jnp.where(rows == lanes, 1.0, 0.0)
     system = gram + shift * identity
     norm = jnp.sqrt(jnp.sum(system * system, axis=(0, 1), keepdims=True))
@@ -400,7 +403,6 @@
     root = (jnp.sqrt((members - 1.0) / norm)) * inverse
     transform = (root + jnp.concatenate([weights, weights], axis=1)).astype(BF16)
 
-    means = mean_ref[...].T
     stores = []
     for v in range(lev_dev):
         loads[v].wait()
@@ -415,7 +417,7 @@
 def solve_and_apply(core, mine, other, mean_state, anomalies):
     vmem = pl.BlockSpec(memory_space=pltpu.VMEM)
     anywhere = pl.BlockSpec(memory_space=pl.ANY)
-    lev_dev, _, members = anomalies.shape
+    lev_dev, col_dev, members = anomalies.shape
     return pl.pallas_call(
         apply_kernel,
         in_specs=[pl.BlockSpec(memory_space=pltpu.SMEM), vmem, vmem, vmem, anywhere],
@@ -424,6 +426,7 @@
         scratch_shapes=[
             pltpu.VMEM(anomalies.shape, BF16),
             pltpu.VMEM(anomalies.shape, BF16),
+            pltpu.VMEM((col_dev, lev_dev), F32),
             pltpu.VMEM((members, members), F32),
             pltpu.VMEM((members, members), F32),
             pltpu.SemaphoreType.DMA((lev_dev,)),

time: 99.9 us -> 96 us (0.961)
  starting transfers between devices: 34.8 us -> 26.3 us
  Pallas kernels: 45.3 us -> 49.9 us
  waiting for transfers between devices: 16.4 us -> 18.5 us
  local copies, waits for them, and re-layouts: 2.31 us -> 0.22 us
    ppermute x11, starting transfers between devices: 27.2 us -> 18.7 us  [swap(): return lax.ppermute(value, AXES, [(d, d ^ mask) for d in range(devices)])]
    pallas_call x1, Pallas kernels: 7.71 us -> 16 us  [gram_sums(): pl.pallas_call(gram_kernel, in_specs=[smem, smem, smem, anywhere, anywher...]
    all_to_all x1, waiting for transfers between devices: 1.88 us -> 4.79 us  [per_device(): lax.all_to_all(outgoing, 'tile', split_axis=0, concat_axis=0, tiled=True)]
    pallas_call x1, Pallas kernels: 8.4 us -> 6.13 us  [gather_sent(): pl.pallas_call(send_kernel, in_specs=[pl.BlockSpec(memory_space=pltpu.SME...]
    pallas_call x1, Pallas kernels: 16.5 us -> 14.9 us  [prepare(): pl.pallas_call(prepare_kernel, in_specs=[pl.BlockSpec(memory_space=pltpu....]
  transfers between devices with their start and end apart: 12 -> 12, of which waited for: 11 -> 11; matrix products, arithmetic and copies ran while one was open for 2% -> 0% of each run, Pallas kernels for 17% -> 16%
where the time goes in v4:
time: 96 us
  Pallas kernels  49.9 us (52%)
  starting transfers between devices  26.3 us (27%)
  waiting for transfers between devices  18.5 us (19%)
  between operations  0.97 us (1%)
    ppermute x11, starting transfers between devices, swap(): return lax.ppermute(value, AXES, [(d, d ^ mask) for d in range(devices)])  18.7 us
    pallas_call x1, Pallas kernels, gram_sums(): pl.pallas_call(gram_kernel, in_specs=[smem, smem, smem, anywhere, anywher...  16 us
    pallas_call x1, Pallas kernels, prepare(): pl.pallas_call(prepare_kernel, in_specs=[pl.BlockSpec(memory_space=pltpu....  14.9 us
    ppermute x11, waiting for transfers between devices, swap(): return lax.ppermute(value, AXES, [(d, d ^ mask) for d in range(devices)])  13.7 us
    pallas_call x1, Pallas kernels, solve_and_apply(): pl.pallas_call(apply_kernel, in_specs=[pl.BlockSpec(memory_space=pltpu.SM...  12.9 us
    all_to_all x1, starting transfers between devices, per_device(): lax.all_to_all(outgoing, 'tile', split_axis=0, concat_axis=0, tiled=True)  7.6 us
    pallas_call x1, Pallas kernels, gather_sent(): pl.pallas_call(send_kernel, in_specs=[pl.BlockSpec(memory_space=pltpu.SME...  6.13 us
    all_to_all x1, waiting for transfers between devices, per_device(): lax.all_to_all(outgoing, 'tile', split_axis=0, concat_axis=0, tiled=True)  4.79 us
  transfers between devices with their start and end apart: 12, of which 11 were waited for; matrix products, arithmetic and copies ran while one was open for 0% of the time, Pallas kernels for 16%

profile of v4, /device:TPU:1, one launch (start us, length us, event | category | flops | bytes accessed | tf_op | source)
XLA Modules:
  0.0 96.0 jit_solution(1238414210599896662)
XLA Ops:
  0.0 0.0 copy-start.2
  0.0 0.0 copy-start.3
  0.0 6.1 %gather_sent.1 = bf16[384,8,256]{2,1,0:T(8,128)(2,1)} custom-call(s32[1,384]{1,0:T(1,128)} %send_ref.1, bf16[8,2048,256]{2,1,0:T(8,128)(2,1)} %anom_ref.5), custom_call_target="tpu_custom_call" | custom-call | tf_op jit(solution)/shard_map/gather_sent/pallas_call | solution.py:53
  6.1 0.0 copy-start.1
  6.2 7.6 %all-to-all-start = ((bf16[384,8,256]{2,1,0:T(8,128)(2,1)}), bf16[384,8,256]{2,1,0:T(8,128)(2,1)S(1)}, u32[]{:S(2)}, u32[]{:S(2)}) async-start(bf16[384,8,256]{2,1,0:T(8,128)(2,1)} %gather_sent.1), calls=%async_computation | async-start | bytes 3145728 | tf_op jit(solution)/shard_map/all_to_all | solution.py:456
  14.4 0.0 copy-done.2
  14.4 0.1 reshape.11.innov_ref
  14.5 0.0 copy-done.3
  14.5 0.1 reshape.10.rinv_ref
  14.7 14.9 %prepare_operators.1 = (bf16[256,144,128]{2,1,0:T(8,128)(2,1)}, f32[8,256]{1,0:T(8,128)S(1)}, bf16[2048,8,256]{2,1,0:T(8,128)(2,1)}) custom-call(s32[1]{0:T(128)S(6)} %copy.9.count_ref, bf16[512,4096]{1,0:T(8,128)(2,1)} %op_ref.1, f32[512,64]{1,0:T(8,128)S(1)} %reshape.10.rinv_ref, f32[512,64]{1,0:T(8,128)S(1)} %reshape.11.innov_ref, ...), custom_call_target="tpu_custom_call" | custom-call | tf_op jit(solution)/shard_map/prepare_operators/pallas_call | solution.py:183
  29.6 4.8 %all-to-all-done.remote_ref = bf16[384,8,256]{2,1,0:T(8,128)(2,1)S(1)} async-done(((bf16[384,8,256]{2,1,0:T(8,128)(2,1)}), bf16[384,8,256]{2,1,0:T(8,128)(2,1)S(1)}, u32[]{:S(2)}, u32[]{:S(2)}) %all-to-all-start) | async-done | bytes 1572896 | tf_op jit(solution)/shard_map/all_to_all | solution.py:456
  34.4 0.0 copy-done.1
  34.4 0.0 copy-start
  34.4 16.0 %gram_sums.1 = (f32[88,256]{1,0:T(8,128)S(1)}, f32[88,256]{1,0:T(8,128)S(1)}) custom-call(s32[4096]{0:T(1024)S(1)} %copy-done.1, s32[1]{0:T(128)S(6)} %copy.9.count_ref, s32[1]{0:T(128)} %bitcast.core_ref, bf16[2048,8,256]{2,1,0:T(8,128)(2,1)} %get-tuple-element.10.own_ref, bf16[384,8,256]{2,1,0:T(8,128)(2,1)S(1)} %all-to-all-done.remote_ref, ...), custom_call_target="tpu_custom_call" | custom-call | tf_op jit(solution)/shard_map/gram_sums/pallas_call | solution.py:301
  50.4 4.2 %collective-permute-start = (f32[88,256]{1,0:T(8,128)S(1)}, f32[88,256]{1,0:T(8,128)S(1)}, u32[]{:S(2)}, u32[]{:S(2)}) collective-permute-start(f32[88,256]{1,0:T(8,128)S(1)} %get-tuple-element.14), channel_id=1, source_target_pairs={{0,1},{1,0},{2,3},{3,2},{4,5},{5,4},{6,7},{7,6},{8,9},{9,8},{10,11... | collective-permute-start | bytes 270344 | tf_op jit(solution)/shard_map/ppermute | solution.py:441
  54.6 0.9 collective-permute-done
  55.5 0.1 collective-permute-start.3
  55.6 2.8 %collective-permute-start.2 = (f32[88,256]{1,0:T(8,128)S(1)}, f32[88,256]{1,0:T(8,128)S(1)}, u32[]{:S(2)}, u32[]{:S(2)}) collective-permute-start(f32[88,256]{1,0:T(8,128)S(1)} %add.35), channel_id=1, source_target_pairs={{0,8},{1,9},{2,10},{3,11},{4,12},{5,13},{6,14},{7,15},{8,0},{9,1},... | collective-permute-start | bytes 270344 | tf_op jit(solution)/shard_map/ppermute | solution.py:441
  58.4 0.0 collective-permute-start.1
  58.4 1.9 %collective-permute-done.3 = f32[88,256]{1,0:T(8,128)S(1)} collective-permute-done((f32[88,256]{1,0:T(8,128)S(1)}, f32[88,256]{1,0:T(8,128)S(1)}, u32[]{:S(2)}, u32[]{:S(2)}) %collective-permute-start.3) | collective-permute-done | bytes 90144 | tf_op jit(solution)/shard_map/ppermute | solution.py:441
  60.3 2.4 %collective-permute-done.2 = f32[88,256]{1,0:T(8,128)S(1)} collective-permute-done((f32[88,256]{1,0:T(8,128)S(1)}, f32[88,256]{1,0:T(8,128)S(1)}, u32[]{:S(2)}, u32[]{:S(2)}) %collective-permute-start.2) | collective-permute-done | bytes 90144 | tf_op jit(solution)/shard_map/ppermute | solution.py:441
  62.7 0.0 collective-permute-done.1
  62.8 0.3 collective-permute-start.6
  63.1 2.1 %collective-permute-start.5 = (f32[88,256]{1,0:T(8,128)S(1)}, f32[88,256]{1,0:T(8,128)S(1)}, u32[]{:S(2)}, u32[]{:S(2)}) collective-permute-start(f32[88,256]{1,0:T(8,128)S(1)} %add_add_fusion.2), channel_id=1, source_target_pairs={{0,6},{1,7},{2,4},{3,5},{4,2},{5,3},{6,0},{7,1},{8,14},{9,15},{10,... | collective-permute-start | bytes 270344 | tf_op jit(solution)/shard_map/ppermute | solution.py:441
  65.2 1.5 %collective-permute-start.4 = (f32[88,256]{1,0:T(8,128)S(1)}, f32[88,256]{1,0:T(8,128)S(1)}, u32[]{:S(2)}, u32[]{:S(2)}) collective-permute-start(f32[88,256]{1,0:T(8,128)S(1)} %add_add_fusion.2), channel_id=1, source_target_pairs={{0,32},{1,33},{2,34},{3,35},{4,36},{5,37},{6,38},{7,39},{8,40},{9,... | collective-permute-start | bytes 270344 | tf_op jit(solution)/shard_map/ppermute | solution.py:441
  66.7 1.7 %collective-permute-done.6 = f32[88,256]{1,0:T(8,128)S(1)} collective-permute-done((f32[88,256]{1,0:T(8,128)S(1)}, f32[88,256]{1,0:T(8,128)S(1)}, u32[]{:S(2)}, u32[]{:S(2)}) %collective-permute-start.6) | collective-permute-done | bytes 90144 | tf_op jit(solution)/shard_map/ppermute | solution.py:441
  68.4 0.6 collective-permute-done.5
  69.0 0.6 collective-permute-done.4
  69.7 1.7 %collective-permute-start.9 = (f32[88,256]{1,0:T(8,128)S(1)}, f32[88,256]{1,0:T(8,128)S(1)}, u32[]{:S(2)}, u32[]{:S(2)}) collective-permute-start(f32[88,256]{1,0:T(8,128)S(1)} %add_add_fusion.1), channel_id=1, source_target_pairs={{0,120},{1,121},{2,122},{3,123},{4,124},{5,125},{6,126},{7,127},{8... | collective-permute-start | bytes 270344 | tf_op jit(solution)/shard_map/ppermute | solution.py:441
  71.4 2.9 %collective-permute-start.8 = (f32[88,256]{1,0:T(8,128)S(1)}, f32[88,256]{1,0:T(8,128)S(1)}, u32[]{:S(2)}, u32[]{:S(2)}) collective-permute-start(f32[88,256]{1,0:T(8,128)S(1)} %add_add_fusion.1), channel_id=1, source_target_pairs={{0,96},{1,97},{2,98},{3,99},{4,100},{5,101},{6,102},{7,103},{8,104... | collective-permute-start | bytes 270344 | tf_op jit(solution)/shard_map/ppermute | solution.py:441
  74.2 1.0 %collective-permute-start.7 = (f32[88,256]{1,0:T(8,128)S(1)}, f32[88,256]{1,0:T(8,128)S(1)}, u32[]{:S(2)}, u32[]{:S(2)}) collective-permute-start(f32[88,256]{1,0:T(8,128)S(1)} %add_add_fusion.1), channel_id=1, source_target_pairs={{0,24},{1,25},{2,26},{3,27},{4,28},{5,29},{6,30},{7,31},{8,16},{9,... | collective-permute-start | bytes 270344 | tf_op jit(solution)/shard_map/ppermute | solution.py:441
  75.2 1.2 %collective-permute-done.9 = f32[88,256]{1,0:T(8,128)S(1)} collective-permute-done((f32[88,256]{1,0:T(8,128)S(1)}, f32[88,256]{1,0:T(8,128)S(1)}, u32[]{:S(2)}, u32[]{:S(2)}) %collective-permute-start.9) | collective-permute-done | bytes 90144 | tf_op jit(solution)/shard_map/ppermute | solution.py:441
  76.5 0.7 collective-permute-done.8
  77.2 2.7 %collective-permute-done.7 = f32[88,256]{1,0:T(8,128)S(1)} collective-permute-done((f32[88,256]{1,0:T(8,128)S(1)}, f32[88,256]{1,0:T(8,128)S(1)}, u32[]{:S(2)}, u32[]{:S(2)}) %collective-permute-start.7) | collective-permute-done | bytes 90144 | tf_op jit(solution)/shard_map/ppermute | solution.py:441
  79.9 2.1 %collective-permute-start.10 = (f32[88,256]{1,0:T(8,128)S(1)}, f32[88,256]{1,0:T(8,128)S(1)}, u32[]{:S(2)}, u32[]{:S(2)}) collective-permute-start(f32[88,256]{1,0:T(8,128)S(1)} %add_add_fusion.mine_ref), channel_id=1, source_target_pairs={{0,1},{1,0},{2,3},{3,2},{4,5},{5,4},{6,7},{7,6},{8,9},{9,8},{10,11... | collective-permute-start | bytes 270344 | tf_op jit(solution)/shard_map/ppermute | solution.py:441
  82.0 0.9 collective-permute-done.10.other_ref
  82.9 0.0 copy-done
  83.0 12.9 %solve_and_apply.1 = bf16[8,2048,256]{2,1,0:T(8,128)(2,1)} custom-call(s32[1]{0:T(128)} %bitcast.core_ref, f32[88,256]{1,0:T(8,128)S(1)} %add_add_fusion.mine_ref, f32[88,256]{1,0:T(8,128)S(1)} %collective-permute-done.10.other_ref, f32[8,2048]{1,0:T(8,128)S(1)} %copy-done, bf16[8,2048,256]{2,1,0:T(8,128)(2,1)} %anom_ref.5), custom_call_target="tpu_custom_call" | custom-call | tf_op jit(solution)/shard_map/solve_and_apply/pallas_call | solution.py:421
  (4 shorter events, 0.1 us)
Async XLA Ops:
  0.0 14.4 %copy-start.2 = (f32[32768]{0:T(1024)S(1)}, f32[32768]{0:T(1024)}, u32[]{:S(2)}) copy-start(f32[32768]{0:T(1024)} %param.11) | copy-start | bytes 393220
  0.0 14.5 %copy-start.3 = (f32[32768]{0:T(1024)S(1)}, f32[32768]{0:T(1024)}, u32[]{:S(2)}) copy-start(f32[32768]{0:T(1024)} %param.12) | copy-start | bytes 393220
  6.1 28.2 %copy-start.1 = (s32[4096]{0:T(1024)S(1)}, s32[4096]{0:T(1024)}, u32[]{:S(2)}) copy-start(s32[4096]{0:T(1024)} %cols_ref.1) | copy-start | bytes 49156
  6.2 28.2 %all-to-all-start = ((bf16[384,8,256]{2,1,0:T(8,128)(2,1)}), bf16[384,8,256]{2,1,0:T(8,128)(2,1)S(1)}, u32[]{:S(2)}, u32[]{:S(2)}) async-start(bf16[384,8,256]{2,1,0:T(8,128)(2,1)} %gather_sent.1), calls=%async_computation | async-start | bytes 3145728 | tf_op jit(solution)/shard_map/all_to_all | solution.py:456
  34.4 48.6 %copy-start = (f32[8,2048]{1,0:T(8,128)S(1)}, f32[8,2048]{1,0:T(8,128)}, u32[]{:S(2)}) copy-start(f32[8,2048]{1,0:T(8,128)} %mean_ref.1) | copy-start | bytes 196612
  50.4 5.1 %collective-permute-start = (f32[88,256]{1,0:T(8,128)S(1)}, f32[88,256]{1,0:T(8,128)S(1)}, u32[]{:S(2)}, u32[]{:S(2)}) collective-permute-start(f32[88,256]{1,0:T(8,128)S(1)} %get-tuple-element.14), channel_id=1, source_target_pairs={{0,1},{1,0},{2,3},{3,2},{4,5},{5,4},{6,7},{7,6},{8,9},{9,8},{10,11... | collective-permute-start | bytes 270344 | tf_op jit(solution)/shard_map/ppermute | solution.py:441
  55.5 4.8 %collective-permute-start.3 = (f32[88,256]{1,0:T(8,128)S(1)}, f32[88,256]{1,0:T(8,128)S(1)}, u32[]{:S(2)}, u32[]{:S(2)}) collective-permute-start(f32[88,256]{1,0:T(8,128)S(1)} %add.35), channel_id=1, source_target_pairs={{0,10},{1,11},{2,8},{3,9},{4,14},{5,15},{6,12},{7,13},{8,2},{9,3},... | collective-permute-start | bytes 270344 | tf_op jit(solution)/shard_map/ppermute | solution.py:441
  55.6 7.1 %collective-permute-start.2 = (f32[88,256]{1,0:T(8,128)S(1)}, f32[88,256]{1,0:T(8,128)S(1)}, u32[]{:S(2)}, u32[]{:S(2)}) collective-permute-start(f32[88,256]{1,0:T(8,128)S(1)} %add.35), channel_id=1, source_target_pairs={{0,8},{1,9},{2,10},{3,11},{4,12},{5,13},{6,14},{7,15},{8,0},{9,1},... | collective-permute-start | bytes 270344 | tf_op jit(solution)/shard_map/ppermute | solution.py:441
  58.4 4.3 %collective-permute-start.1 = (f32[88,256]{1,0:T(8,128)S(1)}, f32[88,256]{1,0:T(8,128)S(1)}, u32[]{:S(2)}, u32[]{:S(2)}) collective-permute-start(f32[88,256]{1,0:T(8,128)S(1)} %add.35), channel_id=1, source_target_pairs={{0,2},{1,3},{2,0},{3,1},{4,6},{5,7},{6,4},{7,5},{8,10},{9,11},{10,... | collective-permute-start | bytes 270344 | tf_op jit(solution)/shard_map/ppermute | solution.py:441
  62.8 5.7 %collective-permute-start.6 = (f32[88,256]{1,0:T(8,128)S(1)}, f32[88,256]{1,0:T(8,128)S(1)}, u32[]{:S(2)}, u32[]{:S(2)}) collective-permute-start(f32[88,256]{1,0:T(8,128)S(1)} %add_add_fusion.2), channel_id=1, source_target_pairs={{0,38},{1,39},{2,36},{3,37},{4,34},{5,35},{6,32},{7,33},{8,46},{9,... | collective-permute-start | bytes 270344 | tf_op jit(solution)/shard_map/ppermute | solution.py:441
  63.1 6.0 %collective-permute-start.5 = (f32[88,256]{1,0:T(8,128)S(1)}, f32[88,256]{1,0:T(8,128)S(1)}, u32[]{:S(2)}, u32[]{:S(2)}) collective-permute-start(f32[88,256]{1,0:T(8,128)S(1)} %add_add_fusion.2), channel_id=1, source_target_pairs={{0,6},{1,7},{2,4},{3,5},{4,2},{5,3},{6,0},{7,1},{8,14},{9,15},{10,... | collective-permute-start | bytes 270344 | tf_op jit(solution)/shard_map/ppermute | solution.py:441
  65.2 4.5 %collective-permute-start.4 = (f32[88,256]{1,0:T(8,128)S(1)}, f32[88,256]{1,0:T(8,128)S(1)}, u32[]{:S(2)}, u32[]{:S(2)}) collective-permute-start(f32[88,256]{1,0:T(8,128)S(1)} %add_add_fusion.2), channel_id=1, source_target_pairs={{0,32},{1,33},{2,34},{3,35},{4,36},{5,37},{6,38},{7,39},{8,40},{9,... | collective-permute-start | bytes 270344 | tf_op jit(solution)/shard_map/ppermute | solution.py:441
  69.7 6.8 %collective-permute-start.9 = (f32[88,256]{1,0:T(8,128)S(1)}, f32[88,256]{1,0:T(8,128)S(1)}, u32[]{:S(2)}, u32[]{:S(2)}) collective-permute-start(f32[88,256]{1,0:T(8,128)S(1)} %add_add_fusion.1), channel_id=1, source_target_pairs={{0,120},{1,121},{2,122},{3,123},{4,124},{5,125},{6,126},{7,127},{8... | collective-permute-start | bytes 270344 | tf_op jit(solution)/shard_map/ppermute | solution.py:441
  71.4 5.8 %collective-permute-start.8 = (f32[88,256]{1,0:T(8,128)S(1)}, f32[88,256]{1,0:T(8,128)S(1)}, u32[]{:S(2)}, u32[]{:S(2)}) collective-permute-start(f32[88,256]{1,0:T(8,128)S(1)} %add_add_fusion.1), channel_id=1, source_target_pairs={{0,96},{1,97},{2,98},{3,99},{4,100},{5,101},{6,102},{7,103},{8,104... | collective-permute-start | bytes 270344 | tf_op jit(solution)/shard_map/ppermute | solution.py:441
  74.2 5.6 %collective-permute-start.7 = (f32[88,256]{1,0:T(8,128)S(1)}, f32[88,256]{1,0:T(8,128)S(1)}, u32[]{:S(2)}, u32[]{:S(2)}) collective-permute-start(f32[88,256]{1,0:T(8,128)S(1)} %add_add_fusion.1), channel_id=1, source_target_pairs={{0,24},{1,25},{2,26},{3,27},{4,28},{5,29},{6,30},{7,31},{8,16},{9,... | collective-permute-start | bytes 270344 | tf_op jit(solution)/shard_map/ppermute | solution.py:441
  79.9 3.1 %collective-permute-start.10 = (f32[88,256]{1,0:T(8,128)S(1)}, f32[88,256]{1,0:T(8,128)S(1)}, u32[]{:S(2)}, u32[]{:S(2)}) collective-permute-start(f32[88,256]{1,0:T(8,128)S(1)} %add_add_fusion.mine_ref), channel_id=1, source_target_pairs={{0,1},{1,0},{2,3},{3,2},{4,5},{5,4},{6,7},{7,6},{8,9},{9,8},{10,11... | collective-permute-start | bytes 270344 | tf_op jit(solution)/shard_map/ppermute | solution.py:441

commit v5 on v4

--- a/solution.py
+++ b/solution.py
@@ -23,7 +23,7 @@
     return high, middle, low
 
 
-def send_kernel(send_ref, anom_ref, out_ref, levels, table, sems):
+def send_kernel(send_ref, anom_ref, out_ref, levels, table, picked, sems, out_sems):
     col_dev = anom_ref.shape[1]
     slots = out_ref.shape[0]
     steps = sems.shape[0]
@@ -38,13 +38,17 @@
         part = slice(k * some, (k + 1) * some)
         table[part] = jnp.swapaxes(levels[:, part, :], 0, 1)
 
-    def pick(step, carried):
-        for i in range(64):
-            slot = step * 64 + i
-            out_ref[slot] = table[send_ref[0, slot]]
-        return carried
-
-    lax.fori_loop(0, slots // 64, pick, 0)
+    batch = slots // 6
+    stores = []
+    for k in range(6):
+        for i in range(batch):
+            slot = k * batch + i
+            picked[slot] = table[send_ref[0, slot]]
+        part = pl.ds(k * batch, batch)
+        stores.append(pltpu.make_async_copy(picked.at[part], out_ref.at[part], out_sems.at[k]))
+        stores[k].start()
+    for store in stores:
+        store.wait()
 
 
 def gather_sent(send_cols, anomalies):
@@ -53,12 +57,14 @@
     return pl.pallas_call(
         send_kernel,
         in_specs=[pl.BlockSpec(memory_space=pltpu.SMEM), pl.BlockSpec(memory_space=pl.ANY)],
-        out_specs=pl.BlockSpec(memory_space=pltpu.VMEM),
+        out_specs=pl.BlockSpec(memory_space=pl.ANY),
         out_shape=jax.ShapeDtypeStruct((slots, lev_dev, members), BF16),
         scratch_shapes=[
             pltpu.VMEM((lev_dev, col_dev, members), BF16),
             pltpu.VMEM((col_dev, lev_dev, members), BF16),
+            pltpu.VMEM((slots, lev_dev, members), BF16),
             pltpu.SemaphoreType.DMA((8,)),
+            pltpu.SemaphoreType.DMA((6,)),
         ],
         compiler_params=pltpu.CompilerParams(vmem_limit_bytes=60 << 20),
         name="gather_sent",
@@ -371,33 +377,40 @@
     identity = jnp.where(rows == lanes, 1.0, 0.0)
     system = gram + shift * identity
     norm = jnp.sqrt(jnp.sum(system * system, axis=(0, 1), keepdims=True))
-    approx_ref[...] = system / norm
-    inverse_ref[...] = identity
     lowest = jnp.minimum(jnp.sqrt(shift / norm), 1.0)[0, 0]
 
-    def advance(scale):
-        approx, inverse = approx_ref[...], inverse_ref[...]
-        middle = (1.5 * scale) * identity - (0.5 * scale * scale * scale) * dot3(inverse, approx)
-        approx_ref[...] = dot3(approx, middle)
-        inverse_ref[...] = dot3(middle, inverse)
+    def factor(scale, product):
+        return (1.5 * scale) * identity - (0.5 * scale * scale * scale) * product
+
+    def next_scale(low):
+        x = jnp.maximum(low, 0.02)
+        scale = 1.7323 + x * (-0.88804 + x * (-0.071549 + x * (0.385863 - 0.15965 * x)))
+        scale = jnp.maximum(scale, 1.0)
+        at_low = 0.5 * scale * low * (3.0 - scale * scale * low * low)
+        at_one = 0.5 * scale * (3.0 - scale * scale)
+        return scale, jnp.minimum(at_low, at_one)
 
     def more(carried):
         turn, low = carried
         return jnp.logical_and(turn < 60, low < 0.999)
 
-    def turn_once(carried):
+    def advance(carried):
         turn, low = carried
-        x = jnp.maximum(low, 0.02)
-        scale = 1.7323 + x * (-0.88804 + x * (-0.071549 + x * (0.385863 - 0.15965 * x)))
-        scale = jnp.maximum(scale, 1.0)
-        advance(scale)
-        at_low = 0.5 * scale * low * (3.0 - scale * scale * low * low)
-        at_one = 0.5 * scale * (3.0 - scale * scale)
-        return turn + 1, jnp.minimum(at_low, at_one)
-
-    lax.while_loop(more, turn_once, (jnp.int32(0), lowest))
-    advance(1.0)
+        scale, low = next_scale(low)
+        approx, inverse = approx_ref[...], inverse_ref[...]
+        middle = factor(scale, dot3(inverse, approx))
+        approx_ref[...] = dot3(approx, middle)
+        inverse_ref[...] = dot3(middle, inverse)
+        return turn + 1, low
+
+    start = system / norm
+    scale, lowest = next_scale(lowest)
+    middle = factor(scale, start)
+    approx_ref[...] = dot3(start, middle)
+    inverse_ref[...] = middle
+    lax.while_loop(more, advance, (jnp.int32(0), lowest))
     inverse = inverse_ref[...]
+    inverse = dot3(factor(1.0, dot3(inverse, approx_ref[...])), inverse)
     line = jnp.broadcast_to(projection, (128, members)).T
     weights = dot3(inverse, dot3(inverse, line)) / norm
     root = (jnp.sqrt((members - 1.0) / norm)) * inverse

time: 96 us -> 96.1 us (level)
  starting transfers between devices: 26.3 us -> 27.3 us
  transfers between devices with their start and end apart: 12 -> 12, of which waited for: 11 -> 10; matrix products, arithmetic and copies ran while one was open for 0% -> 0% of each run, Pallas kernels for 16% -> 16%
where the time goes in v5:
time: 96.1 us; the launch traced here: 95.8 us
  Pallas kernels  49.2 us (51%)
  starting transfers between devices  27.3 us (28%)
  waiting for transfers between devices  18.1 us (19%)
  between operations  0.97 us (1%)
    ppermute x11, starting transfers between devices, swap(): return lax.ppermute(value, AXES, [(d, d ^ mask) for d in range(devices)])  19.7 us
    pallas_call x1, Pallas kernels, gram_sums(): pl.pallas_call(gram_kernel, in_specs=[smem, smem, smem, anywhere, anywher...  16 us
    pallas_call x1, Pallas kernels, prepare(): pl.pallas_call(prepare_kernel, in_specs=[pl.BlockSpec(memory_space=pltpu....  14.9 us
    ppermute x11, waiting for transfers between devices, swap(): return lax.ppermute(value, AXES, [(d, d ^ mask) for d in range(devices)])  13.3 us
    pallas_call x1, Pallas kernels, solve_and_apply(): pl.pallas_call(apply_kernel, in_specs=[pl.BlockSpec(memory_space=pltpu.SM...  12.5 us
    all_to_all x1, starting transfers between devices, per_device(): lax.all_to_all(outgoing, 'tile', split_axis=0, concat_axis=0, tiled=True)  7.6 us
    pallas_call x1, Pallas kernels, gather_sent(): pl.pallas_call(send_kernel, in_specs=[pl.BlockSpec(memory_space=pltpu.SME...  5.79 us
    all_to_all x1, waiting for transfers between devices, per_device(): lax.all_to_all(outgoing, 'tile', split_axis=0, concat_axis=0, tiled=True)  4.8 us
  transfers between devices with their start and end apart: 12, of which 10 were waited for; matrix products, arithmetic and copies ran while one was open for 0% of the time, Pallas kernels for 16%

profile of v5, /device:TPU:1, one launch (start us, length us, event | category | flops | bytes accessed | tf_op | source)
XLA Modules:
  0.0 95.8 jit_solution(16110120138153431723)
XLA Ops:
  0.0 0.0 copy-start.2
  0.0 0.0 copy-start.3
  0.0 5.8 %gather_sent.1 = bf16[384,8,256]{2,1,0:T(8,128)(2,1)} custom-call(s32[1,384]{1,0:T(1,128)} %send_ref.1, bf16[8,2048,256]{2,1,0:T(8,128)(2,1)} %anom_ref.5), custom_call_target="tpu_custom_call" | custom-call | tf_op jit(solution)/shard_map/gather_sent/pallas_call | solution.py:57
  5.8 0.0 copy-start.1
  5.8 7.6 %all-to-all-start = ((bf16[384,8,256]{2,1,0:T(8,128)(2,1)}), bf16[384,8,256]{2,1,0:T(8,128)(2,1)S(1)}, u32[]{:S(2)}, u32[]{:S(2)}) async-start(bf16[384,8,256]{2,1,0:T(8,128)(2,1)} %gather_sent.1), calls=%async_computation | async-start | bytes 3145728 | tf_op jit(solution)/shard_map/all_to_all | solution.py:469
  14.1 0.0 copy-done.2
  14.1 0.1 reshape.11.innov_ref
  14.2 0.0 copy-done.3
  14.2 0.1 reshape.10.rinv_ref
  14.3 14.9 %prepare_operators.1 = (bf16[256,144,128]{2,1,0:T(8,128)(2,1)}, f32[8,256]{1,0:T(8,128)S(1)}, bf16[2048,8,256]{2,1,0:T(8,128)(2,1)}) custom-call(s32[1]{0:T(128)S(6)} %copy.9.count_ref, bf16[512,4096]{1,0:T(8,128)(2,1)} %op_ref.1, f32[512,64]{1,0:T(8,128)S(1)} %reshape.10.rinv_ref, f32[512,64]{1,0:T(8,128)S(1)} %reshape.11.innov_ref, ...), custom_call_target="tpu_custom_call" | custom-call | tf_op jit(solution)/shard_map/prepare_operators/pallas_call | solution.py:189
  29.3 4.8 %all-to-all-done.remote_ref = bf16[384,8,256]{2,1,0:T(8,128)(2,1)S(1)} async-done(((bf16[384,8,256]{2,1,0:T(8,128)(2,1)}), bf16[384,8,256]{2,1,0:T(8,128)(2,1)S(1)}, u32[]{:S(2)}, u32[]{:S(2)}) %all-to-all-start) | async-done | bytes 1572896 | tf_op jit(solution)/shard_map/all_to_all | solution.py:469
  34.0 0.0 copy-done.1
  34.1 0.0 copy-start
  34.1 16.0 %gram_sums.1 = (f32[88,256]{1,0:T(8,128)S(1)}, f32[88,256]{1,0:T(8,128)S(1)}) custom-call(s32[4096]{0:T(1024)S(1)} %copy-done.1, s32[1]{0:T(128)S(6)} %copy.9.count_ref, s32[1]{0:T(128)} %bitcast.core_ref, bf16[2048,8,256]{2,1,0:T(8,128)(2,1)} %get-tuple-element.10.own_ref, bf16[384,8,256]{2,1,0:T(8,128)(2,1)S(1)} %all-to-all-done.remote_ref, ...), custom_call_target="tpu_custom_call" | custom-call | tf_op jit(solution)/shard_map/gram_sums/pallas_call | solution.py:307
  50.1 0.1 collective-permute-start
  50.2 1.3 %collective-permute-done = f32[88,256]{1,0:T(8,128)S(1)} collective-permute-done((f32[88,256]{1,0:T(8,128)S(1)}, f32[88,256]{1,0:T(8,128)S(1)}, u32[]{:S(2)}, u32[]{:S(2)}) %collective-permute-start) | collective-permute-done | bytes 90144 | tf_op jit(solution)/shard_map/ppermute | solution.py:454
  51.4 1.8 %collective-permute-start.3 = (f32[88,256]{1,0:T(8,128)S(1)}, f32[88,256]{1,0:T(8,128)S(1)}, u32[]{:S(2)}, u32[]{:S(2)}) collective-permute-start(f32[88,256]{1,0:T(8,128)S(1)} %add.35), channel_id=1, source_target_pairs={{0,10},{1,11},{2,8},{3,9},{4,14},{5,15},{6,12},{7,13},{8,2},{9,3},... | collective-permute-start | bytes 270344 | tf_op jit(solution)/shard_map/ppermute | solution.py:454
  53.2 0.0 collective-permute-start.2
  53.2 1.0 %collective-permute-start.1 = (f32[88,256]{1,0:T(8,128)S(1)}, f32[88,256]{1,0:T(8,128)S(1)}, u32[]{:S(2)}, u32[]{:S(2)}) collective-permute-start(f32[88,256]{1,0:T(8,128)S(1)} %add.35), channel_id=1, source_target_pairs={{0,2},{1,3},{2,0},{3,1},{4,6},{5,7},{6,4},{7,5},{8,10},{9,11},{10,... | collective-permute-start | bytes 270344 | tf_op jit(solution)/shard_map/ppermute | solution.py:454
  54.2 2.3 %collective-permute-done.3 = f32[88,256]{1,0:T(8,128)S(1)} collective-permute-done((f32[88,256]{1,0:T(8,128)S(1)}, f32[88,256]{1,0:T(8,128)S(1)}, u32[]{:S(2)}, u32[]{:S(2)}) %collective-permute-start.3) | collective-permute-done | bytes 90144 | tf_op jit(solution)/shard_map/ppermute | solution.py:454
  56.5 0.6 collective-permute-done.2
  57.1 1.7 %collective-permute-done.1 = f32[88,256]{1,0:T(8,128)S(1)} collective-permute-done((f32[88,256]{1,0:T(8,128)S(1)}, f32[88,256]{1,0:T(8,128)S(1)}, u32[]{:S(2)}, u32[]{:S(2)}) %collective-permute-start.1) | collective-permute-done | bytes 90144 | tf_op jit(solution)/shard_map/ppermute | solution.py:454
  58.9 4.9 %collective-permute-start.6 = (f32[88,256]{1,0:T(8,128)S(1)}, f32[88,256]{1,0:T(8,128)S(1)}, u32[]{:S(2)}, u32[]{:S(2)}) collective-permute-start(f32[88,256]{1,0:T(8,128)S(1)} %add_add_fusion.2), channel_id=1, source_target_pairs={{0,38},{1,39},{2,36},{3,37},{4,34},{5,35},{6,32},{7,33},{8,46},{9,... | collective-permute-start | bytes 270344 | tf_op jit(solution)/shard_map/ppermute | solution.py:454
  63.7 2.8 %collective-permute-start.5 = (f32[88,256]{1,0:T(8,128)S(1)}, f32[88,256]{1,0:T(8,128)S(1)}, u32[]{:S(2)}, u32[]{:S(2)}) collective-permute-start(f32[88,256]{1,0:T(8,128)S(1)} %add_add_fusion.2), channel_id=1, source_target_pairs={{0,6},{1,7},{2,4},{3,5},{4,2},{5,3},{6,0},{7,1},{8,14},{9,15},{10,... | collective-permute-start | bytes 270344 | tf_op jit(solution)/shard_map/ppermute | solution.py:454
  66.6 1.1 %collective-permute-start.4 = (f32[88,256]{1,0:T(8,128)S(1)}, f32[88,256]{1,0:T(8,128)S(1)}, u32[]{:S(2)}, u32[]{:S(2)}) collective-permute-start(f32[88,256]{1,0:T(8,128)S(1)} %add_add_fusion.2), channel_id=1, source_target_pairs={{0,32},{1,33},{2,34},{3,35},{4,36},{5,37},{6,38},{7,39},{8,40},{9,... | collective-permute-start | bytes 270344 | tf_op jit(solution)/shard_map/ppermute | solution.py:454
  67.7 0.0 collective-permute-done.6
  67.7 0.8 collective-permute-done.5
  68.5 3.0 %collective-permute-done.4 = f32[88,256]{1,0:T(8,128)S(1)} collective-permute-done((f32[88,256]{1,0:T(8,128)S(1)}, f32[88,256]{1,0:T(8,128)S(1)}, u32[]{:S(2)}, u32[]{:S(2)}) %collective-permute-start.4) | collective-permute-done | bytes 90144 | tf_op jit(solution)/shard_map/ppermute | solution.py:454
  71.6 0.1 collective-permute-start.9
  71.7 1.5 %collective-permute-start.8 = (f32[88,256]{1,0:T(8,128)S(1)}, f32[88,256]{1,0:T(8,128)S(1)}, u32[]{:S(2)}, u32[]{:S(2)}) collective-permute-start(f32[88,256]{1,0:T(8,128)S(1)} %add_add_fusion.1), channel_id=1, source_target_pairs={{0,96},{1,97},{2,98},{3,99},{4,100},{5,101},{6,102},{7,103},{8,104... | collective-permute-start | bytes 270344 | tf_op jit(solution)/shard_map/ppermute | solution.py:454
  73.2 3.5 %collective-permute-start.7 = (f32[88,256]{1,0:T(8,128)S(1)}, f32[88,256]{1,0:T(8,128)S(1)}, u32[]{:S(2)}, u32[]{:S(2)}) collective-permute-start(f32[88,256]{1,0:T(8,128)S(1)} %add_add_fusion.1), channel_id=1, source_target_pairs={{0,24},{1,25},{2,26},{3,27},{4,28},{5,29},{6,30},{7,31},{8,16},{9,... | collective-permute-start | bytes 270344 | tf_op jit(solution)/shard_map/ppermute | solution.py:454
  76.7 1.7 %collective-permute-done.9 = f32[88,256]{1,0:T(8,128)S(1)} collective-permute-done((f32[88,256]{1,0:T(8,128)S(1)}, f32[88,256]{1,0:T(8,128)S(1)}, u32[]{:S(2)}, u32[]{:S(2)}) %collective-permute-start.9) | collective-permute-done | bytes 90144 | tf_op jit(solution)/shard_map/ppermute | solution.py:454
  78.4 0.0 collective-permute-done.8
  78.4 0.9 collective-permute-done.7
  79.3 2.9 %collective-permute-start.10 = (f32[88,256]{1,0:T(8,128)S(1)}, f32[88,256]{1,0:T(8,128)S(1)}, u32[]{:S(2)}, u32[]{:S(2)}) collective-permute-start(f32[88,256]{1,0:T(8,128)S(1)} %add_add_fusion.mine_ref), channel_id=1, source_target_pairs={{0,1},{1,0},{2,3},{3,2},{4,5},{5,4},{6,7},{7,6},{8,9},{9,8},{10,11... | collective-permute-start | bytes 270344 | tf_op jit(solution)/shard_map/ppermute | solution.py:454
  82.2 0.9 collective-permute-done.10.other_ref
  83.2 0.0 copy-done
  83.2 12.5 %solve_and_apply.1 = bf16[8,2048,256]{2,1,0:T(8,128)(2,1)} custom-call(s32[1]{0:T(128)} %bitcast.core_ref, f32[88,256]{1,0:T(8,128)S(1)} %add_add_fusion.mine_ref, f32[88,256]{1,0:T(8,128)S(1)} %collective-permute-done.10.other_ref, f32[8,2048]{1,0:T(8,128)S(1)} %copy-done, bf16[8,2048,256]{2,1,0:T(8,128)(2,1)} %anom_ref.5), custom_call_target="tpu_custom_call" | custom-call | tf_op jit(solution)/shard_map/solve_and_apply/pallas_call | solution.py:434
  (4 shorter events, 0.1 us)
Async XLA Ops:
  0.0 14.1 %copy-start.2 = (f32[32768]{0:T(1024)S(1)}, f32[32768]{0:T(1024)}, u32[]{:S(2)}) copy-start(f32[32768]{0:T(1024)} %param.11) | copy-start | bytes 393220
  0.0 14.2 %copy-start.3 = (f32[32768]{0:T(1024)S(1)}, f32[32768]{0:T(1024)}, u32[]{:S(2)}) copy-start(f32[32768]{0:T(1024)} %param.12) | copy-start | bytes 393220
  5.8 28.2 %copy-start.1 = (s32[4096]{0:T(1024)S(1)}, s32[4096]{0:T(1024)}, u32[]{:S(2)}) copy-start(s32[4096]{0:T(1024)} %cols_ref.1) | copy-start | bytes 49156
  5.8 28.2 %all-to-all-start = ((bf16[384,8,256]{2,1,0:T(8,128)(2,1)}), bf16[384,8,256]{2,1,0:T(8,128)(2,1)S(1)}, u32[]{:S(2)}, u32[]{:S(2)}) async-start(bf16[384,8,256]{2,1,0:T(8,128)(2,1)} %gather_sent.1), calls=%async_computation | async-start | bytes 3145728 | tf_op jit(solution)/shard_map/all_to_all | solution.py:469
  34.1 49.1 %copy-start = (f32[8,2048]{1,0:T(8,128)S(1)}, f32[8,2048]{1,0:T(8,128)}, u32[]{:S(2)}) copy-start(f32[8,2048]{1,0:T(8,128)} %mean_ref.1) | copy-start | bytes 196612
  50.1 1.4 %collective-permute-start = (f32[88,256]{1,0:T(8,128)S(1)}, f32[88,256]{1,0:T(8,128)S(1)}, u32[]{:S(2)}, u32[]{:S(2)}) collective-permute-start(f32[88,256]{1,0:T(8,128)S(1)} %get-tuple-element.14), channel_id=1, source_target_pairs={{0,1},{1,0},{2,3},{3,2},{4,5},{5,4},{6,7},{7,6},{8,9},{9,8},{10,11... | collective-permute-start | bytes 270344 | tf_op jit(solution)/shard_map/ppermute | solution.py:454
  51.4 5.1 %collective-permute-start.3 = (f32[88,256]{1,0:T(8,128)S(1)}, f32[88,256]{1,0:T(8,128)S(1)}, u32[]{:S(2)}, u32[]{:S(2)}) collective-permute-start(f32[88,256]{1,0:T(8,128)S(1)} %add.35), channel_id=1, source_target_pairs={{0,10},{1,11},{2,8},{3,9},{4,14},{5,15},{6,12},{7,13},{8,2},{9,3},... | collective-permute-start | bytes 270344 | tf_op jit(solution)/shard_map/ppermute | solution.py:454
  53.2 3.9 %collective-permute-start.2 = (f32[88,256]{1,0:T(8,128)S(1)}, f32[88,256]{1,0:T(8,128)S(1)}, u32[]{:S(2)}, u32[]{:S(2)}) collective-permute-start(f32[88,256]{1,0:T(8,128)S(1)} %add.35), channel_id=1, source_target_pairs={{0,8},{1,9},{2,10},{3,11},{4,12},{5,13},{6,14},{7,15},{8,0},{9,1},... | collective-permute-start | bytes 270344 | tf_op jit(solution)/shard_map/ppermute | solution.py:454
  53.2 5.6 %collective-permute-start.1 = (f32[88,256]{1,0:T(8,128)S(1)}, f32[88,256]{1,0:T(8,128)S(1)}, u32[]{:S(2)}, u32[]{:S(2)}) collective-permute-start(f32[88,256]{1,0:T(8,128)S(1)} %add.35), channel_id=1, source_target_pairs={{0,2},{1,3},{2,0},{3,1},{4,6},{5,7},{6,4},{7,5},{8,10},{9,11},{10,... | collective-permute-start | bytes 270344 | tf_op jit(solution)/shard_map/ppermute | solution.py:454
  58.9 8.8 %collective-permute-start.6 = (f32[88,256]{1,0:T(8,128)S(1)}, f32[88,256]{1,0:T(8,128)S(1)}, u32[]{:S(2)}, u32[]{:S(2)}) collective-permute-start(f32[88,256]{1,0:T(8,128)S(1)} %add_add_fusion.2), channel_id=1, source_target_pairs={{0,38},{1,39},{2,36},{3,37},{4,34},{5,35},{6,32},{7,33},{8,46},{9,... | collective-permute-start | bytes 270344 | tf_op jit(solution)/shard_map/ppermute | solution.py:454
  63.7 4.8 %collective-permute-start.5 = (f32[88,256]{1,0:T(8,128)S(1)}, f32[88,256]{1,0:T(8,128)S(1)}, u32[]{:S(2)}, u32[]{:S(2)}) collective-permute-start(f32[88,256]{1,0:T(8,128)S(1)} %add_add_fusion.2), channel_id=1, source_target_pairs={{0,6},{1,7},{2,4},{3,5},{4,2},{5,3},{6,0},{7,1},{8,14},{9,15},{10,... | collective-permute-start | bytes 270344 | tf_op jit(solution)/shard_map/ppermute | solution.py:454
  66.6 5.0 %collective-permute-start.4 = (f32[88,256]{1,0:T(8,128)S(1)}, f32[88,256]{1,0:T(8,128)S(1)}, u32[]{:S(2)}, u32[]{:S(2)}) collective-permute-start(f32[88,256]{1,0:T(8,128)S(1)} %add_add_fusion.2), channel_id=1, source_target_pairs={{0,32},{1,33},{2,34},{3,35},{4,36},{5,37},{6,38},{7,39},{8,40},{9,... | collective-permute-start | bytes 270344 | tf_op jit(solution)/shard_map/ppermute | solution.py:454
  71.6 6.8 %collective-permute-start.9 = (f32[88,256]{1,0:T(8,128)S(1)}, f32[88,256]{1,0:T(8,128)S(1)}, u32[]{:S(2)}, u32[]{:S(2)}) collective-permute-start(f32[88,256]{1,0:T(8,128)S(1)} %add_add_fusion.1), channel_id=1, source_target_pairs={{0,120},{1,121},{2,122},{3,123},{4,124},{5,125},{6,126},{7,127},{8... | collective-permute-start | bytes 270344 | tf_op jit(solution)/shard_map/ppermute | solution.py:454
  71.7 6.7 %collective-permute-start.8 = (f32[88,256]{1,0:T(8,128)S(1)}, f32[88,256]{1,0:T(8,128)S(1)}, u32[]{:S(2)}, u32[]{:S(2)}) collective-permute-start(f32[88,256]{1,0:T(8,128)S(1)} %add_add_fusion.1), channel_id=1, source_target_pairs={{0,96},{1,97},{2,98},{3,99},{4,100},{5,101},{6,102},{7,103},{8,104... | collective-permute-start | bytes 270344 | tf_op jit(solution)/shard_map/ppermute | solution.py:454
  73.2 6.1 %collective-permute-start.7 = (f32[88,256]{1,0:T(8,128)S(1)}, f32[88,256]{1,0:T(8,128)S(1)}, u32[]{:S(2)}, u32[]{:S(2)}) collective-permute-start(f32[88,256]{1,0:T(8,128)S(1)} %add_add_fusion.1), channel_id=1, source_target_pairs={{0,24},{1,25},{2,26},{3,27},{4,28},{5,29},{6,30},{7,31},{8,16},{9,... | collective-permute-start | bytes 270344 | tf_op jit(solution)/shard_map/ppermute | solution.py:454
  79.3 3.8 %collective-permute-start.10 = (f32[88,256]{1,0:T(8,128)S(1)}, f32[88,256]{1,0:T(8,128)S(1)}, u32[]{:S(2)}, u32[]{:S(2)}) collective-permute-start(f32[88,256]{1,0:T(8,128)S(1)} %add_add_fusion.mine_ref), channel_id=1, source_target_pairs={{0,1},{1,0},{2,3},{3,2},{4,5},{5,4},{6,7},{7,6},{8,9},{9,8},{10,11... | collective-permute-start | bytes 270344 | tf_op jit(solution)/shard_map/ppermute | solution.py:454

commit v6 on v5

--- a/solution.py
+++ b/solution.py
@@ -12,7 +12,7 @@
 AXES = ("tile", "lev")
 GROUP = 128
 CHUNK = 64
-PACK = 88
+PACK = 72
 
 
 def split3(value):
@@ -276,16 +276,20 @@
     lax.fori_loop(0, groups, step, 0)
 
     projection = pulled[0:1, :] + pulled[1:2, :] + pulled[2:3, :]
-    row = lax.broadcasted_iota(jnp.int32, (8, 256), 0)
-    ending = jnp.where(row == 0, projection, jnp.where(row == 1, sums_ref[...], 0.0))
-    zeros = jnp.zeros((8, 256), F32)
-    last = pltpu.roll(total[192:256, 128:256], 64, 1)
-    low_half = lax.broadcasted_iota(jnp.int32, (64, 128), 1) < 64
-    side = jnp.where(low_half, last, total[64:128, 0:128])
-    side = jnp.concatenate([side, total[64:128, 128:256]], axis=1)
-    corner = jnp.concatenate([total[128:160, 128:256], total[160:192, 128:256]], axis=1)
-    first = jnp.concatenate([total[0:64, :], side[: PACK - 64]], axis=0)
-    second = jnp.concatenate([side[PACK - 64 :], corner, ending, zeros], axis=0)
+    rows = lax.broadcasted_iota(jnp.int32, (128, 128), 0)
+    lanes = lax.broadcasted_iota(jnp.int32, (128, 128), 1)
+    corner = total[128:256, 128:256]
+    left = jnp.where(lanes >= rows, total[0:128, 0:128], corner)
+    diagonal = jnp.sum(jnp.where(lanes == rows, corner, 0.0), axis=0, keepdims=True)
+    diagonal = jnp.concatenate([diagonal, jnp.zeros((1, 128), F32)], axis=1)
+    row = lax.broadcasted_iota(jnp.int32, (16, 256), 0)
+    sums = jnp.concatenate([sums_ref[...], sums_ref[...]], axis=0)
+    ending = jnp.where(row == 2, sums, 0.0)
+    ending = jnp.where(row == 1, diagonal, ending)
+    ending = jnp.where(row == 0, projection, ending)
+    packed = jnp.concatenate([left, total[0:128, 128:256]], axis=1)
+    first = packed[0:PACK]
+    second = jnp.concatenate([packed[PACK:128], ending], axis=0)
     core = core_ref[0]
 
     @pl.when(core == 0)
@@ -353,23 +357,24 @@
     packed = jnp.concatenate(
         [jnp.where(core == 0, mine, other), jnp.where(core == 0, other, mine)], axis=0
     )
-    side = packed[64:128]
-    corner = jnp.concatenate([packed[128:160, :128], packed[128:160, 128:]], axis=0)
-    corner = jnp.concatenate([corner, pltpu.roll(side[:, :128], 64, 1)], axis=0)
-    corner = jnp.concatenate([jnp.zeros((128, 128), F32), corner], axis=1)
-    upper = jnp.concatenate([packed[0:128], corner], axis=0)
-    lower = upper.T
+    half_rows = lax.broadcasted_iota(jnp.int32, (128, 128), 0)
+    half_lanes = lax.broadcasted_iota(jnp.int32, (128, 128), 1)
+    left, right = packed[0:128, 0:128], packed[0:128, 128:256]
+    turned = left.T
+    first = jnp.where(half_lanes >= half_rows, left, turned)
+    last = jnp.where(half_lanes > half_rows, turned, left)
+    last = jnp.where(half_lanes == half_rows, packed[129:130, 0:128], last)
+    gram = jnp.concatenate(
+        [
+            jnp.concatenate([first, right], axis=1),
+            jnp.concatenate([right.T, last], axis=1),
+        ],
+        axis=0,
+    )
+    projection = packed[128:129]
+    sums = packed[130:131]
     rows = lax.broadcasted_iota(jnp.int32, (members, members), 0)
     lanes = lax.broadcasted_iota(jnp.int32, (members, members), 1)
-    row_block = lax.shift_right_logical(rows, 6)
-    lane_block = lax.shift_right_logical(lanes, 6)
-    gram = jnp.where(
-        lane_block > row_block,
-        upper,
-        jnp.where(lane_block < row_block, lower, 0.5 * (upper + lower)),
-    )
-    projection = packed[160:161]
-    sums = packed[161:162]
     means[...] = mean_ref[...].T
 
     numerator, obs_total = sums[:, 0:1], sums[:, 1:2]

time: 96.1 us -> 93.9 us (0.977)
  Pallas kernels: 49.2 us -> 43.7 us
  starting transfers between devices: 27.3 us -> 32.8 us
  waiting for transfers between devices: 18.1 us -> 15.4 us
    ppermute x11, starting transfers between devices: 19.7 us -> 25.2 us  [swap(): return lax.ppermute(value, AXES, [(d, d ^ mask) for d in range(devices)])]
    pallas_call x1, Pallas kernels: 16 us -> 10.5 us  [gram_sums(): pl.pallas_call(gram_kernel, in_specs=[smem, smem, smem, anywhere, anywher...]
    ppermute x11, waiting for transfers between devices: 13.3 us -> 10.6 us  [swap(): return lax.ppermute(value, AXES, [(d, d ^ mask) for d in range(devices)])]
  transfers between devices with their start and end apart: 12 -> 12, of which waited for: 10 -> 9; matrix products, arithmetic and copies ran while one was open for 0% -> 0% of each run, Pallas kernels for 16% -> 16%
where the time goes in v6:
time: 93.9 us; the launch traced here: 93.1 us
  Pallas kernels  43.7 us (47%)
  starting transfers between devices  32.8 us (35%)
  waiting for transfers between devices  15.4 us (16%)
  between operations  0.97 us (1%)
    ppermute x11, starting transfers between devices, swap(): return lax.ppermute(value, AXES, [(d, d ^ mask) for d in range(devices)])  25.2 us
    pallas_call x1, Pallas kernels, prepare(): pl.pallas_call(prepare_kernel, in_specs=[pl.BlockSpec(memory_space=pltpu....  14.9 us
    pallas_call x1, Pallas kernels, solve_and_apply(): pl.pallas_call(apply_kernel, in_specs=[pl.BlockSpec(memory_space=pltpu.SM...  12.5 us
    ppermute x11, waiting for transfers between devices, swap(): return lax.ppermute(value, AXES, [(d, d ^ mask) for d in range(devices)])  10.6 us
    pallas_call x1, Pallas kernels, gram_sums(): pl.pallas_call(gram_kernel, in_specs=[smem, smem, smem, anywhere, anywher...  10.5 us
    all_to_all x1, starting transfers between devices, per_device(): lax.all_to_all(outgoing, 'tile', split_axis=0, concat_axis=0, tiled=True)  7.6 us
    pallas_call x1, Pallas kernels, gather_sent(): pl.pallas_call(send_kernel, in_specs=[pl.BlockSpec(memory_space=pltpu.SME...  5.79 us
    all_to_all x1, waiting for transfers between devices, per_device(): lax.all_to_all(outgoing, 'tile', split_axis=0, concat_axis=0, tiled=True)  4.8 us
  transfers between devices with their start and end apart: 12, of which 9 were waited for; matrix products, arithmetic and copies ran while one was open for 0% of the time, Pallas kernels for 16%

profile of v6, /device:TPU:1, one launch (start us, length us, event | category | flops | bytes accessed | tf_op | source)
XLA Modules:
  0.0 93.1 jit_solution(17208396665559389568)
XLA Ops:
  0.0 0.0 copy-start.2
  0.0 0.0 copy-start.3
  0.0 5.8 %gather_sent.1 = bf16[384,8,256]{2,1,0:T(8,128)(2,1)} custom-call(s32[1,384]{1,0:T(1,128)} %send_ref.1, bf16[8,2048,256]{2,1,0:T(8,128)(2,1)} %anom_ref.5), custom_call_target="tpu_custom_call" | custom-call | tf_op jit(solution)/shard_map/gather_sent/pallas_call | solution.py:57
  5.8 0.0 copy-start.1
  5.8 7.6 %all-to-all-start = ((bf16[384,8,256]{2,1,0:T(8,128)(2,1)}), bf16[384,8,256]{2,1,0:T(8,128)(2,1)S(1)}, u32[]{:S(2)}, u32[]{:S(2)}) async-start(bf16[384,8,256]{2,1,0:T(8,128)(2,1)} %gather_sent.1), calls=%async_computation | async-start | bytes 3145728 | tf_op jit(solution)/shard_map/all_to_all | solution.py:474
  14.1 0.0 copy-done.2
  14.1 0.1 reshape.11.innov_ref
  14.2 0.0 copy-done.3
  14.2 0.1 reshape.10.rinv_ref
  14.3 14.9 %prepare_operators.1 = (bf16[256,144,128]{2,1,0:T(8,128)(2,1)}, f32[8,256]{1,0:T(8,128)S(1)}, bf16[2048,8,256]{2,1,0:T(8,128)(2,1)}) custom-call(s32[1]{0:T(128)S(6)} %copy.9.count_ref, bf16[512,4096]{1,0:T(8,128)(2,1)} %op_ref.1, f32[512,64]{1,0:T(8,128)S(1)} %reshape.10.rinv_ref, f32[512,64]{1,0:T(8,128)S(1)} %reshape.11.innov_ref, ...), custom_call_target="tpu_custom_call" | custom-call | tf_op jit(solution)/shard_map/prepare_operators/pallas_call | solution.py:189
  29.3 4.8 %all-to-all-done.remote_ref = bf16[384,8,256]{2,1,0:T(8,128)(2,1)S(1)} async-done(((bf16[384,8,256]{2,1,0:T(8,128)(2,1)}), bf16[384,8,256]{2,1,0:T(8,128)(2,1)S(1)}, u32[]{:S(2)}, u32[]{:S(2)}) %all-to-all-start) | async-done | bytes 1572896 | tf_op jit(solution)/shard_map/all_to_all | solution.py:474
  34.0 0.0 copy-done.1
  34.1 0.0 copy-start
  34.1 10.5 %gram_sums.1 = (f32[72,256]{1,0:T(8,128)S(1)}, f32[72,256]{1,0:T(8,128)S(1)}) custom-call(s32[4096]{0:T(1024)S(1)} %copy-done.1, s32[1]{0:T(128)S(6)} %copy.9.count_ref, s32[1]{0:T(128)} %bitcast.core_ref, bf16[2048,8,256]{2,1,0:T(8,128)(2,1)} %get-tuple-element.10.own_ref, bf16[384,8,256]{2,1,0:T(8,128)(2,1)S(1)} %all-to-all-done.remote_ref, ...), custom_call_target="tpu_custom_call" | custom-call | tf_op jit(solution)/shard_map/gram_sums/pallas_call | solution.py:311
  44.5 9.7 %collective-permute-start = (f32[72,256]{1,0:T(8,128)S(1)}, f32[72,256]{1,0:T(8,128)S(1)}, u32[]{:S(2)}, u32[]{:S(2)}) collective-permute-start(f32[72,256]{1,0:T(8,128)S(1)} %get-tuple-element.14), channel_id=1, source_target_pairs={{0,1},{1,0},{2,3},{3,2},{4,5},{5,4},{6,7},{7,6},{8,9},{9,8},{10,11... | collective-permute-start | bytes 221192 | tf_op jit(solution)/shard_map/ppermute | solution.py:459
  54.2 0.9 collective-permute-done
  55.1 0.1 collective-permute-start.3
  55.2 0.1 collective-permute-start.2
  55.3 2.5 %collective-permute-start.1 = (f32[72,256]{1,0:T(8,128)S(1)}, f32[72,256]{1,0:T(8,128)S(1)}, u32[]{:S(2)}, u32[]{:S(2)}) collective-permute-start(f32[72,256]{1,0:T(8,128)S(1)} %add.35), channel_id=1, source_target_pairs={{0,2},{1,3},{2,0},{3,1},{4,6},{5,7},{6,4},{7,5},{8,10},{9,11},{10,... | collective-permute-start | bytes 221192 | tf_op jit(solution)/shard_map/ppermute | solution.py:459
  57.8 1.5 %collective-permute-done.3 = f32[72,256]{1,0:T(8,128)S(1)} collective-permute-done((f32[72,256]{1,0:T(8,128)S(1)}, f32[72,256]{1,0:T(8,128)S(1)}, u32[]{:S(2)}, u32[]{:S(2)}) %collective-permute-start.3) | collective-permute-done | bytes 73760 | tf_op jit(solution)/shard_map/ppermute | solution.py:459
  59.4 0.0 collective-permute-done.2
  59.4 2.3 %collective-permute-done.1 = f32[72,256]{1,0:T(8,128)S(1)} collective-permute-done((f32[72,256]{1,0:T(8,128)S(1)}, f32[72,256]{1,0:T(8,128)S(1)}, u32[]{:S(2)}, u32[]{:S(2)}) %collective-permute-start.1) | collective-permute-done | bytes 73760 | tf_op jit(solution)/shard_map/ppermute | solution.py:459
  61.7 0.1 collective-permute-start.6
  61.8 2.0 %collective-permute-start.5 = (f32[72,256]{1,0:T(8,128)S(1)}, f32[72,256]{1,0:T(8,128)S(1)}, u32[]{:S(2)}, u32[]{:S(2)}) collective-permute-start(f32[72,256]{1,0:T(8,128)S(1)} %add_add_fusion.2), channel_id=1, source_target_pairs={{0,6},{1,7},{2,4},{3,5},{4,2},{5,3},{6,0},{7,1},{8,14},{9,15},{10,... | collective-permute-start | bytes 221192 | tf_op jit(solution)/shard_map/ppermute | solution.py:459
  63.8 1.9 %collective-permute-start.4 = (f32[72,256]{1,0:T(8,128)S(1)}, f32[72,256]{1,0:T(8,128)S(1)}, u32[]{:S(2)}, u32[]{:S(2)}) collective-permute-start(f32[72,256]{1,0:T(8,128)S(1)} %add_add_fusion.2), channel_id=1, source_target_pairs={{0,32},{1,33},{2,34},{3,35},{4,36},{5,37},{6,38},{7,39},{8,40},{9,... | collective-permute-start | bytes 221192 | tf_op jit(solution)/shard_map/ppermute | solution.py:459
  65.6 1.5 %collective-permute-done.6 = f32[72,256]{1,0:T(8,128)S(1)} collective-permute-done((f32[72,256]{1,0:T(8,128)S(1)}, f32[72,256]{1,0:T(8,128)S(1)}, u32[]{:S(2)}, u32[]{:S(2)}) %collective-permute-start.6) | collective-permute-done | bytes 73760 | tf_op jit(solution)/shard_map/ppermute | solution.py:459
  67.1 0.0 collective-permute-done.5
  67.1 0.6 collective-permute-done.4
  67.7 2.1 %collective-permute-start.9 = (f32[72,256]{1,0:T(8,128)S(1)}, f32[72,256]{1,0:T(8,128)S(1)}, u32[]{:S(2)}, u32[]{:S(2)}) collective-permute-start(f32[72,256]{1,0:T(8,128)S(1)} %add_add_fusion.1), channel_id=1, source_target_pairs={{0,120},{1,121},{2,122},{3,123},{4,124},{5,125},{6,126},{7,127},{8... | collective-permute-start | bytes 221192 | tf_op jit(solution)/shard_map/ppermute | solution.py:459
  69.8 1.6 %collective-permute-start.8 = (f32[72,256]{1,0:T(8,128)S(1)}, f32[72,256]{1,0:T(8,128)S(1)}, u32[]{:S(2)}, u32[]{:S(2)}) collective-permute-start(f32[72,256]{1,0:T(8,128)S(1)} %add_add_fusion.1), channel_id=1, source_target_pairs={{0,96},{1,97},{2,98},{3,99},{4,100},{5,101},{6,102},{7,103},{8,104... | collective-permute-start | bytes 221192 | tf_op jit(solution)/shard_map/ppermute | solution.py:459
  71.3 1.5 %collective-permute-start.7 = (f32[72,256]{1,0:T(8,128)S(1)}, f32[72,256]{1,0:T(8,128)S(1)}, u32[]{:S(2)}, u32[]{:S(2)}) collective-permute-start(f32[72,256]{1,0:T(8,128)S(1)} %add_add_fusion.1), channel_id=1, source_target_pairs={{0,24},{1,25},{2,26},{3,27},{4,28},{5,29},{6,30},{7,31},{8,16},{9,... | collective-permute-start | bytes 221192 | tf_op jit(solution)/shard_map/ppermute | solution.py:459
  72.9 1.5 %collective-permute-done.9 = f32[72,256]{1,0:T(8,128)S(1)} collective-permute-done((f32[72,256]{1,0:T(8,128)S(1)}, f32[72,256]{1,0:T(8,128)S(1)}, u32[]{:S(2)}, u32[]{:S(2)}) %collective-permute-start.9) | collective-permute-done | bytes 73760 | tf_op jit(solution)/shard_map/ppermute | solution.py:459
  74.3 0.0 collective-permute-done.8
  74.3 1.4 %collective-permute-done.7 = f32[72,256]{1,0:T(8,128)S(1)} collective-permute-done((f32[72,256]{1,0:T(8,128)S(1)}, f32[72,256]{1,0:T(8,128)S(1)}, u32[]{:S(2)}, u32[]{:S(2)}) %collective-permute-start.7) | collective-permute-done | bytes 73760 | tf_op jit(solution)/shard_map/ppermute | solution.py:459
  75.8 3.8 %collective-permute-start.10 = (f32[72,256]{1,0:T(8,128)S(1)}, f32[72,256]{1,0:T(8,128)S(1)}, u32[]{:S(2)}, u32[]{:S(2)}) collective-permute-start(f32[72,256]{1,0:T(8,128)S(1)} %add_add_fusion.mine_ref), channel_id=1, source_target_pairs={{0,1},{1,0},{2,3},{3,2},{4,5},{5,4},{6,7},{7,6},{8,9},{9,8},{10,11... | collective-permute-start | bytes 221192 | tf_op jit(solution)/shard_map/ppermute | solution.py:459
  79.5 0.9 collective-permute-done.10.other_ref
  80.5 0.0 copy-done
  80.5 12.5 %solve_and_apply.1 = bf16[8,2048,256]{2,1,0:T(8,128)(2,1)} custom-call(s32[1]{0:T(128)} %bitcast.core_ref, f32[72,256]{1,0:T(8,128)S(1)} %add_add_fusion.mine_ref, f32[72,256]{1,0:T(8,128)S(1)} %collective-permute-done.10.other_ref, f32[8,2048]{1,0:T(8,128)S(1)} %copy-done, bf16[8,2048,256]{2,1,0:T(8,128)(2,1)} %anom_ref.5), custom_call_target="tpu_custom_call" | custom-call | tf_op jit(solution)/shard_map/solve_and_apply/pallas_call | solution.py:439
  (4 shorter events, 0.1 us)
Async XLA Ops:
  0.0 14.1 %copy-start.2 = (f32[32768]{0:T(1024)S(1)}, f32[32768]{0:T(1024)}, u32[]{:S(2)}) copy-start(f32[32768]{0:T(1024)} %param.11) | copy-start | bytes 393220
  0.0 14.2 %copy-start.3 = (f32[32768]{0:T(1024)S(1)}, f32[32768]{0:T(1024)}, u32[]{:S(2)}) copy-start(f32[32768]{0:T(1024)} %param.12) | copy-start | bytes 393220
  5.8 28.2 %copy-start.1 = (s32[4096]{0:T(1024)S(1)}, s32[4096]{0:T(1024)}, u32[]{:S(2)}) copy-start(s32[4096]{0:T(1024)} %cols_ref.1) | copy-start | bytes 49156
  5.8 28.2 %all-to-all-start = ((bf16[384,8,256]{2,1,0:T(8,128)(2,1)}), bf16[384,8,256]{2,1,0:T(8,128)(2,1)S(1)}, u32[]{:S(2)}, u32[]{:S(2)}) async-start(bf16[384,8,256]{2,1,0:T(8,128)(2,1)} %gather_sent.1), calls=%async_computation | async-start | bytes 3145728 | tf_op jit(solution)/shard_map/all_to_all | solution.py:474
  34.1 46.4 %copy-start = (f32[8,2048]{1,0:T(8,128)S(1)}, f32[8,2048]{1,0:T(8,128)}, u32[]{:S(2)}) copy-start(f32[8,2048]{1,0:T(8,128)} %mean_ref.1) | copy-start | bytes 196612
  44.5 10.6 %collective-permute-start = (f32[72,256]{1,0:T(8,128)S(1)}, f32[72,256]{1,0:T(8,128)S(1)}, u32[]{:S(2)}, u32[]{:S(2)}) collective-permute-start(f32[72,256]{1,0:T(8,128)S(1)} %get-tuple-element.14), channel_id=1, source_target_pairs={{0,1},{1,0},{2,3},{3,2},{4,5},{5,4},{6,7},{7,6},{8,9},{9,8},{10,11... | collective-permute-start | bytes 221192 | tf_op jit(solution)/shard_map/ppermute | solution.py:459
  55.1 4.2 %collective-permute-start.3 = (f32[72,256]{1,0:T(8,128)S(1)}, f32[72,256]{1,0:T(8,128)S(1)}, u32[]{:S(2)}, u32[]{:S(2)}) collective-permute-start(f32[72,256]{1,0:T(8,128)S(1)} %add.35), channel_id=1, source_target_pairs={{0,10},{1,11},{2,8},{3,9},{4,14},{5,15},{6,12},{7,13},{8,2},{9,3},... | collective-permute-start | bytes 221192 | tf_op jit(solution)/shard_map/ppermute | solution.py:459
  55.2 4.1 %collective-permute-start.2 = (f32[72,256]{1,0:T(8,128)S(1)}, f32[72,256]{1,0:T(8,128)S(1)}, u32[]{:S(2)}, u32[]{:S(2)}) collective-permute-start(f32[72,256]{1,0:T(8,128)S(1)} %add.35), channel_id=1, source_target_pairs={{0,8},{1,9},{2,10},{3,11},{4,12},{5,13},{6,14},{7,15},{8,0},{9,1},... | collective-permute-start | bytes 221192 | tf_op jit(solution)/shard_map/ppermute | solution.py:459
  55.3 6.4 %collective-permute-start.1 = (f32[72,256]{1,0:T(8,128)S(1)}, f32[72,256]{1,0:T(8,128)S(1)}, u32[]{:S(2)}, u32[]{:S(2)}) collective-permute-start(f32[72,256]{1,0:T(8,128)S(1)} %add.35), channel_id=1, source_target_pairs={{0,2},{1,3},{2,0},{3,1},{4,6},{5,7},{6,4},{7,5},{8,10},{9,11},{10,... | collective-permute-start | bytes 221192 | tf_op jit(solution)/shard_map/ppermute | solution.py:459
  61.7 5.4 %collective-permute-start.6 = (f32[72,256]{1,0:T(8,128)S(1)}, f32[72,256]{1,0:T(8,128)S(1)}, u32[]{:S(2)}, u32[]{:S(2)}) collective-permute-start(f32[72,256]{1,0:T(8,128)S(1)} %add_add_fusion.2), channel_id=1, source_target_pairs={{0,38},{1,39},{2,36},{3,37},{4,34},{5,35},{6,32},{7,33},{8,46},{9,... | collective-permute-start | bytes 221192 | tf_op jit(solution)/shard_map/ppermute | solution.py:459
  61.8 5.3 %collective-permute-start.5 = (f32[72,256]{1,0:T(8,128)S(1)}, f32[72,256]{1,0:T(8,128)S(1)}, u32[]{:S(2)}, u32[]{:S(2)}) collective-permute-start(f32[72,256]{1,0:T(8,128)S(1)} %add_add_fusion.2), channel_id=1, source_target_pairs={{0,6},{1,7},{2,4},{3,5},{4,2},{5,3},{6,0},{7,1},{8,14},{9,15},{10,... | collective-permute-start | bytes 221192 | tf_op jit(solution)/shard_map/ppermute | solution.py:459
  63.8 3.9 %collective-permute-start.4 = (f32[72,256]{1,0:T(8,128)S(1)}, f32[72,256]{1,0:T(8,128)S(1)}, u32[]{:S(2)}, u32[]{:S(2)}) collective-permute-start(f32[72,256]{1,0:T(8,128)S(1)} %add_add_fusion.2), channel_id=1, source_target_pairs={{0,32},{1,33},{2,34},{3,35},{4,36},{5,37},{6,38},{7,39},{8,40},{9,... | collective-permute-start | bytes 221192 | tf_op jit(solution)/shard_map/ppermute | solution.py:459
  67.7 6.6 %collective-permute-start.9 = (f32[72,256]{1,0:T(8,128)S(1)}, f32[72,256]{1,0:T(8,128)S(1)}, u32[]{:S(2)}, u32[]{:S(2)}) collective-permute-start(f32[72,256]{1,0:T(8,128)S(1)} %add_add_fusion.1), channel_id=1, source_target_pairs={{0,120},{1,121},{2,122},{3,123},{4,124},{5,125},{6,126},{7,127},{8... | collective-permute-start | bytes 221192 | tf_op jit(solution)/shard_map/ppermute | solution.py:459
  69.8 4.5 %collective-permute-start.8 = (f32[72,256]{1,0:T(8,128)S(1)}, f32[72,256]{1,0:T(8,128)S(1)}, u32[]{:S(2)}, u32[]{:S(2)}) collective-permute-start(f32[72,256]{1,0:T(8,128)S(1)} %add_add_fusion.1), channel_id=1, source_target_pairs={{0,96},{1,97},{2,98},{3,99},{4,100},{5,101},{6,102},{7,103},{8,104... | collective-permute-start | bytes 221192 | tf_op jit(solution)/shard_map/ppermute | solution.py:459
  71.3 4.4 %collective-permute-start.7 = (f32[72,256]{1,0:T(8,128)S(1)}, f32[72,256]{1,0:T(8,128)S(1)}, u32[]{:S(2)}, u32[]{:S(2)}) collective-permute-start(f32[72,256]{1,0:T(8,128)S(1)} %add_add_fusion.1), channel_id=1, source_target_pairs={{0,24},{1,25},{2,26},{3,27},{4,28},{5,29},{6,30},{7,31},{8,16},{9,... | collective-permute-start | bytes 221192 | tf_op jit(solution)/shard_map/ppermute | solution.py:459
  75.8 4.7 %collective-permute-start.10 = (f32[72,256]{1,0:T(8,128)S(1)}, f32[72,256]{1,0:T(8,128)S(1)}, u32[]{:S(2)}, u32[]{:S(2)}) collective-permute-start(f32[72,256]{1,0:T(8,128)S(1)} %add_add_fusion.mine_ref), channel_id=1, source_target_pairs={{0,1},{1,0},{2,3},{3,2},{4,5},{5,4},{6,7},{7,6},{8,9},{9,8},{10,11... | collective-permute-start | bytes 221192 | tf_op jit(solution)/shard_map/ppermute | solution.py:459

commit v7 on v6

--- a/solution.py
+++ b/solution.py
@@ -422,12 +422,20 @@
     transform = (root + jnp.concatenate([weights, weights], axis=1)).astype(BF16)
 
     stores = []
+    some = anom_ref.shape[1] // 2
     for v in range(lev_dev):
         loads[v].wait()
-        updated = jnp.dot(levels[v], transform, preferred_element_type=F32)
-        results[v] = (means[:, v : v + 1] + updated).astype(BF16)
-        stores.append(pltpu.make_async_copy(results.at[v], out_ref.at[v], out_sems.at[v]))
-        stores[v].start()
+        for h in range(2):
+            part = slice(h * some, (h + 1) * some)
+            updated = jnp.dot(levels[v, part], transform, preferred_element_type=F32)
+            results[v, part] = (means[part, v : v + 1] + updated).astype(BF16)
+            place = pl.ds(h * some, some)
+            stores.append(
+                pltpu.make_async_copy(
+                    results.at[v, place], out_ref.at[v, place], out_sems.at[2 * v + h]
+                )
+            )
+            stores[-1].start()
     for store in stores:
         store.wait()
 
@@ -448,7 +456,7 @@
             pltpu.VMEM((members, members), F32),
             pltpu.VMEM((members, members), F32),
             pltpu.SemaphoreType.DMA((lev_dev,)),
-            pltpu.SemaphoreType.DMA((lev_dev,)),
+            pltpu.SemaphoreType.DMA((2 * lev_dev,)),
         ],
         compiler_params=pltpu.CompilerParams(vmem_limit_bytes=53 << 20),
         name="solve_and_apply",

time: 93.9 us -> 92 us (0.980)
  starting transfers between devices: 32.8 us -> 26.8 us
  Pallas kernels: 43.7 us -> 47.2 us
  waiting for transfers between devices: 15.4 us -> 16.4 us
    ppermute x11, starting transfers between devices: 25.2 us -> 19.2 us  [swap(): return lax.ppermute(value, AXES, [(d, d ^ mask) for d in range(devices)])]
    pallas_call x1, Pallas kernels: 10.5 us -> 16 us  [gram_sums(): pl.pallas_call(gram_kernel, in_specs=[smem, smem, smem, anywhere, anywher...]
    pallas_call x1, Pallas kernels: 12.5 us -> 10.6 us  [solve_and_apply(): pl.pallas_call(apply_kernel, in_specs=[pl.BlockSpec(memory_space=pltpu.SM...]
    ppermute x11, waiting for transfers between devices: 10.6 us -> 11.6 us  [swap(): return lax.ppermute(value, AXES, [(d, d ^ mask) for d in range(devices)])]
  transfers between devices with their start and end apart: 12 -> 12, of which waited for: 9 -> 10; matrix products, arithmetic and copies ran while one was open for 0% -> 0% of each run, Pallas kernels for 16% -> 16%
where the time goes in v7:
time: 92 us; the launch traced here: 91.7 us
  Pallas kernels  47.2 us (51%)
  starting transfers between devices  26.8 us (29%)
  waiting for transfers between devices  16.4 us (18%)
  between operations  0.94 us (1%)
    ppermute x11, starting transfers between devices, swap(): return lax.ppermute(value, AXES, [(d, d ^ mask) for d in range(devices)])  19.2 us
    pallas_call x1, Pallas kernels, gram_sums(): pl.pallas_call(gram_kernel, in_specs=[smem, smem, smem, anywhere, anywher...  16 us
    pallas_call x1, Pallas kernels, prepare(): pl.pallas_call(prepare_kernel, in_specs=[pl.BlockSpec(memory_space=pltpu....  14.9 us
    ppermute x11, waiting for transfers between devices, swap(): return lax.ppermute(value, AXES, [(d, d ^ mask) for d in range(devices)])  11.6 us
    pallas_call x1, Pallas kernels, solve_and_apply(): pl.pallas_call(apply_kernel, in_specs=[pl.BlockSpec(memory_space=pltpu.SM...  10.6 us
    all_to_all x1, starting transfers between devices, per_device(): lax.all_to_all(outgoing, 'tile', split_axis=0, concat_axis=0, tiled=True)  7.6 us
    pallas_call x1, Pallas kernels, gather_sent(): pl.pallas_call(send_kernel, in_specs=[pl.BlockSpec(memory_space=pltpu.SME...  5.79 us
    all_to_all x1, waiting for transfers between devices, per_device(): lax.all_to_all(outgoing, 'tile', split_axis=0, concat_axis=0, tiled=True)  4.8 us
  transfers between devices with their start and end apart: 12, of which 10 were waited for; matrix products, arithmetic and copies ran while one was open for 0% of the time, Pallas kernels for 16%

profile of v7, /device:TPU:1, one launch (start us, length us, event | category | flops | bytes accessed | tf_op | source)
XLA Modules:
  0.0 91.7 jit_solution(18399851440856599755)
XLA Ops:
  0.0 0.0 copy-start.2
  0.0 0.0 copy-start.3
  0.0 5.8 %gather_sent.1 = bf16[384,8,256]{2,1,0:T(8,128)(2,1)} custom-call(s32[1,384]{1,0:T(1,128)} %send_ref.1, bf16[8,2048,256]{2,1,0:T(8,128)(2,1)} %anom_ref.5), custom_call_target="tpu_custom_call" | custom-call | tf_op jit(solution)/shard_map/gather_sent/pallas_call | solution.py:57
  5.8 0.0 copy-start.1
  5.8 7.6 %all-to-all-start = ((bf16[384,8,256]{2,1,0:T(8,128)(2,1)}), bf16[384,8,256]{2,1,0:T(8,128)(2,1)S(1)}, u32[]{:S(2)}, u32[]{:S(2)}) async-start(bf16[384,8,256]{2,1,0:T(8,128)(2,1)} %gather_sent.1), calls=%async_computation | async-start | bytes 3145728 | tf_op jit(solution)/shard_map/all_to_all | solution.py:482
  14.1 0.0 copy-done.2
  14.1 0.1 reshape.11.innov_ref
  14.2 0.0 copy-done.3
  14.2 0.1 reshape.10.rinv_ref
  14.3 14.9 %prepare_operators.1 = (bf16[256,144,128]{2,1,0:T(8,128)(2,1)}, f32[8,256]{1,0:T(8,128)S(1)}, bf16[2048,8,256]{2,1,0:T(8,128)(2,1)}) custom-call(s32[1]{0:T(128)S(6)} %copy.9.count_ref, bf16[512,4096]{1,0:T(8,128)(2,1)} %op_ref.1, f32[512,64]{1,0:T(8,128)S(1)} %reshape.10.rinv_ref, f32[512,64]{1,0:T(8,128)S(1)} %reshape.11.innov_ref, ...), custom_call_target="tpu_custom_call" | custom-call | tf_op jit(solution)/shard_map/prepare_operators/pallas_call | solution.py:189
  29.3 4.8 %all-to-all-done.remote_ref = bf16[384,8,256]{2,1,0:T(8,128)(2,1)S(1)} async-done(((bf16[384,8,256]{2,1,0:T(8,128)(2,1)}), bf16[384,8,256]{2,1,0:T(8,128)(2,1)S(1)}, u32[]{:S(2)}, u32[]{:S(2)}) %all-to-all-start) | async-done | bytes 1572896 | tf_op jit(solution)/shard_map/all_to_all | solution.py:482
  34.0 0.0 copy-done.1
  34.1 0.0 copy-start
  34.1 16.0 %gram_sums.1 = (f32[72,256]{1,0:T(8,128)S(1)}, f32[72,256]{1,0:T(8,128)S(1)}) custom-call(s32[4096]{0:T(1024)S(1)} %copy-done.1, s32[1]{0:T(128)S(6)} %copy.9.count_ref, s32[1]{0:T(128)} %bitcast.core_ref, bf16[2048,8,256]{2,1,0:T(8,128)(2,1)} %get-tuple-element.10.own_ref, bf16[384,8,256]{2,1,0:T(8,128)(2,1)S(1)} %all-to-all-done.remote_ref, ...), custom_call_target="tpu_custom_call" | custom-call | tf_op jit(solution)/shard_map/gram_sums/pallas_call | solution.py:311
  50.0 4.2 %collective-permute-start = (f32[72,256]{1,0:T(8,128)S(1)}, f32[72,256]{1,0:T(8,128)S(1)}, u32[]{:S(2)}, u32[]{:S(2)}) collective-permute-start(f32[72,256]{1,0:T(8,128)S(1)} %get-tuple-element.14), channel_id=1, source_target_pairs={{0,1},{1,0},{2,3},{3,2},{4,5},{5,4},{6,7},{7,6},{8,9},{9,8},{10,11... | collective-permute-start | bytes 221192 | tf_op jit(solution)/shard_map/ppermute | solution.py:467
  54.2 0.9 collective-permute-done
  55.1 0.1 collective-permute-start.3
  55.2 0.4 collective-permute-start.2
  55.6 2.3 %collective-permute-start.1 = (f32[72,256]{1,0:T(8,128)S(1)}, f32[72,256]{1,0:T(8,128)S(1)}, u32[]{:S(2)}, u32[]{:S(2)}) collective-permute-start(f32[72,256]{1,0:T(8,128)S(1)} %add.35), channel_id=1, source_target_pairs={{0,2},{1,3},{2,0},{3,1},{4,6},{5,7},{6,4},{7,5},{8,10},{9,11},{10,... | collective-permute-start | bytes 221192 | tf_op jit(solution)/shard_map/ppermute | solution.py:467
  57.8 1.5 %collective-permute-done.3 = f32[72,256]{1,0:T(8,128)S(1)} collective-permute-done((f32[72,256]{1,0:T(8,128)S(1)}, f32[72,256]{1,0:T(8,128)S(1)}, u32[]{:S(2)}, u32[]{:S(2)}) %collective-permute-start.3) | collective-permute-done | bytes 73760 | tf_op jit(solution)/shard_map/ppermute | solution.py:467
  59.3 0.1 collective-permute-done.2
  59.4 2.2 %collective-permute-done.1 = f32[72,256]{1,0:T(8,128)S(1)} collective-permute-done((f32[72,256]{1,0:T(8,128)S(1)}, f32[72,256]{1,0:T(8,128)S(1)}, u32[]{:S(2)}, u32[]{:S(2)}) %collective-permute-start.1) | collective-permute-done | bytes 73760 | tf_op jit(solution)/shard_map/ppermute | solution.py:467
  61.7 2.8 %collective-permute-start.6 = (f32[72,256]{1,0:T(8,128)S(1)}, f32[72,256]{1,0:T(8,128)S(1)}, u32[]{:S(2)}, u32[]{:S(2)}) collective-permute-start(f32[72,256]{1,0:T(8,128)S(1)} %add_add_fusion.2), channel_id=1, source_target_pairs={{0,38},{1,39},{2,36},{3,37},{4,34},{5,35},{6,32},{7,33},{8,46},{9,... | collective-permute-start | bytes 221192 | tf_op jit(solution)/shard_map/ppermute | solution.py:467
  64.5 0.0 collective-permute-start.5
  64.5 1.1 %collective-permute-start.4 = (f32[72,256]{1,0:T(8,128)S(1)}, f32[72,256]{1,0:T(8,128)S(1)}, u32[]{:S(2)}, u32[]{:S(2)}) collective-permute-start(f32[72,256]{1,0:T(8,128)S(1)} %add_add_fusion.2), channel_id=1, source_target_pairs={{0,32},{1,33},{2,34},{3,35},{4,36},{5,37},{6,38},{7,39},{8,40},{9,... | collective-permute-start | bytes 221192 | tf_op jit(solution)/shard_map/ppermute | solution.py:467
  65.6 1.5 %collective-permute-done.6 = f32[72,256]{1,0:T(8,128)S(1)} collective-permute-done((f32[72,256]{1,0:T(8,128)S(1)}, f32[72,256]{1,0:T(8,128)S(1)}, u32[]{:S(2)}, u32[]{:S(2)}) %collective-permute-start.6) | collective-permute-done | bytes 73760 | tf_op jit(solution)/shard_map/ppermute | solution.py:467
  67.1 1.9 %collective-permute-done.5 = f32[72,256]{1,0:T(8,128)S(1)} collective-permute-done((f32[72,256]{1,0:T(8,128)S(1)}, f32[72,256]{1,0:T(8,128)S(1)}, u32[]{:S(2)}, u32[]{:S(2)}) %collective-permute-start.5) | collective-permute-done | bytes 73760 | tf_op jit(solution)/shard_map/ppermute | solution.py:467
  69.0 0.0 collective-permute-done.4
  69.0 1.6 %collective-permute-start.9 = (f32[72,256]{1,0:T(8,128)S(1)}, f32[72,256]{1,0:T(8,128)S(1)}, u32[]{:S(2)}, u32[]{:S(2)}) collective-permute-start(f32[72,256]{1,0:T(8,128)S(1)} %add_add_fusion.1), channel_id=1, source_target_pairs={{0,120},{1,121},{2,122},{3,123},{4,124},{5,125},{6,126},{7,127},{8... | collective-permute-start | bytes 221192 | tf_op jit(solution)/shard_map/ppermute | solution.py:467
  70.6 0.6 collective-permute-start.8
  71.2 2.9 %collective-permute-start.7 = (f32[72,256]{1,0:T(8,128)S(1)}, f32[72,256]{1,0:T(8,128)S(1)}, u32[]{:S(2)}, u32[]{:S(2)}) collective-permute-start(f32[72,256]{1,0:T(8,128)S(1)} %add_add_fusion.1), channel_id=1, source_target_pairs={{0,24},{1,25},{2,26},{3,27},{4,28},{5,29},{6,30},{7,31},{8,16},{9,... | collective-permute-start | bytes 221192 | tf_op jit(solution)/shard_map/ppermute | solution.py:467
  74.2 1.5 %collective-permute-done.9 = f32[72,256]{1,0:T(8,128)S(1)} collective-permute-done((f32[72,256]{1,0:T(8,128)S(1)}, f32[72,256]{1,0:T(8,128)S(1)}, u32[]{:S(2)}, u32[]{:S(2)}) %collective-permute-start.9) | collective-permute-done | bytes 73760 | tf_op jit(solution)/shard_map/ppermute | solution.py:467
  75.7 0.0 collective-permute-done.8
  75.7 1.0 %collective-permute-done.7 = f32[72,256]{1,0:T(8,128)S(1)} collective-permute-done((f32[72,256]{1,0:T(8,128)S(1)}, f32[72,256]{1,0:T(8,128)S(1)}, u32[]{:S(2)}, u32[]{:S(2)}) %collective-permute-start.7) | collective-permute-done | bytes 73760 | tf_op jit(solution)/shard_map/ppermute | solution.py:467
  76.8 3.3 %collective-permute-start.10 = (f32[72,256]{1,0:T(8,128)S(1)}, f32[72,256]{1,0:T(8,128)S(1)}, u32[]{:S(2)}, u32[]{:S(2)}) collective-permute-start(f32[72,256]{1,0:T(8,128)S(1)} %add_add_fusion.mine_ref), channel_id=1, source_target_pairs={{0,1},{1,0},{2,3},{3,2},{4,5},{5,4},{6,7},{7,6},{8,9},{9,8},{10,11... | collective-permute-start | bytes 221192 | tf_op jit(solution)/shard_map/ppermute | solution.py:467
  80.0 0.9 collective-permute-done.10.other_ref
  80.9 0.0 copy-done
  80.9 10.6 %solve_and_apply.1 = bf16[8,2048,256]{2,1,0:T(8,128)(2,1)} custom-call(s32[1]{0:T(128)} %bitcast.core_ref, f32[72,256]{1,0:T(8,128)S(1)} %add_add_fusion.mine_ref, f32[72,256]{1,0:T(8,128)S(1)} %collective-permute-done.10.other_ref, f32[8,2048]{1,0:T(8,128)S(1)} %copy-done, bf16[8,2048,256]{2,1,0:T(8,128)(2,1)} %anom_ref.5), custom_call_target="tpu_custom_call" | custom-call | tf_op jit(solution)/shard_map/solve_and_apply/pallas_call | solution.py:447
  (4 shorter events, 0.1 us)
Async XLA Ops:
  0.0 14.1 %copy-start.2 = (f32[32768]{0:T(1024)S(1)}, f32[32768]{0:T(1024)}, u32[]{:S(2)}) copy-start(f32[32768]{0:T(1024)} %param.11) | copy-start | bytes 393220
  0.0 14.2 %copy-start.3 = (f32[32768]{0:T(1024)S(1)}, f32[32768]{0:T(1024)}, u32[]{:S(2)}) copy-start(f32[32768]{0:T(1024)} %param.12) | copy-start | bytes 393220
  5.8 28.2 %copy-start.1 = (s32[4096]{0:T(1024)S(1)}, s32[4096]{0:T(1024)}, u32[]{:S(2)}) copy-start(s32[4096]{0:T(1024)} %cols_ref.1) | copy-start | bytes 49156
  5.8 28.2 %all-to-all-start = ((bf16[384,8,256]{2,1,0:T(8,128)(2,1)}), bf16[384,8,256]{2,1,0:T(8,128)(2,1)S(1)}, u32[]{:S(2)}, u32[]{:S(2)}) async-start(bf16[384,8,256]{2,1,0:T(8,128)(2,1)} %gather_sent.1), calls=%async_computation | async-start | bytes 3145728 | tf_op jit(solution)/shard_map/all_to_all | solution.py:482
  34.1 46.9 %copy-start = (f32[8,2048]{1,0:T(8,128)S(1)}, f32[8,2048]{1,0:T(8,128)}, u32[]{:S(2)}) copy-start(f32[8,2048]{1,0:T(8,128)} %mean_ref.1) | copy-start | bytes 196612
  50.0 5.1 %collective-permute-start = (f32[72,256]{1,0:T(8,128)S(1)}, f32[72,256]{1,0:T(8,128)S(1)}, u32[]{:S(2)}, u32[]{:S(2)}) collective-permute-start(f32[72,256]{1,0:T(8,128)S(1)} %get-tuple-element.14), channel_id=1, source_target_pairs={{0,1},{1,0},{2,3},{3,2},{4,5},{5,4},{6,7},{7,6},{8,9},{9,8},{10,11... | collective-permute-start | bytes 221192 | tf_op jit(solution)/shard_map/ppermute | solution.py:467
  55.1 4.2 %collective-permute-start.3 = (f32[72,256]{1,0:T(8,128)S(1)}, f32[72,256]{1,0:T(8,128)S(1)}, u32[]{:S(2)}, u32[]{:S(2)}) collective-permute-start(f32[72,256]{1,0:T(8,128)S(1)} %add.35), channel_id=1, source_target_pairs={{0,10},{1,11},{2,8},{3,9},{4,14},{5,15},{6,12},{7,13},{8,2},{9,3},... | collective-permute-start | bytes 221192 | tf_op jit(solution)/shard_map/ppermute | solution.py:467
  55.2 4.2 %collective-permute-start.2 = (f32[72,256]{1,0:T(8,128)S(1)}, f32[72,256]{1,0:T(8,128)S(1)}, u32[]{:S(2)}, u32[]{:S(2)}) collective-permute-start(f32[72,256]{1,0:T(8,128)S(1)} %add.35), channel_id=1, source_target_pairs={{0,8},{1,9},{2,10},{3,11},{4,12},{5,13},{6,14},{7,15},{8,0},{9,1},... | collective-permute-start | bytes 221192 | tf_op jit(solution)/shard_map/ppermute | solution.py:467
  55.6 6.1 %collective-permute-start.1 = (f32[72,256]{1,0:T(8,128)S(1)}, f32[72,256]{1,0:T(8,128)S(1)}, u32[]{:S(2)}, u32[]{:S(2)}) collective-permute-start(f32[72,256]{1,0:T(8,128)S(1)} %add.35), channel_id=1, source_target_pairs={{0,2},{1,3},{2,0},{3,1},{4,6},{5,7},{6,4},{7,5},{8,10},{9,11},{10,... | collective-permute-start | bytes 221192 | tf_op jit(solution)/shard_map/ppermute | solution.py:467
  61.7 5.4 %collective-permute-start.6 = (f32[72,256]{1,0:T(8,128)S(1)}, f32[72,256]{1,0:T(8,128)S(1)}, u32[]{:S(2)}, u32[]{:S(2)}) collective-permute-start(f32[72,256]{1,0:T(8,128)S(1)} %add_add_fusion.2), channel_id=1, source_target_pairs={{0,38},{1,39},{2,36},{3,37},{4,34},{5,35},{6,32},{7,33},{8,46},{9,... | collective-permute-start | bytes 221192 | tf_op jit(solution)/shard_map/ppermute | solution.py:467
  64.5 4.5 %collective-permute-start.5 = (f32[72,256]{1,0:T(8,128)S(1)}, f32[72,256]{1,0:T(8,128)S(1)}, u32[]{:S(2)}, u32[]{:S(2)}) collective-permute-start(f32[72,256]{1,0:T(8,128)S(1)} %add_add_fusion.2), channel_id=1, source_target_pairs={{0,6},{1,7},{2,4},{3,5},{4,2},{5,3},{6,0},{7,1},{8,14},{9,15},{10,... | collective-permute-start | bytes 221192 | tf_op jit(solution)/shard_map/ppermute | solution.py:467
  64.5 4.5 %collective-permute-start.4 = (f32[72,256]{1,0:T(8,128)S(1)}, f32[72,256]{1,0:T(8,128)S(1)}, u32[]{:S(2)}, u32[]{:S(2)}) collective-permute-start(f32[72,256]{1,0:T(8,128)S(1)} %add_add_fusion.2), channel_id=1, source_target_pairs={{0,32},{1,33},{2,34},{3,35},{4,36},{5,37},{6,38},{7,39},{8,40},{9,... | collective-permute-start | bytes 221192 | tf_op jit(solution)/shard_map/ppermute | solution.py:467
  69.0 6.7 %collective-permute-start.9 = (f32[72,256]{1,0:T(8,128)S(1)}, f32[72,256]{1,0:T(8,128)S(1)}, u32[]{:S(2)}, u32[]{:S(2)}) collective-permute-start(f32[72,256]{1,0:T(8,128)S(1)} %add_add_fusion.1), channel_id=1, source_target_pairs={{0,120},{1,121},{2,122},{3,123},{4,124},{5,125},{6,126},{7,127},{8... | collective-permute-start | bytes 221192 | tf_op jit(solution)/shard_map/ppermute | solution.py:467
  70.6 5.1 %collective-permute-start.8 = (f32[72,256]{1,0:T(8,128)S(1)}, f32[72,256]{1,0:T(8,128)S(1)}, u32[]{:S(2)}, u32[]{:S(2)}) collective-permute-start(f32[72,256]{1,0:T(8,128)S(1)} %add_add_fusion.1), channel_id=1, source_target_pairs={{0,96},{1,97},{2,98},{3,99},{4,100},{5,101},{6,102},{7,103},{8,104... | collective-permute-start | bytes 221192 | tf_op jit(solution)/shard_map/ppermute | solution.py:467
  71.2 5.5 %collective-permute-start.7 = (f32[72,256]{1,0:T(8,128)S(1)}, f32[72,256]{1,0:T(8,128)S(1)}, u32[]{:S(2)}, u32[]{:S(2)}) collective-permute-start(f32[72,256]{1,0:T(8,128)S(1)} %add_add_fusion.1), channel_id=1, source_target_pairs={{0,24},{1,25},{2,26},{3,27},{4,28},{5,29},{6,30},{7,31},{8,16},{9,... | collective-permute-start | bytes 221192 | tf_op jit(solution)/shard_map/ppermute | solution.py:467
  76.8 4.2 %collective-permute-start.10 = (f32[72,256]{1,0:T(8,128)S(1)}, f32[72,256]{1,0:T(8,128)S(1)}, u32[]{:S(2)}, u32[]{:S(2)}) collective-permute-start(f32[72,256]{1,0:T(8,128)S(1)} %add_add_fusion.mine_ref), channel_id=1, source_target_pairs={{0,1},{1,0},{2,3},{3,2},{4,5},{5,4},{6,7},{7,6},{8,9},{9,8},{10,11... | collective-permute-start | bytes 221192 | tf_op jit(solution)/shard_map/ppermute | solution.py:467
